TPU v7x, 128 devices: a whole 4x4x4 slice. The times are simulated.
128 devices in a mesh: lat: 4 (over z), lon: 32 (over y, x, core).
Axes of the slice: x: 4, y: 4, z: 4, core: 2. Of those that a mesh axis runs over, the one named last changes fastest.
Arguments:
- conc: float32 [150, 262144], P(None, ('lat', 'lon')), may hold values from 0.2 to 2
- dest_tile: int32 [262144, 1], P(('lat', 'lon')), may hold values from 0 to 127; in each aligned block of 2048 rows (0 to 2047, 2048 to 4095, ...) at most 32 rows name the same one
- mixing_share: float32 [524288], P(('lat', 'lon')), may hold values from 0.1 to 0.6
- partner: int32 [524288], P(('lat', 'lon')), may hold values from 0 to 127
- photolysis: float32 [524288], P(('lat', 'lon')), may hold values from 0.1 to 1
- production: float32 [150], replicated, may hold values from 0.2 to 1
- loss: float32 [150], replicated, may hold values from 0.05 to 0.5
- rates: float32 [150, 150], replicated, may hold values from -0.5 to 0.5
- pattern: int32 [10, 10], replicated, may hold values 0 or 1
- precond: float32 [150, 150], replicated, may hold values from -2 to 2
Outputs:
- chem: float32 [150, 524288], P(None, ('lat', 'lon'))
Inputs may be any that keep to these rules, and one draw needn't show every extreme that they name: `dest_tile`: no tile sends more than 32 parcels to one tile, and some tile sends exactly 32 to one.
All inputs are finite; a program needn't handle non-finite values.
Results may differ from a plain program's by a relative error of at most 0.0003.
Values sent between devices are 32-bit elements; how exact they have to be, the bound alone decides.
No kernel may reach another device: no remote copies, remote signals or barrier semaphores. Data moves between devices by JAX's collectives and lax.ppermute only.
A program may use at most 64 MiB of HBM per device.

v0:
```python
import jax
import jax.numpy as jnp
from jax import lax
from jax.sharding import PartitionSpec as P

SB = 15
MIXING_BLOCK = 128
NEWTON = 2


time_step = 0.5


def passed_along(value, axis, steps):
    count = lax.axis_size(axis)
    pairs = [(source, (source + steps) % count) for source in range(count)]
    return lax.ppermute(value, axis, pairs)


def block_mask(pattern):
    return jnp.kron(pattern.astype(jnp.float32), jnp.ones((SB, SB), jnp.float32))


def chemistry(initial, photo_rate, present_mask, coupled, production, loss, precond):
    current = initial
    for iteration in range(NEWTON):
        tendency = jnp.dot(
            coupled, current, precision=lax.Precision.HIGHEST, preferred_element_type=jnp.float32
        )
        tendency = (
            tendency + production[:, None] * photo_rate[None, :] - loss[:, None] * current * current
        )
        misfit = current - initial - time_step * tendency
        first_pass = jnp.dot(
            precond, misfit, precision=lax.Precision.HIGHEST, preferred_element_type=jnp.float32
        )
        second_pass = jnp.dot(
            precond,
            2.0 * time_step * loss[:, None] * current * first_pass,
            precision=lax.Precision.HIGHEST,
            preferred_element_type=jnp.float32,
        )
        current = current - (first_pass - second_pass)
    return current * present_mask[None, :]


def ranks_within(targets, devices):
    columns = jnp.arange(devices, dtype=jnp.int32)
    onehot = (targets[:, None] == columns[None, :]).astype(jnp.int32)
    before = jnp.cumsum(onehot, axis=0) - onehot
    return jnp.sum(before * onehot, axis=1)


def whole_east(placed_parcels):
    return passed_along(placed_parcels, "lon", -1)


def shards(
    conc, dest_tile, mixing_share, partner, photolysis, production, loss, rates, pattern, precond
):
    lat_count = lax.axis_size("lat")
    lon_count = lax.axis_size("lon")
    devices = lat_count * lon_count
    species, parcels = conc.shape
    tile_slots = 2 * parcels
    capacity = tile_slots // devices
    targets = dest_tile[:, 0]
    ranking = ranks_within(targets, devices)
    send_slot = targets * capacity + ranking
    outgoing = jnp.zeros((species, tile_slots), jnp.float32).at[:, send_slot].set(conc)
    arrived = lax.all_to_all(
        outgoing.reshape(species, devices, capacity),
        ("lat", "lon"),
        split_axis=1,
        concat_axis=1,
        tiled=True,
    )
    placed_parcels = arrived.reshape(species, tile_slots)
    present_mask = (placed_parcels[0] > 0.0).astype(jnp.float32)
    eastern = whole_east(placed_parcels)
    partner_slot = jnp.arange(tile_slots, dtype=jnp.int32) // MIXING_BLOCK * MIXING_BLOCK + partner
    partner_conc = jnp.take(eastern, partner_slot, axis=1)
    partner_alive = (partner_conc[0] > 0.0).astype(jnp.float32)
    weight_mix = mixing_share * present_mask * partner_alive
    mixed = placed_parcels + weight_mix[None, :] * (partner_conc - placed_parcels)
    coupled = rates * block_mask(pattern)
    reacted_tile = chemistry(mixed, photolysis, present_mask, coupled, production, loss, precond)
    return reacted_tile


def solution(mesh):
    placed = (
        P(None, ("lat", "lon")),
        P(("lat", "lon"), None),
        P(("lat", "lon")),
        P(("lat", "lon")),
        P(("lat", "lon")),
        P(),
        P(),
        P(),
        P(),
        P(),
    )
    return jax.shard_map(
        shards, mesh=mesh, in_specs=placed, out_specs=P(None, ("lat", "lon")), check_vma=False
    )
```

profile of v0, /device:TPU:1, one launch (start us, length us, event | category | flops | bytes accessed | tf_op | source)
XLA Modules:
  0.0 161.0 jit_solution(10632514237159562733)
XLA Ops:
  0.0 0.0 copy-start
  0.0 0.8 copy.24
  0.8 0.0 copy-start.5
  0.8 0.3 fusion.18
  1.2 0.0 copy-start.3
  1.2 0.1 broadcast_add_fusion
  1.3 0.3 copy.25
  1.7 0.0 copy-done.5
  1.7 0.6 fusion.17
  2.4 0.2 copy-done.3
  2.5 0.8 copy.26
  3.3 11.2 %scatter_custom_fusion = f32[150,4096]{0,1:T(8,128)} fusion(s32[2048]{0:T(1024)S(1)} %bitcast.54, f32[2048,150]{1,0:T(8,128)S(1)} %copy.26, f32[]{:T(128)} %constant.40.clone.1), kind=kCustom, calls=%fused_computation.26 | custom fusion | bytes 2457604 | tf_op jit(solution)/shard_map/scatter | solution.py:70
  14.6 64.6 %all_to_all.5 = f32[150,128,32]{0,2,1:T(8,128)} all-to-all(f32[150,128,32]{0,2,1:T(8,128)} %bitcast.49), channel_id=1, replica_groups=mesh['lat'=4,'lon'=32] {'lat','lon'}, dimensions={1} | all-to-all | bytes 4915200 | tf_op jit(solution)/shard_map/all_to_all | solution.py:71
  79.2 0.0 copy-start.10
  79.2 3.7 %copy.31 = f32[150,4096]{1,0:T(8,128)S(1)} copy(f32[150,4096]{0,1:T(8,128)} %bitcast.48) | data formatting | bytes 4915200 | tf_op jit(solution)/shard_map/reshape | solution.py:78
  82.9 0.0 copy-start.1
  82.9 0.0 copy-start.6
  82.9 1.0 collective-permute-start
  83.9 0.0 copy-done.10
  83.9 1.2 mul.126
  85.1 1.6 %mul.127 = f32[150,150]{1,0:T(8,128)S(1)} reshape(f32[10,15,10,15]{3,2,1,0:T(8,128)} %mul.126) | data formatting | bytes 180000 | tf_op jit(solution)/shard_map/jit(kron)/mul | solution.py:21
  86.7 0.0 copy-done.6
  86.7 3.8 %fusion.13 = pred[128,32]{1,0:T(8,128)(4,1)S(1)} fusion(f32[150,128,32]{0,2,1:T(8,128)} %all_to_all.5), kind=kLoop, calls=%fused_computation.28 | loop fusion | flops 4096 | bytes 20480 | tf_op jit(solution)/shard_map/gt | solution.py:79
  90.6 0.1 gt.19
  90.7 22.0 %collective-permute-done = f32[150,4096]{1,0:T(8,128)} collective-permute-done((f32[150,4096]{1,0:T(8,128)S(1)}, f32[150,4096]{1,0:T(8,128)}, u32[]{:S(2)}, u32[]{:S(2)}) %collective-permute-start) | collective-permute-done | bytes 2457632 | tf_op jit(solution)/shard_map/ppermute | solution.py:17
  112.7 4.8 %copy.28 = f32[150,4096]{0,1:T(8,128)} copy(f32[150,4096]{1,0:T(8,128)} %collective-permute-done) | data formatting | bytes 4915200 | tf_op jit(solution)/shard_map/ppermute | solution.py:17
  117.5 0.0 copy-done.1
  117.5 18.3 %gather_fusion = f32[4096,150]{1,0:T(8,128)} fusion(f32[150,4096]{0,1:T(8,128)} %copy.28, s32[4096]{0:T(1024)S(1)} %broadcast_clamp_fusion), kind=kCustom, calls=%fused_computation | custom fusion | bytes 4931584 | tf_op jit(solution)/shard_map/jit(_take)/gather | solution.py:82
  135.8 3.8 %copy.29 = f32[4096,150]{0,1:T(8,128)S(1)} copy(f32[4096,150]{1,0:T(8,128)} %gather_fusion) | data formatting | bytes 4915200 | tf_op jit(solution)/shard_map/jit(_take)/gather | solution.py:82
  139.7 0.0 copy-start.8
  139.7 0.0 copy-start.2
  139.7 0.2 select_bitcast_fusion
  139.9 0.1 compare_reduce_fusion
  140.0 0.4 copy-done.8
  140.4 1.0 copy-done.2
  141.4 0.0 copy-start.4
  141.4 0.0 copy-start.7
  141.4 0.0 copy-start.9
  141.4 0.0 copy-start.11
  141.4 0.5 multiply_add_fusion
  141.9 0.4 copy-done.4
  142.3 0.0 copy-done.7
  142.3 0.0 copy-done.9
  142.3 0.0 copy-done.11
  142.3 2.9 %fusion.10 = f32[150,4096]{1,0:T(8,128)S(1)} fusion(f32[150,4096]{1,0:T(8,128)S(1)} %multiply_add_fusion, f32[150]{0:T(256)S(1)} %copy-done.9, f32[4096]{0:T(1024)S(1)} %copy-done.7, f32[150]{0:T(256)S(1)} %copy-done.11, f32[150,150]{1,0:T(8,128)S(1)} %copy-done.4, f32[150,150]{1,0:T(8,128)S(1)} %mul.127), kind=kOutput, calls=%fused_computation.18 | convolution fusion | flops 1110857728 | bytes 5112784 | tf_op jit(solution)/shard_map/dot_general | solution.py:27
  145.2 0.0 copy-done
  145.2 2.4 %convolution_bitcast_fusion.3 = f32[150,4096]{1,0:T(8,128)S(1)} fusion(f32[150,4096]{1,0:T(8,128)S(1)} %fusion.10, f32[150,150]{1,0:T(8,128)S(1)} %copy-done), kind=kOutput, calls=%fused_computation.14 | convolution fusion | flops 1105920000 | bytes 5005200 | tf_op jit(solution)/shard_map/dot_general | solution.py:34
  147.7 3.0 %fusion.7 = f32[150,4096]{1,0:T(8,128)S(1)} fusion(f32[150,4096]{1,0:T(8,128)S(1)} %multiply_add_fusion, f32[150,4096]{1,0:T(8,128)S(1)} %convolution_bitcast_fusion.3, f32[150,150]{1,0:T(8,128)S(1)} %copy-done, f32[150]{0:T(256)S(1)} %copy-done.9), kind=kOutput, calls=%fused_computation.13 | convolution fusion | flops 1108377600 | bytes 7463400 | tf_op jit(solution)/shard_map/dot_general | solution.py:37
  150.7 3.0 %fusion.5 = f32[150,4096]{1,0:T(8,128)S(1)} fusion(f32[150,4096]{1,0:T(8,128)S(1)} %fusion.7, f32[150,4096]{1,0:T(8,128)S(1)} %multiply_add_fusion, f32[150]{0:T(256)S(1)} %copy-done.9, f32[4096]{0:T(1024)S(1)} %copy-done.7, f32[150]{0:T(256)S(1)} %copy-done.11, f32[150,150]{1,0:T(8,128)S(1)} %copy-done.4, f32[150,150]{1,0:T(8,128)S(1)} %mul.127), kind=kOutput, calls=%fused_computation.10 | convolution fusion | flops 1110857728 | bytes 7570384 | tf_op jit(solution)/shard_map/dot_general | solution.py:27
  153.7 2.7 %convolution_bitcast_fusion.1 = f32[150,4096]{1,0:T(8,128)S(1)} fusion(f32[150,4096]{1,0:T(8,128)S(1)} %fusion.5, f32[150,150]{1,0:T(8,128)S(1)} %copy-done), kind=kOutput, calls=%fused_computation.6 | convolution fusion | flops 1105920000 | bytes 5005200 | tf_op jit(solution)/shard_map/dot_general | solution.py:34
  156.4 4.6 %fusion.2 = f32[150,4096]{1,0:T(8,128)} fusion(f32[150,4096]{1,0:T(8,128)S(1)} %fusion.7, f32[150,4096]{1,0:T(8,128)S(1)} %convolution_bitcast_fusion.1, f32[150,150]{1,0:T(8,128)S(1)} %copy-done, f32[4096]{0:T(1024)S(1)} %convert_element_type.21, f32[150]{0:T(256)S(1)} %copy-done.9), kind=kOutput, calls=%fused_computation.5 | convolution fusion | flops 1108992000 | bytes 7479784 | tf_op jit(solution)/shard_map/dot_general | solution.py:37
  (9 shorter events, 0.1 us)
Async XLA Ops:
  0.0 145.2 %copy-start = (f32[150,150]{1,0:T(8,128)S(1)}, f32[150,150]{1,0:T(8,128)}, u32[]{:S(2)}) copy-start(f32[150,150]{1,0:T(8,128)} %param.19) | copy-start | bytes 270004
  0.8 0.8 copy-start.5
  1.2 1.3 copy-start.3
  79.2 4.7 %copy-start.10 = (s32[10,10]{1,0:T(8,128)S(1)}, s32[10,10]{1,0:T(8,128)}, u32[]{:S(2)}) copy-start(s32[10,10]{1,0:T(8,128)} %param.18) | copy-start | bytes 1204
  82.9 34.7 %copy-start.1 = (f32[150,4096]{1,0:T(8,128)}, f32[150,4096]{1,0:T(8,128)S(1)}, u32[]{:S(2)}) copy-start(f32[150,4096]{1,0:T(8,128)S(1)} %copy.31) | copy-start | bytes 7372804
  82.9 3.8 %copy-start.6 = (s32[4096]{0:T(1024)S(1)}, s32[4096]{0:T(1024)}, u32[]{:S(2)}) copy-start(s32[4096]{0:T(1024)} %param.13) | copy-start | bytes 49156
  82.9 29.8 %collective-permute-start = (f32[150,4096]{1,0:T(8,128)S(1)}, f32[150,4096]{1,0:T(8,128)}, u32[]{:S(2)}, u32[]{:S(2)}) collective-permute-start(f32[150,4096]{1,0:T(8,128)S(1)} %copy.31), channel_id=1, source_target_pairs={{0,31},{1,0},{2,1},{3,2},{4,3},{5,4},{6,5},{7,6},{8,7},{9,8},{10,9... | collective-permute-start | bytes 7372808 | tf_op jit(solution)/shard_map/ppermute | solution.py:17
  139.7 0.7 copy-start.8
  139.7 1.7 %copy-start.2 = (f32[150,4096]{1,0:T(8,128)S(1)}, f32[150,4096]{1,0:T(8,128)}, u32[]{:S(2)}) copy-start(f32[150,4096]{1,0:T(8,128)} %copy-done.1) | copy-start | bytes 7372804
  141.4 0.9 copy-start.4
  141.4 0.9 copy-start.7
  141.4 0.9 copy-start.9
  141.4 0.9 copy-start.11
where the time goes:
time: 162 us; the launch traced here: 161 us
  blocking collectives  64.6 us (40%)
  local copies, waits for them, and re-layouts  48.8 us (30%)
  waiting for transfers between devices  22 us (14%)
  matrix products  18.6 us (11%)
  other arithmetic  5.71 us (4%)
    all_to_all x1, blocking collectives, shards(): lax.all_to_all(outgoing.reshape(species, devices, capacity), ('lat', 'lon...  64.6 us
    gather x2, local copies, waits for them, and re-layouts, shards(): partner_conc = jnp.take(eastern, partner_slot, axis=1)  22.1 us
    ppermute x1, waiting for transfers between devices, passed_along(): return lax.ppermute(value, axis, pairs)  22 us
    scatter x1, local copies, waits for them, and re-layouts, shards(): jnp.zeros((species, tile_slots), jnp.float32).at[:, send_slot].set(conc)  11.2 us
    dot_general x2, matrix products, chemistry(): jnp.dot(precond, 2.0 * time_step * loss[:, None] * current * first_pass,...  7.59 us
    dot_general x2, matrix products, chemistry(): jnp.dot(coupled, current, precision=lax.Precision.HIGHEST, preferred_elem...  5.91 us
    dot_general x2, matrix products, chemistry(): jnp.dot(precond, misfit, precision=lax.Precision.HIGHEST, preferred_eleme...  5.12 us
    ppermute x1, local copies, waits for them, and re-layouts, passed_along(): return lax.ppermute(value, axis, pairs)  4.8 us
  transfers between devices with their start and end apart: 1, of which 1 were waited for; matrix products, arithmetic and copies ran while one was open for 4% of the time, Pallas kernels for 0%

commit v1 on v0

v1 whole, which is shorter than its diff:
```python
import functools

import jax
import jax.numpy as jnp
from jax import lax
from jax.experimental import pallas as pl
from jax.experimental.pallas import tpu as pltpu
from jax.sharding import PartitionSpec as P

SB = 15
NEWTON = 2
time_step = 0.5

LANES = 128
CAP = 32
QUARTER = 40
ROWS = 4 * QUARTER
TILES = QUARTER // 8


def regroup(first, second, third, fourth, lane):
    low_half = lane < 64
    low_quarter = (lane % 64) < 32
    t0 = jnp.where(low_half, first, pltpu.roll(third, 64, 1))
    t2 = jnp.where(low_half, pltpu.roll(first, 64, 1), third)
    t1 = jnp.where(low_half, second, pltpu.roll(fourth, 64, 1))
    t3 = jnp.where(low_half, pltpu.roll(second, 64, 1), fourth)
    return (
        jnp.where(low_quarter, t0, pltpu.roll(t1, 32, 1)),
        jnp.where(low_quarter, pltpu.roll(t0, 96, 1), t1),
        jnp.where(low_quarter, t2, pltpu.roll(t3, 32, 1)),
        jnp.where(low_quarter, pltpu.roll(t2, 96, 1), t3),
    )


def slot_table(targets_ref):
    blocks = targets_ref.shape[0]
    row = lax.broadcasted_iota(jnp.int32, (LANES, LANES), 0)
    column = lax.broadcasted_iota(jnp.int32, (LANES, LANES), 1)
    earlier = (row < column).astype(jnp.float32).astype(jnp.bfloat16)
    ones = jnp.ones((LANES, LANES), jnp.bfloat16)
    counted = jnp.zeros((LANES, LANES), jnp.float32)
    table = jnp.zeros((3 * CAP, LANES), jnp.float32)
    group = lax.broadcasted_iota(jnp.int32, (CAP, LANES), 0)
    place = lax.broadcasted_iota(jnp.int32, (CAP, LANES), 1).astype(jnp.float32)
    for block in range(blocks):
        targets = targets_ref[block : block + 1, :]
        onehot = (row == targets).astype(jnp.float32)
        packed = onehot.astype(jnp.bfloat16)
        before = jnp.dot(packed, earlier, preferred_element_type=jnp.float32)
        ranking = jnp.sum(onehot * (before + counted), axis=0, keepdims=True)
        counted = counted + jnp.dot(packed, ones, preferred_element_type=jnp.float32)
        slot = targets * CAP + ranking.astype(jnp.int32)
        here = (row == slot % LANES).astype(jnp.float32).astype(jnp.bfloat16)
        mine = (group == slot // LANES).astype(jnp.float32)
        left = jnp.concatenate([mine, mine * float(block), mine * place], axis=0)
        table = table + lax.dot_general(
            left.astype(jnp.bfloat16),
            here,
            (((1,), (1,)), ((), ())),
            preferred_element_type=jnp.float32,
        )
    return table


def pack_kernel(conc_ref, targets_ref, out_ref, padded, table_ref):
    species, parcels = conc_ref.shape
    blocks = parcels // LANES
    whole = species // 8 * 8
    padded[whole:ROWS, :] = jnp.zeros((ROWS - whole, parcels), jnp.float32)
    padded[0:species, :] = conc_ref[...]
    table_ref[...] = slot_table(targets_ref).astype(jnp.int32)
    lane = lax.broadcasted_iota(jnp.int32, (8, LANES), 1)

    def step(group, carry):
        filled = jnp.broadcast_to(table_ref[pl.ds(group, 1), :], (8, LANES))
        block = jnp.broadcast_to(table_ref[pl.ds(CAP + group, 1), :], (8, LANES))
        place = jnp.broadcast_to(table_ref[pl.ds(2 * CAP + group, 1), :], (8, LANES))
        block = jnp.where(filled > 0, block, -1)
        masks = [block == b for b in range(blocks)]
        for k in range(TILES):
            parts = []
            for j in range(4):
                base = QUARTER * j + 8 * k
                if base >= species:
                    parts.append(jnp.zeros((8, LANES), jnp.float32))
                    continue
                value = jnp.zeros((8, LANES), jnp.float32)
                for b in range(blocks):
                    source = padded[base : base + 8, b * LANES : (b + 1) * LANES]
                    value = jnp.where(
                        masks[b], jnp.take_along_axis(source, place, axis=1), value
                    )
                parts.append(value)
            for d, chunk in enumerate(regroup(*parts, lane)):
                out_ref[group * 4 + d, 8 * k : 8 * k + 8, :] = chunk
        return carry

    lax.fori_loop(0, CAP, step, 0)


def pack(conc, targets):
    devices = 128
    species, parcels = conc.shape
    return pl.pallas_call(
        pack_kernel,
        out_shape=jax.ShapeDtypeStruct((devices, QUARTER, LANES), jnp.float32),
        in_specs=[pl.BlockSpec(memory_space=pltpu.VMEM)] * 2,
        out_specs=pl.BlockSpec(memory_space=pltpu.VMEM),
        scratch_shapes=[
            pltpu.VMEM((ROWS, parcels), jnp.float32),
            pltpu.VMEM((3 * CAP, LANES), jnp.int32),
        ],
        compiler_params=pltpu.CompilerParams(vmem_limit_bytes=32 * 1024 * 1024),
        name="pack",
    )(conc, targets)


def product(weights, value):
    high = value.astype(jnp.bfloat16)
    low = (value - high.astype(jnp.float32)).astype(jnp.bfloat16)
    return jnp.dot(
        weights,
        jnp.concatenate([high, low, high], axis=0),
        preferred_element_type=jnp.float32,
    )


def react_kernel(
    own_ref, east_ref, share_ref, partner_ref, photo_ref, coupled_ref, precond_ref, production_ref, loss_ref, *rest
):
    out_ref, mixed_ref, present_ref = rest[-3:]
    blocks = own_ref.shape[0] // 4
    species = out_ref.shape[0]
    lane = lax.broadcasted_iota(jnp.int32, (8, LANES), 1)
    step = pl.program_id(0)
    for m in range(blocks):
        span = slice(m * LANES, (m + 1) * LANES)
        index = jnp.broadcast_to(partner_ref[pl.ds(m, 1), :], (8, LANES))
        weight = None
        for k in range(TILES):
            rows = slice(8 * k, 8 * k + 8)
            own = regroup(*[own_ref[4 * m + s, rows, :] for s in range(4)], lane)
            east = regroup(*[east_ref[4 * m + s, rows, :] for s in range(4)], lane)
            for j in range(4):
                base = QUARTER * j + 8 * k
                chosen = jnp.take_along_axis(east[j], index, axis=1)
                if weight is None:
                    present = (own[0][0:1] > 0.0).astype(jnp.float32)
                    alive = (chosen[0:1] > 0.0).astype(jnp.float32)
                    weight = share_ref[pl.ds(m, 1), :] * present * alive
                    present_ref[:, span] = present
                mixed_ref[base : base + 8, span] = own[j] + weight * (chosen - own[j])
    width = blocks * LANES
    photo = jnp.concatenate([photo_ref[pl.ds(m, 1), :] for m in range(blocks)], axis=1)
    initial = mixed_ref[...]
    loss = jnp.broadcast_to(loss_ref[:, 0:1], (ROWS, width))
    source = jnp.broadcast_to(production_ref[:, 0:1], (ROWS, width)) * photo
    current = initial
    for _ in range(NEWTON):
        tendency = product(coupled_ref[...], current) + source - loss * current * current
        misfit = current - initial - time_step * tendency
        first_pass = product(precond_ref[...], misfit)
        second_pass = product(precond_ref[...], 2.0 * time_step * loss * current * first_pass)
        current = current - (first_pass - second_pass)
    result = current * present_ref[...]
    out_ref[...] = result[:species]


def react(part, parts, species, own, east, share, partner, photo, weights, so_far):
    sources = own.shape[0]
    blocks = 8
    steps = sources // (4 * blocks) // parts
    width = blocks * LANES
    first = part * steps

    def at_own(i):
        return (first + i, 0, 0)

    def at_east(i):
        return (i, 0, 0)

    def at_row(i):
        return (first + i, 0)

    def once(i):
        return (0, 0)

    in_specs = [
        pl.BlockSpec((4 * blocks, QUARTER, LANES), at_own),
        pl.BlockSpec((4 * blocks, QUARTER, LANES), at_east),
        pl.BlockSpec((blocks, LANES), at_row),
        pl.BlockSpec((blocks, LANES), at_row),
        pl.BlockSpec((blocks, LANES), at_row),
        pl.BlockSpec((ROWS, 3 * ROWS), once),
        pl.BlockSpec((ROWS, 3 * ROWS), once),
        pl.BlockSpec((ROWS, LANES), once),
        pl.BlockSpec((ROWS, LANES), once),
    ]
    operands = [own, east, share, partner, photo, *weights]
    aliases = {}
    if so_far is not None:
        in_specs.append(pl.BlockSpec(memory_space=pl.ANY))
        operands.append(so_far)
        aliases = {len(operands) - 1: 0}
    columns = steps * width
    return pl.pallas_call(
        react_kernel,
        grid=(steps,),
        out_shape=jax.ShapeDtypeStruct((species, sources * CAP), jnp.float32),
        in_specs=in_specs,
        out_specs=pl.BlockSpec((species, width), lambda i: (0, first + i)),
        scratch_shapes=[
            pltpu.VMEM((ROWS, width), jnp.float32),
            pltpu.VMEM((1, width), jnp.float32),
        ],
        input_output_aliases=aliases,
        compiler_params=pltpu.CompilerParams(vmem_limit_bytes=48 * 1024 * 1024),
        cost_estimate=pl.CostEstimate(
            flops=6 * 2 * 256 * 512 * columns, bytes_accessed=12 * ROWS * columns, transcendentals=0
        ),
        name="react",
    )(*operands)


def split(matrix):
    size = matrix.shape[0]
    padded = jnp.pad(matrix, ((0, ROWS - size), (0, ROWS - size)))
    high = lax.reduce_precision(padded, 8, 7)
    low = padded - high
    return jnp.concatenate([high, high, low], axis=1).astype(jnp.bfloat16)


def column(vector):
    return jnp.broadcast_to(jnp.pad(vector, (0, ROWS - vector.shape[0]))[:, None], (ROWS, LANES))


PARTS = 2


def shards(
    conc, dest_tile, mixing_share, partner, photolysis, production, loss, rates, pattern, precond
):
    species, parcels = conc.shape
    packed = pack(conc, dest_tile.reshape(parcels // LANES, LANES))
    arrived = lax.all_to_all(packed, ("lat", "lon"), split_axis=0, concat_axis=0, tiled=True)
    lon_count = lax.axis_size("lon")
    west = [(source, (source - 1) % lon_count) for source in range(lon_count)]
    length = arrived.shape[0] // PARTS
    eastern = [
        lax.ppermute(arrived[part * length : (part + 1) * length], "lon", west) for part in range(PARTS)
    ]
    coupled = rates * jnp.kron(pattern.astype(jnp.float32), jnp.ones((SB, SB), jnp.float32))
    weights = (split(coupled), split(precond), column(production), column(loss))
    rows = mixing_share.shape[0] // LANES
    share, index, photo = (a.reshape(rows, LANES) for a in (mixing_share, partner, photolysis))
    result = None
    for part in range(PARTS):
        result = react(
            part, PARTS, species, arrived, eastern[part], share, index, photo, weights, result
        )
    return result


def solution(mesh):
    placed = (
        P(None, ("lat", "lon")),
        P(("lat", "lon"), None),
        P(("lat", "lon")),
        P(("lat", "lon")),
        P(("lat", "lon")),
        P(),
        P(),
        P(),
        P(),
        P(),
    )
    return jax.shard_map(
        shards, mesh=mesh, in_specs=placed, out_specs=P(None, ("lat", "lon")), check_vma=False
    )
```

time: 162 us -> 123 us (0.76)
  Pallas kernels: 0 us -> 48 us
  local copies, waits for them, and re-layouts: 48.8 us -> 6.67 us
  matrix products: 18.6 us -> 0 us
  blocking collectives: 64.6 us -> 47.3 us
  other arithmetic: 5.71 us -> 0.27 us
  waiting for transfers between devices: 22 us -> 19 us
    pallas_call x0 -> x3, Pallas kernels: none -> 48 us  [the longest x1 33.2 us: pack(): pl.pallas_call(pack_kernel, out_shape=jax.ShapeDtypeStruct((devices, QUAR...]
    gather x2 -> x0, local copies, waits for them, and re-layouts: 22.1 us -> none  [shards(): partner_conc = jnp.take(eastern, partner_slot, axis=1)]
    dot_general x6 -> x0, matrix products: 18.6 us -> none  [the longest x2 7.59 us: chemistry(): jnp.dot(precond, 2.0 * time_step * loss[:, None] * current * first_pass,...]
    all_to_all x1, blocking collectives: 64.6 us -> 47.3 us  [shards(): lax.all_to_all(packed, ('lat', 'lon'), split_axis=0, concat_axis=0, tiled...]
    scatter x1 -> x0, local copies, waits for them, and re-layouts: 11.2 us -> none  [shards(): jnp.zeros((species, tile_slots), jnp.float32).at[:, send_slot].set(conc)]
    ppermute x1 -> x0, local copies, waits for them, and re-layouts: 4.8 us -> none  [passed_along(): return lax.ppermute(value, axis, pairs)]
    gt x2 -> x0, other arithmetic: 3.89 us -> none  [the longest x1 3.84 us: shards(): present_mask = (placed_parcels[0] > 0.0).astype(jnp.float32)]
    reshape x1 -> x0, local copies, waits for them, and re-layouts: 3.68 us -> none  [shards(): placed_parcels = arrived.reshape(species, tile_slots)]
  transfers between devices with their start and end apart: 1 -> 2, of which waited for: 1 -> 2; matrix products, arithmetic and copies ran while one was open for 4% -> 3% of each run, Pallas kernels for 0% -> 6%
where the time goes in v1:
time: 123 us
  Pallas kernels  48 us (39%)
  blocking collectives  47.3 us (38%)
  waiting for transfers between devices  19 us (15%)
  local copies, waits for them, and re-layouts  6.67 us (5%)
  starting transfers between devices  1.55 us (1%)
    all_to_all x1, blocking collectives, shards(): lax.all_to_all(packed, ('lat', 'lon'), split_axis=0, concat_axis=0, tiled...  47.3 us
    pallas_call x1, Pallas kernels, pack(): pl.pallas_call(pack_kernel, out_shape=jax.ShapeDtypeStruct((devices, QUAR...  33.2 us
    ppermute x2, waiting for transfers between devices, shards(): lax.ppermute(arrived[part * length:(part + 1) * length], 'lon', west)  19 us
    pallas_call x2, Pallas kernels, react(): pl.pallas_call(react_kernel, grid=(steps,), out_shape=jax.ShapeDtypeStruc...  14.9 us
    mul x2, local copies, waits for them, and re-layouts, shards(): jnp.kron(pattern.astype(jnp.float32), jnp.ones((SB, SB), jnp.float32))  2.8 us
  transfers between devices with their start and end apart: 2, of which 2 were waited for; matrix products, arithmetic and copies ran while one was open for 3% of the time, Pallas kernels for 6%

profile of v1, /device:TPU:1, one launch (start us, length us, event | category | flops | bytes accessed | tf_op | source)
XLA Modules:
  0.0 122.9 jit_solution(12593447911649948895)
XLA Ops:
  0.0 0.0 copy-start
  0.0 1.3 %copy-done = f32[150,2048]{1,0:T(8,128)S(1)} copy-done((f32[150,2048]{1,0:T(8,128)S(1)}, f32[150,2048]{1,0:T(8,128)}, u32[]{:S(2)}) %copy-start) | copy-done | bytes 1228824
  1.3 0.0 copy-start.1
  1.3 0.7 copy-done.1
  2.0 33.2 %pack.1 = f32[128,40,128]{2,1,0:T(8,128)S(1)} custom-call(f32[150,2048]{1,0:T(8,128)S(1)} %copy-done, s32[16,128]{1,0:T(8,128)S(1)} %bitcast.4), custom_call_target="tpu_custom_call" | custom-call | tf_op jit(solution)/shard_map/pack/pallas_call | solution.py:105
  35.2 47.3 %all_to_all.5.own_ref = f32[128,40,128]{2,1,0:T(8,128)S(1)} all-to-all(f32[128,40,128]{2,1,0:T(8,128)S(1)} %pack.1), channel_id=1, replica_groups=mesh['lat'=4,'lon'=32] {'lat','lon'}, dimensions={0} | all-to-all | bytes 5242880 | tf_op jit(solution)/shard_map/all_to_all | solution.py:246
  82.4 0.0 copy-start.8
  82.4 0.0 copy-start.9
  82.4 0.0 copy-start.7
  82.5 1.7 %fusion.2 = (f32[64,40,128]{2,1,0:T(8,128)}, f32[64,40,128]{2,1,0:T(8,128)}) fusion(f32[128,40,128]{2,1,0:T(8,128)S(1)} %all_to_all.5.own_ref), kind=kLoop, calls=%fused_computation.8 | loop fusion | bytes 5242880 | tf_op jit(solution)/shard_map/slice | solution.py:251
  84.1 1.1 collective-permute-start.1
  85.2 0.5 collective-permute-start
  85.7 0.0 copy-done.8
  85.7 0.0 copy-done.9
  85.7 0.0 copy-done.7
  85.7 0.0 copy-start.5
  85.7 0.0 copy-start.6
  85.7 1.2 mul.22
  86.9 1.6 %mul.23 = f32[150,150]{1,0:T(8,128)S(1)} reshape(f32[10,15,10,15]{3,2,1,0:T(8,128)} %mul.22) | data formatting | bytes 180000 | tf_op jit(solution)/shard_map/jit(kron)/mul | solution.py:253
  88.5 0.0 copy-done.5
  88.6 0.0 copy-start.2
  88.6 0.0 copy-start.3
  88.6 0.0 copy-start.4
  88.6 0.0 copy-done.6
  88.7 0.2 pad_maximum_fusion
  88.9 12.6 %collective-permute-done.1.east_ref = f32[64,40,128]{2,1,0:T(8,128)} collective-permute-done((f32[64,40,128]{2,1,0:T(8,128)}, f32[64,40,128]{2,1,0:T(8,128)}, u32[]{:S(2)}, u32[]{:S(2)}) %collective-permute-start.1) | collective-permute-done | bytes 1310752 | tf_op jit(solution)/shard_map/ppermute | solution.py:251
  101.5 0.1 broadcast_in_dim.9.loss_ref
  101.6 0.1 broadcast_in_dim.8.production_ref
  101.6 0.0 copy-done.2
  101.7 0.0 copy-done.3
  101.7 0.0 copy-done.4
  101.7 7.4 %react.2.rest_0_ = f32[150,4096]{1,0:T(8,128)} custom-call(f32[128,40,128]{2,1,0:T(8,128)S(1)} %all_to_all.5.own_ref, f32[64,40,128]{2,1,0:T(8,128)} %collective-permute-done.1.east_ref, f32[32,128]{1,0:T(8,128)S(1)} %bitcast.5, s32[32,128]{1,0:T(8,128)S(1)} %bitcast.7, f32[32,128]{1,0:T(8,128)S(1)} %bitcast.9, ...), custom_call_target="tpu_custom_call" | custom-call | flops 3221225472 | bytes 3932160 | tf_op jit(solution)/shard_map/react/pallas_call | solution.py:207
  109.1 6.4 %collective-permute-done.east_ref = f32[64,40,128]{2,1,0:T(8,128)} collective-permute-done((f32[64,40,128]{2,1,0:T(8,128)}, f32[64,40,128]{2,1,0:T(8,128)}, u32[]{:S(2)}, u32[]{:S(2)}) %collective-permute-start) | collective-permute-done | bytes 1310752 | tf_op jit(solution)/shard_map/ppermute | solution.py:251
  115.5 7.4 %react.3 = f32[150,4096]{1,0:T(8,128)} custom-call(f32[128,40,128]{2,1,0:T(8,128)S(1)} %all_to_all.5.own_ref, f32[64,40,128]{2,1,0:T(8,128)} %collective-permute-done.east_ref, f32[32,128]{1,0:T(8,128)S(1)} %bitcast.6, s32[32,128]{1,0:T(8,128)S(1)} %bitcast.8, f32[32,128]{1,0:T(8,128)S(1)} %bitcast.10, ...), custom_call_target="tpu_custom_call", output_to_operand_aliasing={{}: (9, {})} | custom-call | flops 3221225472 | bytes 3932160 | tf_op jit(solution)/shard_map/react/pallas_call | solution.py:207
  (6 shorter events, 0.1 us)
Async XLA Ops:
  0.0 1.3 %copy-start = (f32[150,2048]{1,0:T(8,128)S(1)}, f32[150,2048]{1,0:T(8,128)}, u32[]{:S(2)}) copy-start(f32[150,2048]{1,0:T(8,128)} %conc_ref.1) | copy-start | bytes 3686404
  1.3 0.7 copy-start.1
  82.4 3.2 %copy-start.8 = (f32[150]{0:T(256)S(1)}, f32[150]{0:T(256)}, u32[]{:S(2)}) copy-start(f32[150]{0:T(256)} %param.15) | copy-start | bytes 1804
  82.4 3.2 %copy-start.9 = (f32[150]{0:T(256)S(1)}, f32[150]{0:T(256)}, u32[]{:S(2)}) copy-start(f32[150]{0:T(256)} %param.16) | copy-start | bytes 1804
  82.4 3.3 %copy-start.7 = (s32[10,10]{1,0:T(8,128)S(1)}, s32[10,10]{1,0:T(8,128)}, u32[]{:S(2)}) copy-start(s32[10,10]{1,0:T(8,128)} %param.18) | copy-start | bytes 1204
  84.1 17.3 %collective-permute-start.1 = (f32[64,40,128]{2,1,0:T(8,128)}, f32[64,40,128]{2,1,0:T(8,128)}, u32[]{:S(2)}, u32[]{:S(2)}) collective-permute-start(f32[64,40,128]{2,1,0:T(8,128)} %get-tuple-element.5), channel_id=1, source_target_pairs={{0,31},{1,0},{2,1},{3,2},{4,3},{5,4},{6,5},{7,6},{8,7},{9,8},{10,9... | collective-permute-start | bytes 3932168 | tf_op jit(solution)/shard_map/ppermute | solution.py:251
  85.2 30.3 %collective-permute-start = (f32[64,40,128]{2,1,0:T(8,128)}, f32[64,40,128]{2,1,0:T(8,128)}, u32[]{:S(2)}, u32[]{:S(2)}) collective-permute-start(f32[64,40,128]{2,1,0:T(8,128)} %get-tuple-element.6), channel_id=1, source_target_pairs={{0,31},{1,0},{2,1},{3,2},{4,3},{5,4},{6,5},{7,6},{8,7},{9,8},{10,9... | collective-permute-start | bytes 3932168 | tf_op jit(solution)/shard_map/ppermute | solution.py:251
  85.7 2.8 %copy-start.5 = (f32[150,150]{1,0:T(8,128)S(1)}, f32[150,150]{1,0:T(8,128)}, u32[]{:S(2)}) copy-start(f32[150,150]{1,0:T(8,128)} %param.17) | copy-start | bytes 270004
  85.7 2.9 %copy-start.6 = (f32[150,150]{1,0:T(8,128)S(1)}, f32[150,150]{1,0:T(8,128)}, u32[]{:S(2)}) copy-start(f32[150,150]{1,0:T(8,128)} %param.19) | copy-start | bytes 270004
  88.6 13.1 %copy-start.2 = (f32[4096]{0:T(1024)S(1)}, f32[4096]{0:T(1024)}, u32[]{:S(2)}) copy-start(f32[4096]{0:T(1024)} %param.12) | copy-start | bytes 49156
  88.6 13.1 %copy-start.3 = (s32[4096]{0:T(1024)S(1)}, s32[4096]{0:T(1024)}, u32[]{:S(2)}) copy-start(s32[4096]{0:T(1024)} %param.13) | copy-start | bytes 49156
  88.6 13.1 %copy-start.4 = (f32[4096]{0:T(1024)S(1)}, f32[4096]{0:T(1024)}, u32[]{:S(2)}) copy-start(f32[4096]{0:T(1024)} %param.14) | copy-start | bytes 49156

commit v2 on v1

v2 whole, which is shorter than its diff:
```python
import jax
import jax.numpy as jnp
from jax import lax
from jax.experimental import pallas as pl
from jax.experimental.pallas import tpu as pltpu
from jax.sharding import Mesh
from jax.sharding import PartitionSpec as P

SB = 15
NEWTON = 2
time_step = 0.5

LANES = 128
CAP = 32
QUARTER = 40
ROWS = 4 * QUARTER
TILES = QUARTER // 8
GROUP = 256
TOGETHER = 4


def regroup(first, second, third, fourth, lane):
    low_half = lane < 64
    low_quarter = (lane % 64) < 32
    t0 = jnp.where(low_half, first, pltpu.roll(third, 64, 1))
    t2 = jnp.where(low_half, pltpu.roll(first, 64, 1), third)
    t1 = jnp.where(low_half, second, pltpu.roll(fourth, 64, 1))
    t3 = jnp.where(low_half, pltpu.roll(second, 64, 1), fourth)
    return (
        jnp.where(low_quarter, t0, pltpu.roll(t1, 32, 1)),
        jnp.where(low_quarter, pltpu.roll(t0, 96, 1), t1),
        jnp.where(low_quarter, t2, pltpu.roll(t3, 32, 1)),
        jnp.where(low_quarter, pltpu.roll(t2, 96, 1), t3),
    )


def pack_kernel(core_ref, conc_ref, targets_ref, out_ref, parts_ref, place_ref, group_ref, sums_ref):
    species, parcels = conc_ref.shape
    row = lax.broadcasted_iota(jnp.int32, (LANES, LANES), 0)
    column = lax.broadcasted_iota(jnp.int32, (LANES, LANES), 1)
    earlier = (row < column).astype(jnp.float32).astype(jnp.bfloat16)
    sums_of = jnp.concatenate([earlier, jnp.ones((LANES, LANES), jnp.bfloat16)], axis=1)
    counted = jnp.zeros((LANES, LANES), jnp.float32)
    for block in range(parcels // LANES):
        span = slice(block * LANES, (block + 1) * LANES)
        targets = targets_ref[block : block + 1, :]
        onehot = (row == targets).astype(jnp.float32)
        sums = jnp.dot(onehot.astype(jnp.bfloat16), sums_of, preferred_element_type=jnp.float32)
        ranking = jnp.sum(onehot * (sums[:, :LANES] + counted), axis=0, keepdims=True)
        counted = counted + sums[:, LANES:]
        slot = targets * CAP + ranking.astype(jnp.int32)
        group_ref[:, span] = jnp.broadcast_to(slot // GROUP, (16, LANES))
        place = jnp.broadcast_to((slot % GROUP).astype(jnp.float32), (LANES, LANES))
        place = jnp.transpose(place).astype(jnp.int32)
        for half in range(GROUP // LANES):
            here = (place == column + half * LANES).astype(jnp.float32)
            place_ref[span, half * LANES : (half + 1) * LANES] = here.astype(jnp.bfloat16)
    conc = conc_ref[...]
    low = conc - conc.astype(jnp.bfloat16).astype(jnp.float32)
    filler = jnp.zeros((ROWS - species, parcels), jnp.float32)
    parts_ref[0:ROWS, :] = jnp.concatenate([conc, filler], axis=0).astype(jnp.bfloat16)
    parts_ref[ROWS:, :] = jnp.concatenate([low, filler], axis=0).astype(jnp.bfloat16)
    lane = lax.broadcasted_iota(jnp.int32, (8, LANES), 1)
    core = core_ref[0]
    around = out_ref.shape[0] // 4

    def step(i, carry):
        chosen = []
        for t in range(TOGETHER):
            mine = (group_ref[...] == i * TOGETHER + t).astype(jnp.float32).astype(jnp.bfloat16)
            chosen.append(parts_ref[...] * jnp.concatenate([mine] * (2 * ROWS // 16), axis=0))
        moved = jnp.dot(
            jnp.concatenate(chosen, axis=0), place_ref[...], preferred_element_type=jnp.float32
        )
        for t in range(TOGETHER):
            base = 2 * t * ROWS
            sums_ref[...] = moved[base : base + ROWS] + moved[base + ROWS : base + 2 * ROWS]
            for half in range(GROUP // LANES):
                span = slice(half * LANES, (half + 1) * LANES)
                quad = (i * TOGETHER + t) * (GROUP // LANES) + half
                for k in range(TILES):
                    rows = slice(8 * k, 8 * k + 8)
                    quarters = [sums_ref[QUARTER * j + 8 * k : QUARTER * j + 8 * k + 8, span] for j in range(4)]
                    for d, chunk in enumerate(regroup(*quarters, lane)):
                        chip = quad * 2 + d // 2
                        odd = d % 2
                        out_ref[chip, jnp.where(core == 0, odd, 2 - odd), rows, :] = chunk
                        if not odd:
                            west = chip // around * around + (chip + around - 1) % around
                            out_ref[west, jnp.where(core == 0, 2, 0), rows, :] = chunk
        return carry

    lax.fori_loop(0, 16 // TOGETHER, step, 0)


def pack(core, conc, targets, chips):
    parcels = conc.shape[1]
    in_vmem = pl.BlockSpec(memory_space=pltpu.VMEM)
    return pl.pallas_call(
        pack_kernel,
        out_shape=jax.ShapeDtypeStruct((chips, 3, QUARTER, LANES), jnp.float32),
        in_specs=[pl.BlockSpec(memory_space=pltpu.SMEM), in_vmem, in_vmem],
        out_specs=in_vmem,
        scratch_shapes=[
            pltpu.VMEM((2 * ROWS, parcels), jnp.bfloat16),
            pltpu.VMEM((parcels, GROUP), jnp.bfloat16),
            pltpu.VMEM((16, parcels), jnp.int32),
            pltpu.VMEM((ROWS, GROUP), jnp.float32),
        ],
        compiler_params=pltpu.CompilerParams(vmem_limit_bytes=40 * 1024 * 1024),
        name="pack",
    )(core, conc, targets)


def product(weights, value):
    high = value.astype(jnp.bfloat16)
    low = (value - high.astype(jnp.float32)).astype(jnp.bfloat16)
    return jnp.dot(
        weights,
        jnp.concatenate([high, low, high], axis=0),
        preferred_element_type=jnp.float32,
    )


def react_kernel(
    core_ref, mine_ref, other_ref, share_ref, partner_ref, photo_ref, coupled_ref, precond_ref, production_ref, loss_ref, *rest
):
    out_ref, mixed_ref, present_ref = rest[-3:]
    blocks = mine_ref.shape[0] // 2
    core = core_ref[0]
    species = out_ref.shape[0]
    lane = lax.broadcasted_iota(jnp.int32, (8, LANES), 1)

    def sources(m, rows, at_mine, at_other):
        parts = []
        for chip in (2 * m, 2 * m + 1):
            mine = mine_ref[chip, at_mine, rows, :]
            other = other_ref[chip, at_other, rows, :]
            parts += [jnp.where(core == 0, mine, other), jnp.where(core == 0, other, mine)]
        return parts

    for m in range(blocks):
        span = slice(m * LANES, (m + 1) * LANES)
        index = jnp.broadcast_to(partner_ref[pl.ds(m, 1), :], (8, LANES))
        weight = None
        for k in range(TILES):
            rows = slice(8 * k, 8 * k + 8)
            own = regroup(*sources(m, rows, core, 1 - core), lane)
            east = regroup(*sources(m, rows, 1 - core, core), lane)
            for j in range(4):
                base = QUARTER * j + 8 * k
                chosen = jnp.take_along_axis(east[j], index, axis=1)
                if weight is None:
                    present = (own[0][0:1] > 0.0).astype(jnp.float32)
                    alive = (chosen[0:1] > 0.0).astype(jnp.float32)
                    weight = share_ref[pl.ds(m, 1), :] * present * alive
                    present_ref[:, span] = present
                mixed_ref[base : base + 8, span] = own[j] + weight * (chosen - own[j])
    width = blocks * LANES
    photo = jnp.concatenate([photo_ref[pl.ds(m, 1), :] for m in range(blocks)], axis=1)
    initial = mixed_ref[...]
    loss = jnp.broadcast_to(loss_ref[:, 0:1], (ROWS, width))
    source = jnp.broadcast_to(production_ref[:, 0:1], (ROWS, width)) * photo
    current = initial
    for _ in range(NEWTON):
        tendency = product(coupled_ref[...], current) + source - loss * current * current
        misfit = current - initial - time_step * tendency
        first_pass = product(precond_ref[...], misfit)
        second_pass = product(precond_ref[...], 2.0 * time_step * loss * current * first_pass)
        current = current - (first_pass - second_pass)
    result = current * present_ref[...]
    out_ref[...] = result[:species]


def react(part, parts, species, core, mine, other, share, partner, photo, weights, so_far):
    chips = mine.shape[0]
    blocks = 8
    steps = chips // (2 * blocks) // parts
    width = blocks * LANES
    first = part * steps

    def at_row(i):
        return (first + i, 0)

    def once(i):
        return (0, 0)

    in_specs = [
        pl.BlockSpec(memory_space=pltpu.SMEM),
        pl.BlockSpec((2 * blocks, 2, QUARTER, LANES), lambda i: (first + i, 0, 0, 0)),
        pl.BlockSpec((2 * blocks, 2, QUARTER, LANES), lambda i: (i, 0, 0, 0)),
        pl.BlockSpec((blocks, LANES), at_row),
        pl.BlockSpec((blocks, LANES), at_row),
        pl.BlockSpec((blocks, LANES), at_row),
        pl.BlockSpec((ROWS, 3 * ROWS), once),
        pl.BlockSpec((ROWS, 3 * ROWS), once),
        pl.BlockSpec((ROWS, LANES), once),
        pl.BlockSpec((ROWS, LANES), once),
    ]
    operands = [core, mine, other, share, partner, photo, *weights]
    aliases = {}
    if so_far is not None:
        in_specs.append(pl.BlockSpec(memory_space=pl.ANY))
        operands.append(so_far)
        aliases = {len(operands) - 1: 0}
    columns = steps * width
    return pl.pallas_call(
        react_kernel,
        grid=(steps,),
        out_shape=jax.ShapeDtypeStruct((species, chips * 2 * CAP), jnp.float32),
        in_specs=in_specs,
        out_specs=pl.BlockSpec((species, width), lambda i: (0, first + i)),
        scratch_shapes=[
            pltpu.VMEM((ROWS, width), jnp.float32),
            pltpu.VMEM((1, width), jnp.float32),
        ],
        input_output_aliases=aliases,
        compiler_params=pltpu.CompilerParams(vmem_limit_bytes=48 * 1024 * 1024),
        cost_estimate=pl.CostEstimate(
            flops=6 * 2 * 256 * 512 * columns, bytes_accessed=12 * ROWS * columns, transcendentals=0
        ),
        name="react",
    )(*operands)


def split(matrix):
    size = matrix.shape[0]
    padded = jnp.pad(matrix, ((0, ROWS - size), (0, ROWS - size)))
    high = lax.reduce_precision(padded, 8, 7)
    low = padded - high
    return jnp.concatenate([high, high, low], axis=1).astype(jnp.bfloat16)


def column(vector):
    return jnp.broadcast_to(jnp.pad(vector, (0, ROWS - vector.shape[0]))[:, None], (ROWS, LANES))


PARTS = 2


def shards(
    conc, dest_tile, mixing_share, partner, photolysis, production, loss, rates, pattern, precond
):
    species, parcels = conc.shape
    chips = lax.axis_size("lat") * lax.axis_size("chip")
    core = lax.axis_index("core").astype(jnp.int32)[None]
    packed = pack(core, conc, dest_tile.reshape(parcels // LANES, LANES), chips)
    arrived = lax.all_to_all(packed, ("lat", "chip"), split_axis=0, concat_axis=0, tiled=True)
    length = chips // PARTS
    others = [
        lax.ppermute(arrived[part * length : (part + 1) * length, 1:], "core", ((0, 1), (1, 0)))
        for part in range(PARTS)
    ]
    coupled = rates * jnp.kron(pattern.astype(jnp.float32), jnp.ones((SB, SB), jnp.float32))
    weights = (split(coupled), split(precond), column(production), column(loss))
    rows = mixing_share.shape[0] // LANES
    share, index, photo = (a.reshape(rows, LANES) for a in (mixing_share, partner, photolysis))
    result = None
    for part in range(PARTS):
        result = react(
            part, PARTS, species, core, arrived, others[part], share, index, photo, weights, result
        )
    return result


def solution(mesh):
    lat_count, lon_count = mesh.devices.shape
    by_core = Mesh(mesh.devices.reshape(lat_count, lon_count // 2, 2), ("lat", "chip", "core"))
    tiles = ("lat", "chip", "core")
    placed = (P(None, tiles), P(tiles, None), P(tiles), P(tiles), P(tiles), P(), P(), P(), P(), P())
    return jax.shard_map(
        shards, mesh=by_core, in_specs=placed, out_specs=P(None, tiles), check_vma=False
    )
```

time: 123 us -> 94.4 us (0.77)
  Pallas kernels: 48 us -> 21.2 us
  waiting for transfers between devices: 19 us -> 0.01 us
  blocking collectives: 47.3 us -> 60 us
  local copies, waits for them, and re-layouts: 6.67 us -> 10.1 us
    pallas_call x1, Pallas kernels: 33.2 us -> 8.2 us  [pack(): pl.pallas_call(pack_kernel, out_shape=jax.ShapeDtypeStruct((chips, 3, QUA...]
    ppermute x2, waiting for transfers between devices: 19 us -> 0.01 us  [shards(): lax.ppermute(arrived[part * length:(part + 1) * length, 1:], 'core', ((0,...]
    all_to_all x1, blocking collectives: 47.3 us -> 60 us  [shards(): lax.all_to_all(packed, ('lat', 'chip'), split_axis=0, concat_axis=0, tile...]
    unnamed x20 -> x24, local copies, waits for them, and re-layouts: 2.03 us -> 5.2 us
    pallas_call x2, Pallas kernels: 14.9 us -> 13 us  [react(): pl.pallas_call(react_kernel, grid=(steps,), out_shape=jax.ShapeDtypeStruc...]
  transfers between devices with their start and end apart: 2 -> 2, of which waited for: 2 -> 0; matrix products, arithmetic and copies ran while one was open for 3% -> 3% of each run, Pallas kernels for 6% -> 7%
where the time goes in v2:
time: 94.4 us; the launch traced here: 94.1 us
  blocking collectives  60 us (64%)
  Pallas kernels  21.2 us (22%)
  local copies, waits for them, and re-layouts  10.1 us (11%)
  starting transfers between devices  2.33 us (2%)
    all_to_all x1, blocking collectives, shards(): lax.all_to_all(packed, ('lat', 'chip'), split_axis=0, concat_axis=0, tile...  60 us
    pallas_call x2, Pallas kernels, react(): pl.pallas_call(react_kernel, grid=(steps,), out_shape=jax.ShapeDtypeStruc...  13 us
    pallas_call x1, Pallas kernels, pack(): pl.pallas_call(pack_kernel, out_shape=jax.ShapeDtypeStruct((chips, 3, QUA...  8.2 us
    unnamed x24, local copies, waits for them, and re-layouts  5.2 us
    mul x2, local copies, waits for them, and re-layouts, shards(): jnp.kron(pattern.astype(jnp.float32), jnp.ones((SB, SB), jnp.float32))  2.85 us
    ppermute x2, starting transfers between devices, shards(): lax.ppermute(arrived[part * length:(part + 1) * length, 1:], 'core', ((0,...  2.33 us
  transfers between devices with their start and end apart: 2, of which 0 were waited for; matrix products, arithmetic and copies ran while one was open for 3% of the time, Pallas kernels for 7%

profile of v2, /device:TPU:1, one launch (start us, length us, event | category | flops | bytes accessed | tf_op | source)
XLA Modules:
  0.0 94.1 jit_solution(1373279573666194710)
XLA Ops:
  0.0 0.0 copy-start.2
  0.0 1.3 %copy-done.2 = f32[150,2048]{1,0:T(8,128)S(1)} copy-done((f32[150,2048]{1,0:T(8,128)S(1)}, f32[150,2048]{1,0:T(8,128)}, u32[]{:S(2)}) %copy-start.2) | copy-done | bytes 1228824
  1.3 0.0 copy-start.3
  1.3 0.7 copy-done.3
  2.0 8.2 %pack.1 = f32[64,3,40,128]{3,2,1,0:T(8,128)S(1)} custom-call(s32[1]{0:T(128)} %bitcast.core_ref, f32[150,2048]{1,0:T(8,128)S(1)} %copy-done.2, s32[16,128]{1,0:T(8,128)S(1)} %bitcast.5), custom_call_target="tpu_custom_call" | custom-call | tf_op jit(solution)/shard_map/pack/pallas_call | solution.py:99
  10.2 60.0 %all_to_all.5.mine_ref = f32[64,3,40,128]{3,2,1,0:T(8,128)S(1)} all-to-all(f32[64,3,40,128]{3,2,1,0:T(8,128)S(1)} %pack.1), channel_id=1, replica_groups=mesh['lat'=4,'chip'=16,'core'=2] {'lat','chip'}, dimensions={0} | all-to-all | bytes 7864320 | tf_op jit(solution)/shard_map/all_to_all | solution.py:248
  70.2 0.0 copy-start
  70.2 0.0 copy-start.10
  70.2 0.0 copy-start.11
  70.3 0.0 copy-start.9
  70.3 1.8 %fusion.2 = (f32[32,2,40,128]{3,2,1,0:T(8,128)}, f32[32,2,40,128]{3,2,1,0:T(8,128)}) fusion(f32[64,3,40,128]{3,2,1,0:T(8,128)S(1)} %all_to_all.5.mine_ref), kind=kLoop, calls=%fused_computation.8 | loop fusion | bytes 5242880 | tf_op jit(solution)/shard_map/slice | solution.py:251
  72.1 0.8 copy-done
  72.9 2.3 %collective-permute-start.1 = (f32[32,2,40,128]{3,2,1,0:T(8,128)}, f32[32,2,40,128]{3,2,1,0:T(8,128)S(1)}, u32[]{:S(2)}, u32[]{:S(2)}) collective-permute-start(f32[32,2,40,128]{3,2,1,0:T(8,128)} %get-tuple-element.5), channel_id=1, source_target_pairs={{0,1},{1,0},{2,3},{3,2},{4,5},{5,4},{6,7},{7,6},{8,9},{9,8},{10,11... | collective-permute-start | bytes 3932168 | tf_op jit(solution)/shard_map/ppermute | solution.py:251
  75.3 0.0 collective-permute-start
  75.3 0.0 copy-done.10
  75.3 0.0 copy-done.11
  75.3 0.0 copy-done.9
  75.3 0.0 copy-start.7
  75.3 0.0 copy-start.8
  75.3 1.2 %mul.22 = f32[10,15,10,15]{3,2,1,0:T(8,128)} broadcast(f32[10,10]{1,0:T(8,128)S(1)} %convert_element_type.11), dimensions={0,2} | broadcast | bytes 90400 | tf_op jit(solution)/shard_map/jit(kron)/mul | solution.py:254
  76.6 1.6 %mul.23 = f32[150,150]{1,0:T(8,128)S(1)} reshape(f32[10,15,10,15]{3,2,1,0:T(8,128)} %mul.22) | data formatting | bytes 180000 | tf_op jit(solution)/shard_map/jit(kron)/mul | solution.py:254
  78.2 0.0 copy-done.7
  78.2 0.0 copy-start.4
  78.2 0.0 copy-start.5
  78.2 0.0 copy-start.6
  78.3 0.0 copy-done.8
  78.3 0.2 pad_maximum_fusion
  78.5 0.0 collective-permute-done.1.other_ref
  78.6 0.1 broadcast_in_dim.12.loss_ref
  78.6 0.1 broadcast_in_dim.11.production_ref
  78.7 0.2 copy-done.4
  78.9 0.0 copy-done.5
  78.9 0.0 copy-done.6
  79.0 0.0 copy-start.1
  79.0 2.1 %copy-done.1 = f32[64,3,40,128]{3,2,1,0:T(8,128)S(1)} copy-done((f32[64,3,40,128]{3,2,1,0:T(8,128)S(1)}, f32[64,3,40,128]{3,2,1,0:T(8,128)}, u32[]{:S(2)}) %copy-start.1) | copy-done | bytes 3932184
  81.1 6.5 %react.2.rest_0_ = f32[150,4096]{1,0:T(8,128)} custom-call(s32[1]{0:T(128)} %bitcast.core_ref, f32[64,3,40,128]{3,2,1,0:T(8,128)S(1)} %copy-done.1, f32[32,2,40,128]{3,2,1,0:T(8,128)S(1)} %collective-permute-done.1.other_ref, f32[32,128]{1,0:T(8,128)S(1)} %bitcast.6, s32[32,128]{1,0:T(8,128)S(1)} %bitcast.8, f32[32,128]{1,0:T(8,128)S(1)} %bitcast.10, ...), custom_call_target="tpu_custom_call" | custom-call | flops 3221225472 | bytes 3932160 | tf_op jit(solution)/shard_map/react/pallas_call | solution.py:207
  87.6 0.0 collective-permute-done.other_ref
  87.6 6.5 %react.3 = f32[150,4096]{1,0:T(8,128)} custom-call(s32[1]{0:T(128)} %bitcast.core_ref, f32[64,3,40,128]{3,2,1,0:T(8,128)S(1)} %copy-done.1, f32[32,2,40,128]{3,2,1,0:T(8,128)S(1)} %collective-permute-done.other_ref, f32[32,128]{1,0:T(8,128)S(1)} %bitcast.7, s32[32,128]{1,0:T(8,128)S(1)} %bitcast.9, ...), custom_call_target="tpu_custom_call", output_to_operand_aliasing={{}: (10, {})} | custom-call | flops 3221225472 | bytes 3932160 | tf_op jit(solution)/shard_map/react/pallas_call | solution.py:207
  (6 shorter events, 0.1 us)
Async XLA Ops:
  0.0 1.3 %copy-start.2 = (f32[150,2048]{1,0:T(8,128)S(1)}, f32[150,2048]{1,0:T(8,128)}, u32[]{:S(2)}) copy-start(f32[150,2048]{1,0:T(8,128)} %conc_ref.1) | copy-start | bytes 3686404
  1.3 0.7 copy-start.3
  70.2 2.7 %copy-start = (f32[64,3,40,128]{3,2,1,0:T(8,128)}, f32[64,3,40,128]{3,2,1,0:T(8,128)S(1)}, u32[]{:S(2)}) copy-start(f32[64,3,40,128]{3,2,1,0:T(8,128)S(1)} %all_to_all.5.mine_ref) | copy-start | bytes 11796484
  70.2 5.0 %copy-start.10 = (f32[150]{0:T(256)S(1)}, f32[150]{0:T(256)}, u32[]{:S(2)}) copy-start(f32[150]{0:T(256)} %param.15) | copy-start | bytes 1804
  70.2 5.0 %copy-start.11 = (f32[150]{0:T(256)S(1)}, f32[150]{0:T(256)}, u32[]{:S(2)}) copy-start(f32[150]{0:T(256)} %param.16) | copy-start | bytes 1804
  70.3 5.1 %copy-start.9 = (s32[10,10]{1,0:T(8,128)S(1)}, s32[10,10]{1,0:T(8,128)}, u32[]{:S(2)}) copy-start(s32[10,10]{1,0:T(8,128)} %param.18) | copy-start | bytes 1204
  72.9 5.6 %collective-permute-start.1 = (f32[32,2,40,128]{3,2,1,0:T(8,128)}, f32[32,2,40,128]{3,2,1,0:T(8,128)S(1)}, u32[]{:S(2)}, u32[]{:S(2)}) collective-permute-start(f32[32,2,40,128]{3,2,1,0:T(8,128)} %get-tuple-element.5), channel_id=1, source_target_pairs={{0,1},{1,0},{2,3},{3,2},{4,5},{5,4},{6,7},{7,6},{8,9},{9,8},{10,11... | collective-permute-start | bytes 3932168 | tf_op jit(solution)/shard_map/ppermute | solution.py:251
  75.3 12.3 %collective-permute-start = (f32[32,2,40,128]{3,2,1,0:T(8,128)}, f32[32,2,40,128]{3,2,1,0:T(8,128)S(1)}, u32[]{:S(2)}, u32[]{:S(2)}) collective-permute-start(f32[32,2,40,128]{3,2,1,0:T(8,128)} %get-tuple-element.6), channel_id=1, source_target_pairs={{0,1},{1,0},{2,3},{3,2},{4,5},{5,4},{6,7},{7,6},{8,9},{9,8},{10,11... | collective-permute-start | bytes 3932168 | tf_op jit(solution)/shard_map/ppermute | solution.py:251
  75.3 2.9 %copy-start.7 = (f32[150,150]{1,0:T(8,128)S(1)}, f32[150,150]{1,0:T(8,128)}, u32[]{:S(2)}) copy-start(f32[150,150]{1,0:T(8,128)} %param.17) | copy-start | bytes 270004
  75.3 2.9 %copy-start.8 = (f32[150,150]{1,0:T(8,128)S(1)}, f32[150,150]{1,0:T(8,128)}, u32[]{:S(2)}) copy-start(f32[150,150]{1,0:T(8,128)} %param.19) | copy-start | bytes 270004
  78.2 0.7 copy-start.4
  78.2 0.7 copy-start.5
  78.2 0.7 copy-start.6
  79.0 2.1 %copy-start.1 = (f32[64,3,40,128]{3,2,1,0:T(8,128)S(1)}, f32[64,3,40,128]{3,2,1,0:T(8,128)}, u32[]{:S(2)}) copy-start(f32[64,3,40,128]{3,2,1,0:T(8,128)} %copy-done) | copy-start | bytes 11796484

commit v3 on v2

v3 whole, which is shorter than its diff:
```python
import jax
import jax.numpy as jnp
from jax import lax
from jax.experimental import pallas as pl
from jax.experimental.pallas import tpu as pltpu
from jax.sharding import Mesh
from jax.sharding import PartitionSpec as P

SB = 15
NEWTON = 2
time_step = 0.5

LANES = 128
CAP = 32
QUARTER = 20
HALF = 4 * QUARTER
ROWS = 2 * HALF
CHUNK = 3 * QUARTER
GROUP = 256
TOGETHER = 4
PARTS = 2


def regroup(parts):
    first, second, third, fourth = parts
    lane = lax.broadcasted_iota(jnp.int32, first.shape, 1)
    low_half = (lane & 64) == 0
    low_quarter = (lane & 32) == 0
    other_quarter = lane ^ 32

    def halves(a, b):
        moved = pltpu.roll(jnp.where(low_half, b, a), 64, 1)
        return jnp.where(low_half, a, moved), jnp.where(low_half, moved, b)

    def quarters(a, b):
        moved = jnp.take_along_axis(jnp.where(low_quarter, b, a), other_quarter, axis=1)
        return jnp.where(low_quarter, a, moved), jnp.where(low_quarter, moved, b)

    t0, t2 = halves(first, third)
    t1, t3 = halves(second, fourth)
    return (*quarters(t0, t1), *quarters(t2, t3))


def pack_kernel(conc_ref, targets_ref, out_ref, parts_ref, place_ref, group_ref, sums_ref):
    species, parcels = conc_ref.shape
    row = lax.broadcasted_iota(jnp.int32, (LANES, LANES), 0)
    column = lax.broadcasted_iota(jnp.int32, (LANES, LANES), 1)
    earlier = (row < column).astype(jnp.float32).astype(jnp.bfloat16)
    sums_of = jnp.concatenate([earlier, jnp.ones((LANES, LANES), jnp.bfloat16)], axis=1)
    counted = jnp.zeros((LANES, LANES), jnp.float32)
    for block in range(parcels // LANES):
        span = slice(block * LANES, (block + 1) * LANES)
        targets = targets_ref[block : block + 1, :]
        onehot = (row == targets).astype(jnp.float32)
        sums = jnp.dot(onehot.astype(jnp.bfloat16), sums_of, preferred_element_type=jnp.float32)
        ranking = jnp.sum(onehot * (sums[:, :LANES] + counted), axis=0, keepdims=True)
        counted = counted + sums[:, LANES:]
        slot = targets * CAP + ranking.astype(jnp.int32)
        group_ref[:, span] = jnp.broadcast_to(slot // GROUP, (16, LANES))
        place = jnp.broadcast_to((slot % GROUP).astype(jnp.float32), (LANES, LANES))
        place = jnp.transpose(place).astype(jnp.int32)
        for side in range(GROUP // LANES):
            here = (place == column + side * LANES).astype(jnp.float32)
            place_ref[span, side * LANES : (side + 1) * LANES] = here.astype(jnp.bfloat16)
    conc = conc_ref[...]
    low = conc - conc.astype(jnp.bfloat16).astype(jnp.float32)
    filler = jnp.zeros((ROWS - species, parcels), jnp.float32)
    parts_ref[0:ROWS, :] = jnp.concatenate([conc, filler], axis=0).astype(jnp.bfloat16)
    parts_ref[ROWS:, :] = jnp.concatenate([low, filler], axis=0).astype(jnp.bfloat16)
    around = 16

    def step(i, carry):
        chosen = []
        for t in range(TOGETHER):
            mine = (group_ref[...] == i * TOGETHER + t).astype(jnp.float32).astype(jnp.bfloat16)
            chosen.append(parts_ref[...] * jnp.concatenate([mine] * (2 * ROWS // 16), axis=0))
        moved = jnp.dot(
            jnp.concatenate(chosen, axis=0), place_ref[...], preferred_element_type=jnp.float32
        )
        for t in range(TOGETHER):
            base = 2 * t * ROWS
            sums = moved[base : base + ROWS] + moved[base + ROWS : base + 2 * ROWS]
            for side in range(GROUP // LANES):
                sums_ref[t, side] = sums[:, side * LANES : (side + 1) * LANES]
        for t in range(TOGETHER):
            for side in range(GROUP // LANES):
                quad = (i * TOGETHER + t) * (GROUP // LANES) + side
                for half in range(2):
                    quarters = [
                        sums_ref[t, side, half * HALF + QUARTER * j : half * HALF + QUARTER * (j + 1), :]
                        for j in range(4)
                    ]
                    for d, chunk in enumerate(regroup(quarters)):
                        chip = quad * 2 + d // 2
                        to = (chip * 2 + half) * CHUNK + (d % 2) * QUARTER
                        out_ref[pl.ds(to, QUARTER), :] = chunk
                        if d % 2 == 0:
                            west = chip // around * around + (chip + around - 1) % around
                            to = (west * 2 + half) * CHUNK + 2 * QUARTER
                            out_ref[pl.ds(to, QUARTER), :] = chunk
        return carry

    lax.fori_loop(0, 16 // TOGETHER, step, 0)


IN_VMEM = pl.BlockSpec(memory_space=pltpu.VMEM)
IN_SMEM = pl.BlockSpec(memory_space=pltpu.SMEM)


def pack(conc, targets, devices):
    parcels = conc.shape[1]
    return pl.pallas_call(
        pack_kernel,
        out_shape=jax.ShapeDtypeStruct((devices * CHUNK, LANES), jnp.float32),
        in_specs=[IN_VMEM, IN_VMEM],
        out_specs=IN_VMEM,
        scratch_shapes=[
            pltpu.VMEM((2 * ROWS, parcels), jnp.bfloat16),
            pltpu.VMEM((parcels, GROUP), jnp.bfloat16),
            pltpu.VMEM((16, parcels), jnp.int32),
            pltpu.VMEM((TOGETHER, GROUP // LANES, ROWS, LANES), jnp.float32),
        ],
        compiler_params=pltpu.CompilerParams(vmem_limit_bytes=40 * 1024 * 1024),
        name="pack",
    )(conc, targets)


def mix_kernel(first, core_ref, arrived_ref, share_ref, partner_ref, keep_ref, give_ref):
    blocks = keep_ref.shape[0]
    core = core_ref[0]

    def body(m, carry):
        tiles = []
        for tile in range(3):
            parts = []
            for s in range(4):
                start = ((first + m) * 4 + s) * CHUNK + tile * QUARTER
                parts.append(arrived_ref[pl.ds(start, QUARTER), :])
            tiles.append(regroup(parts))
        mixed = []
        for tile in range(2):
            own, east = tiles[tile], tiles[tile + 1]
            place = tile * 32 + first + m
            index = jnp.broadcast_to(partner_ref[pl.ds(place, 1), :], (QUARTER, LANES))
            chosen = [jnp.take_along_axis(e, index, axis=1) for e in east]
            present = (own[0][0:1] > 0.0).astype(jnp.float32)
            alive = (chosen[0][0:1] > 0.0).astype(jnp.float32)
            weight = share_ref[pl.ds(place, 1), :] * present * alive
            weight = jnp.broadcast_to(weight, (QUARTER, LANES))
            mixed.append([o + weight * (c - o) for o, c in zip(own, chosen)])
        for j in range(4):
            rows = slice(QUARTER * j, QUARTER * (j + 1))
            keep_ref[m, rows, :] = jnp.where(core == 0, mixed[0][j], mixed[1][j])
            give_ref[m, rows, :] = jnp.where(core == 0, mixed[1][j], mixed[0][j])
        return carry

    lax.fori_loop(0, blocks, body, 0, unroll=2)


def mix(part, core, arrived, share, partner):
    blocks = arrived.shape[0] // (4 * CHUNK) // PARTS
    shape = jax.ShapeDtypeStruct((blocks, HALF, LANES), jnp.float32)

    def kernel(*refs):
        mix_kernel(part * blocks, *refs)

    return pl.pallas_call(
        kernel,
        out_shape=(shape, shape),
        in_specs=[IN_SMEM, IN_VMEM, IN_VMEM, IN_VMEM],
        out_specs=(IN_VMEM, IN_VMEM),
        compiler_params=pltpu.CompilerParams(vmem_limit_bytes=16 * 1024 * 1024),
        cost_estimate=pl.CostEstimate(flops=0, bytes_accessed=8 * 1024 * 1024, transcendentals=0),
        name="mix",
    )(core, arrived, share, partner)


def product(weights, value):
    high = value.astype(jnp.bfloat16)
    low = (value - high.astype(jnp.float32)).astype(jnp.bfloat16)
    return jnp.dot(
        weights,
        jnp.concatenate([high, low, high], axis=0),
        preferred_element_type=jnp.float32,
    )


def react_kernel(
    first, core_ref, mine_ref, other_ref, photo_ref, coupled_ref, precond_ref, production_ref, loss_ref, *rest
):
    out_ref, result_ref, sems = rest[-3:]
    blocks = mine_ref.shape[0]
    steps = result_ref.shape[0]
    each = blocks // steps
    width = each * LANES
    species = out_ref.shape[0]
    core = core_ref[0]
    copies = []
    for step in range(steps):
        columns = []
        for m in range(step * each, (step + 1) * each):
            mine, other = mine_ref[m], other_ref[m]
            columns.append(
                jnp.concatenate(
                    [jnp.where(core == 0, mine, other), jnp.where(core == 0, other, mine)], axis=0
                )
            )
        initial = jnp.concatenate(columns, axis=1)
        present = (initial[0:1] > 0.0).astype(jnp.float32)
        photo = jnp.concatenate(
            [photo_ref[first + m : first + m + 1, :] for m in range(step * each, (step + 1) * each)], axis=1
        )
        half_loss = jnp.concatenate([loss_ref[...]] * each, axis=1)
        source = jnp.concatenate([production_ref[...]] * each, axis=1) * photo
        current = initial
        for iteration in range(NEWTON):
            part_loss = half_loss * current
            moved = current - (initial + source) if iteration else -source
            misfit = moved - product(coupled_ref[...], current) + part_loss * current
            first_pass = product(precond_ref[...], misfit)
            second_pass = product(precond_ref[...], 2.0 * part_loss * first_pass)
            current = current - (first_pass - second_pass)
        result_ref[step] = (current * present)[:species]
        start = first * LANES + step * width
        copy = pltpu.make_async_copy(
            result_ref.at[step], out_ref.at[:, start : start + width], sems.at[step]
        )
        copy.start()
        copies.append(copy)
    for copy in copies:
        copy.wait()


def react(part, species, core, mine, other, photo, weights, so_far):
    blocks = mine.shape[0]
    steps = 2
    width = blocks * LANES // steps
    in_specs = [IN_SMEM] + [IN_VMEM] * 7
    operands = [core, mine, other, photo, *weights]
    aliases = {}
    if so_far is not None:
        in_specs.append(pl.BlockSpec(memory_space=pl.ANY))
        operands.append(so_far)
        aliases = {len(operands) - 1: 0}

    def kernel(*refs):
        react_kernel(part * blocks, *refs)

    return pl.pallas_call(
        kernel,
        out_shape=jax.ShapeDtypeStruct((species, blocks * PARTS * LANES), jnp.float32),
        in_specs=in_specs,
        out_specs=pl.BlockSpec(memory_space=pl.ANY),
        scratch_shapes=[
            pltpu.VMEM((steps, species, width), jnp.float32),
            pltpu.SemaphoreType.DMA((steps,)),
        ],
        input_output_aliases=aliases,
        compiler_params=pltpu.CompilerParams(vmem_limit_bytes=32 * 1024 * 1024),
        cost_estimate=pl.CostEstimate(
            flops=6 * 2 * 256 * 512 * blocks * LANES, bytes_accessed=8 * 1024 * 1024, transcendentals=0
        ),
        name="react",
    )(*operands)


def split(matrix):
    size = matrix.shape[0]
    padded = jnp.pad(matrix, ((0, ROWS - size), (0, ROWS - size)))
    high = lax.reduce_precision(padded, 8, 7)
    low = padded - high
    return jnp.concatenate([high, high, low], axis=1).astype(jnp.bfloat16)


def column(vector):
    return jnp.broadcast_to(jnp.pad(vector, (0, ROWS - vector.shape[0]))[:, None], (ROWS, LANES))


SWAP = ((0, 1), (1, 0))


def shards(
    conc, dest_tile, mixing_share, partner, photolysis, production, loss, rates, pattern, precond
):
    species, parcels = conc.shape
    devices = lax.axis_size("lat") * lax.axis_size("chip") * 2
    rows = mixing_share.shape[0] // LANES
    core = lax.axis_index("core").astype(jnp.int32)[None]

    def both_tiles(array):
        array = array.reshape(rows, LANES)
        other = lax.ppermute(array, "core", SWAP)
        return jnp.where(core[0] == 0, jnp.concatenate([array, other]), jnp.concatenate([other, array]))

    share, index = both_tiles(mixing_share), both_tiles(partner)
    photo = photolysis.reshape(rows, LANES)
    coupled = rates * jnp.kron(pattern.astype(jnp.float32), jnp.ones((SB, SB), jnp.float32))
    weights = (
        split(time_step * coupled),
        split(precond),
        column(time_step * production),
        column(time_step * loss),
    )
    packed = pack(conc, dest_tile.reshape(parcels // LANES, LANES), devices)
    packed = packed.reshape(devices, CHUNK // 4, 4, LANES)
    arrived = lax.all_to_all(
        packed, ("lat", "chip", "core"), split_axis=0, concat_axis=0, tiled=True
    ).reshape(devices * CHUNK, LANES)
    halves = [mix(part, core, arrived, share, index) for part in range(PARTS)]
    others = [lax.ppermute(give, "core", SWAP) for _, give in halves]
    result = None
    for part in range(PARTS):
        result = react(part, species, core, halves[part][0], others[part], photo, weights, result)
    return result


def solution(mesh):
    lat_count, lon_count = mesh.devices.shape
    by_core = Mesh(mesh.devices.reshape(lat_count, lon_count // 2, 2), ("lat", "chip", "core"))
    tiles = ("lat", "chip", "core")
    placed = (P(None, tiles), P(tiles, None), P(tiles), P(tiles), P(tiles), P(), P(), P(), P(), P())
    return jax.shard_map(
        shards, mesh=by_core, in_specs=placed, out_specs=P(None, tiles), check_vma=False
    )
```

time: 94.4 us -> 94.3 us (level)
  blocking collectives: 60 us -> 0 us
  waiting for transfers between devices: 0.01 us -> 48.6 us
  starting transfers between devices: 2.33 us -> 14.3 us
  local copies, waits for them, and re-layouts: 10.1 us -> 4.57 us
  Pallas kernels: 21.2 us -> 25.1 us
  other arithmetic: 0.27 us -> 1.24 us
    all_to_all x1 -> x0, blocking collectives: 60 us -> none  [shards(): lax.all_to_all(packed, ('lat', 'chip'), split_axis=0, concat_axis=0, tile...]
    all_to_all x0 -> x1, waiting for transfers between devices: none -> 47.5 us  [shards(): lax.all_to_all(packed, ('lat', 'chip', 'core'), split_axis=0, concat_axis...]
    all_to_all x0 -> x1, starting transfers between devices: none -> 11.9 us  [shards(): lax.all_to_all(packed, ('lat', 'chip', 'core'), split_axis=0, concat_axis...]
    pallas_call x3 -> x5, Pallas kernels: 21.2 us -> 25.1 us  [the longest x2 8.78 us: mix(): pl.pallas_call(kernel, out_shape=(shape, shape), in_specs=[IN_SMEM, IN_VM...]
    mul x2, local copies, waits for them, and re-layouts: 2.85 us -> 0.53 us  [shards(): jnp.kron(pattern.astype(jnp.float32), jnp.ones((SB, SB), jnp.float32))]
    slice x1 -> x0, local copies, waits for them, and re-layouts: 1.85 us -> none  [shards(): arrived[part * length:(part + 1) * length, 1:]]
    unnamed x24 -> x20, local copies, waits for them, and re-layouts: 5.2 us -> 3.88 us
    ppermute x2 -> x4, waiting for transfers between devices: 0.01 us -> 1.08 us  [the longest x2 1.07 us: both_tiles(): other = lax.ppermute(array, 'core', SWAP)]
  transfers between devices with their start and end apart: 2 -> 5, of which waited for: 0 -> 3; matrix products, arithmetic and copies ran while one was open for 3% -> 2% of each run, Pallas kernels for 7% -> 9%
where the time goes in v3:
time: 94.3 us; the launch traced here: 94 us
  waiting for transfers between devices  48.6 us (52%)
  Pallas kernels  25.1 us (27%)
  starting transfers between devices  14.3 us (15%)
  local copies, waits for them, and re-layouts  4.57 us (5%)
  other arithmetic  1.24 us (1%)
    all_to_all x1, waiting for transfers between devices, shards(): lax.all_to_all(packed, ('lat', 'chip', 'core'), split_axis=0, concat_axis...  47.5 us
    all_to_all x1, starting transfers between devices, shards(): lax.all_to_all(packed, ('lat', 'chip', 'core'), split_axis=0, concat_axis...  11.9 us
    pallas_call x2, Pallas kernels, mix(): pl.pallas_call(kernel, out_shape=(shape, shape), in_specs=[IN_SMEM, IN_VM...  8.78 us
    pallas_call x2, Pallas kernels, react(): pl.pallas_call(kernel, out_shape=jax.ShapeDtypeStruct((species, blocks *...  8.32 us
    pallas_call x1, Pallas kernels, pack(): pl.pallas_call(pack_kernel, out_shape=jax.ShapeDtypeStruct((devices * CHU...  8.03 us
    unnamed x20, local copies, waits for them, and re-layouts  3.88 us
  transfers between devices with their start and end apart: 5, of which 3 were waited for; matrix products, arithmetic and copies ran while one was open for 2% of the time, Pallas kernels for 9%

profile of v3, /device:TPU:1, one launch (start us, length us, event | category | flops | bytes accessed | tf_op | source)
XLA Modules:
  0.0 94.0 jit_solution(16998317975371204519)
XLA Ops:
  0.0 0.0 copy-start.1
  0.0 1.3 %copy-done.1 = f32[150,2048]{1,0:T(8,128)S(1)} copy-done((f32[150,2048]{1,0:T(8,128)S(1)}, f32[150,2048]{1,0:T(8,128)}, u32[]{:S(2)}) %copy-start.1) | copy-done | bytes 1228824
  1.3 0.0 copy-start.2
  1.3 0.7 copy-done.2
  2.0 8.0 %pack.1 = f32[7680,128]{1,0:T(8,128)S(1)} custom-call(f32[150,2048]{1,0:T(8,128)S(1)} %copy-done.1, s32[16,128]{1,0:T(8,128)S(1)} %bitcast.8), custom_call_target="tpu_custom_call" | custom-call | tf_op jit(solution)/shard_map/pack/pallas_call | solution.py:112
  10.0 0.0 copy-start
  10.0 1.9 %copy-done = f32[7680,128]{1,0:T(8,128)} copy-done((f32[7680,128]{1,0:T(8,128)}, f32[7680,128]{1,0:T(8,128)S(1)}, u32[]{:S(2)}) %copy-start) | copy-done | bytes 3932184
  11.9 0.0 copy-start.5
  11.9 0.0 copy-start.6
  11.9 0.0 copy-start.8
  11.9 11.9 %all-to-all-start = ((f32[128,15,4,128]{3,2,1,0:T(4,128)}), f32[128,15,4,128]{3,2,1,0:T(4,128)}, u32[]{:S(2)}, u32[]{:S(2)}) async-start(f32[128,15,4,128]{3,2,1,0:T(4,128)} %bitcast.7), calls=%async_computation | async-start | bytes 7864320 | tf_op jit(solution)/shard_map/all_to_all | solution.py:306
  23.8 0.0 copy-start.9
  23.8 0.0 copy-start.7
  23.8 0.0 copy-done.5
  23.8 1.2 %collective-permute-start = (f32[32,128]{1,0:T(8,128)S(1)}, f32[32,128]{1,0:T(8,128)S(1)}, u32[]{:S(2)}, u32[]{:S(2)}) collective-permute-start(f32[32,128]{1,0:T(8,128)S(1)} %bitcast.11), channel_id=1, source_target_pairs={{0,1},{1,0},{2,3},{3,2},{4,5},{5,4},{6,7},{7,6},{8,9},{9,8},{10,11... | collective-permute-start | bytes 49160 | tf_op jit(solution)/shard_map/ppermute | solution.py:292
  25.0 0.0 copy-done.6
  25.0 0.1 collective-permute-start.1
  25.1 0.0 copy-done.8
  25.1 0.7 collective-permute-done
  25.9 0.3 collective-permute-done.1
  26.2 47.5 %all-to-all-done = f32[128,15,4,128]{3,2,1,0:T(4,128)} async-done(((f32[128,15,4,128]{3,2,1,0:T(4,128)}), f32[128,15,4,128]{3,2,1,0:T(4,128)}, u32[]{:S(2)}, u32[]{:S(2)}) %all-to-all-start) | async-done | bytes 3932192 | tf_op jit(solution)/shard_map/all_to_all | solution.py:306
  73.7 4.4 %mix.3 = (f32[16,80,128]{2,1,0:T(8,128)S(1)}, f32[16,80,128]{2,1,0:T(8,128)S(1)}) custom-call(s32[1]{0:T(128)} %bitcast.refs_0_, f32[7680,128]{1,0:T(8,128)} %bitcast.3.refs_1_, f32[64,128]{1,0:T(8,128)S(1)} %maximum_select_fusion.refs_2_, s32[64,128]{1,0:T(8,128)S(1)} %add_select_fusion.refs_3_), custom_call_target="tpu_custom_call" | custom-call | bytes 8388608 | tf_op jit(solution)/shard_map/mix/pallas_call | solution.py:167
  78.1 1.0 %collective-permute-start.3 = (f32[16,80,128]{2,1,0:T(8,128)S(1)}, f32[16,80,128]{2,1,0:T(8,128)S(1)}, u32[]{:S(2)}, u32[]{:S(2)}) collective-permute-start(f32[16,80,128]{2,1,0:T(8,128)S(1)} %get-tuple-element.12), channel_id=1, source_target_pairs={{0,1},{1,0},{2,3},{3,2},{4,5},{5,4},{6,7},{7,6},{8,9},{9,8},{10,11... | collective-permute-start | bytes 1966088 | tf_op jit(solution)/shard_map/ppermute | solution.py:310
  79.1 0.0 copy-done.9
  79.1 0.0 copy-done.7
  79.1 0.1 mul.34
  79.3 0.4 mul.35
  79.6 0.0 copy-start.4
  79.6 1.0 %multiply_multiply_fusion = f32[150,150]{1,0:T(8,128)S(1)} fusion(f32[150,150]{1,0:T(8,128)} %param.17, f32[150,150]{1,0:T(8,128)S(1)} %mul.35), kind=kLoop, calls=%fused_computation.8 | loop fusion | flops 45000 | bytes 270000 | tf_op jit(solution)/shard_map/mul | solution.py:299
  80.6 0.0 copy-start.3
  80.6 4.4 %mix.2 = (f32[16,80,128]{2,1,0:T(8,128)S(1)}, f32[16,80,128]{2,1,0:T(8,128)S(1)}) custom-call(s32[1]{0:T(128)} %bitcast.refs_0_, f32[7680,128]{1,0:T(8,128)} %bitcast.3.refs_1_, f32[64,128]{1,0:T(8,128)S(1)} %maximum_select_fusion.refs_2_, s32[64,128]{1,0:T(8,128)S(1)} %add_select_fusion.refs_3_), custom_call_target="tpu_custom_call" | custom-call | bytes 8388608 | tf_op jit(solution)/shard_map/mix/pallas_call | solution.py:167
  85.0 0.1 collective-permute-start.2
  85.2 0.0 copy-done.4
  85.2 0.2 pad_maximum_fusion
  85.4 0.0 collective-permute-done.3.refs_2_
  85.4 0.1 broadcast_in_dim.11.refs_6_
  85.5 0.1 broadcast_in_dim.12.refs_7_
  85.6 0.0 copy-done.3
  85.6 4.2 %react.2.refs_8_ = f32[150,4096]{1,0:T(8,128)} custom-call(s32[1]{0:T(128)} %bitcast.refs_0_, f32[16,80,128]{2,1,0:T(8,128)S(1)} %get-tuple-element.11.refs_1_, f32[16,80,128]{2,1,0:T(8,128)S(1)} %collective-permute-done.3.refs_2_, f32[32,128]{1,0:T(8,128)S(1)} %bitcast.9, bf16[160,480]{1,0:T(8,128)(2,1)S(1)} %get-tuple-element.17.refs_4_, ...), custom_call_target="tpu_custom_call" | custom-call | flops 3221225472 | bytes 8388608 | tf_op jit(solution)/shard_map/react/pallas_call | solution.py:249
  89.8 0.0 collective-permute-done.2.refs_2_
  89.8 4.2 %react.3 = f32[150,4096]{1,0:T(8,128)} custom-call(s32[1]{0:T(128)} %bitcast.refs_0_, f32[16,80,128]{2,1,0:T(8,128)S(1)} %get-tuple-element.9.refs_1_, f32[16,80,128]{2,1,0:T(8,128)S(1)} %collective-permute-done.2.refs_2_, f32[32,128]{1,0:T(8,128)S(1)} %bitcast.10, bf16[160,480]{1,0:T(8,128)(2,1)S(1)} %get-tuple-element.17.refs_4_, ...), custom_call_target="tpu_custom_call", output_to_operand_aliasing={{}: (8, {})} | custom-call | flops 3221225472 | bytes 8388608 | tf_op jit(solution)/shard_map/react/pallas_call | solution.py:249
  (9 shorter events, 0.1 us)
Async XLA Ops:
  0.0 1.3 %copy-start.1 = (f32[150,2048]{1,0:T(8,128)S(1)}, f32[150,2048]{1,0:T(8,128)}, u32[]{:S(2)}) copy-start(f32[150,2048]{1,0:T(8,128)} %conc_ref.1) | copy-start | bytes 3686404
  1.3 0.7 copy-start.2
  10.0 1.9 %copy-start = (f32[7680,128]{1,0:T(8,128)}, f32[7680,128]{1,0:T(8,128)S(1)}, u32[]{:S(2)}) copy-start(f32[7680,128]{1,0:T(8,128)S(1)} %pack.1) | copy-start | bytes 11796484
  11.9 11.9 %copy-start.5 = (f32[4096]{0:T(1024)S(1)}, f32[4096]{0:T(1024)}, u32[]{:S(2)}) copy-start(f32[4096]{0:T(1024)} %param.12) | copy-start | bytes 49156
  11.9 13.2 %copy-start.6 = (s32[4096]{0:T(1024)S(1)}, s32[4096]{0:T(1024)}, u32[]{:S(2)}) copy-start(s32[4096]{0:T(1024)} %param.13) | copy-start | bytes 49156
  11.9 13.3 %copy-start.8 = (f32[150]{0:T(256)S(1)}, f32[150]{0:T(256)}, u32[]{:S(2)}) copy-start(f32[150]{0:T(256)} %param.15) | copy-start | bytes 1804
  11.9 61.8 %all-to-all-start = ((f32[128,15,4,128]{3,2,1,0:T(4,128)}), f32[128,15,4,128]{3,2,1,0:T(4,128)}, u32[]{:S(2)}, u32[]{:S(2)}) async-start(f32[128,15,4,128]{3,2,1,0:T(4,128)} %bitcast.7), calls=%async_computation | async-start | bytes 7864320 | tf_op jit(solution)/shard_map/all_to_all | solution.py:306
  23.8 55.3 %copy-start.9 = (f32[150]{0:T(256)S(1)}, f32[150]{0:T(256)}, u32[]{:S(2)}) copy-start(f32[150]{0:T(256)} %param.16) | copy-start | bytes 1804
  23.8 55.3 %copy-start.7 = (s32[10,10]{1,0:T(8,128)S(1)}, s32[10,10]{1,0:T(8,128)}, u32[]{:S(2)}) copy-start(s32[10,10]{1,0:T(8,128)} %param.18) | copy-start | bytes 1204
  23.8 2.1 %collective-permute-start = (f32[32,128]{1,0:T(8,128)S(1)}, f32[32,128]{1,0:T(8,128)S(1)}, u32[]{:S(2)}, u32[]{:S(2)}) collective-permute-start(f32[32,128]{1,0:T(8,128)S(1)} %bitcast.11), channel_id=1, source_target_pairs={{0,1},{1,0},{2,3},{3,2},{4,5},{5,4},{6,7},{7,6},{8,9},{9,8},{10,11... | collective-permute-start | bytes 49160 | tf_op jit(solution)/shard_map/ppermute | solution.py:292
  25.0 1.2 %collective-permute-start.1 = (s32[32,128]{1,0:T(8,128)S(1)}, s32[32,128]{1,0:T(8,128)S(1)}, u32[]{:S(2)}, u32[]{:S(2)}) collective-permute-start(s32[32,128]{1,0:T(8,128)S(1)} %bitcast.13), channel_id=1, source_target_pairs={{0,1},{1,0},{2,3},{3,2},{4,5},{5,4},{6,7},{7,6},{8,9},{9,8},{10,11... | collective-permute-start | bytes 49160 | tf_op jit(solution)/shard_map/ppermute | solution.py:292
  78.1 7.3 %collective-permute-start.3 = (f32[16,80,128]{2,1,0:T(8,128)S(1)}, f32[16,80,128]{2,1,0:T(8,128)S(1)}, u32[]{:S(2)}, u32[]{:S(2)}) collective-permute-start(f32[16,80,128]{2,1,0:T(8,128)S(1)} %get-tuple-element.12), channel_id=1, source_target_pairs={{0,1},{1,0},{2,3},{3,2},{4,5},{5,4},{6,7},{7,6},{8,9},{9,8},{10,11... | collective-permute-start | bytes 1966088 | tf_op jit(solution)/shard_map/ppermute | solution.py:310
  79.6 5.6 %copy-start.4 = (f32[150,150]{1,0:T(8,128)S(1)}, f32[150,150]{1,0:T(8,128)}, u32[]{:S(2)}) copy-start(f32[150,150]{1,0:T(8,128)} %param.19) | copy-start | bytes 270004
  80.6 5.0 %copy-start.3 = (f32[4096]{0:T(1024)S(1)}, f32[4096]{0:T(1024)}, u32[]{:S(2)}) copy-start(f32[4096]{0:T(1024)} %param.14) | copy-start | bytes 49156
  85.0 4.8 %collective-permute-start.2 = (f32[16,80,128]{2,1,0:T(8,128)S(1)}, f32[16,80,128]{2,1,0:T(8,128)S(1)}, u32[]{:S(2)}, u32[]{:S(2)}) collective-permute-start(f32[16,80,128]{2,1,0:T(8,128)S(1)} %get-tuple-element.10), channel_id=1, source_target_pairs={{0,1},{1,0},{2,3},{3,2},{4,5},{5,4},{6,7},{7,6},{8,9},{9,8},{10,11... | collective-permute-start | bytes 1966088 | tf_op jit(solution)/shard_map/ppermute | solution.py:310

commit v4 on v3

--- a/solution.py
+++ b/solution.py
@@ -19,6 +19,7 @@
 GROUP = 256
 TOGETHER = 4
 PARTS = 2
+PIECES = 4
 
 
 def regroup(parts):
@@ -41,8 +42,13 @@
     return (*quarters(t0, t1), *quarters(t2, t3))
 
 
-def pack_kernel(conc_ref, targets_ref, out_ref, parts_ref, place_ref, group_ref, sums_ref):
+def pack_kernel(conc_hbm, targets_hbm, out_hbm, out_ref, conc_ref, targets_ref, parts_ref, place_ref, group_ref, sums_ref, sems):
     species, parcels = conc_ref.shape
+    read_conc = pltpu.make_async_copy(conc_hbm, conc_ref, sems.at[0])
+    read_targets = pltpu.make_async_copy(targets_hbm, targets_ref, sems.at[1])
+    read_targets.start()
+    read_conc.start()
+    read_targets.wait()
     row = lax.broadcasted_iota(jnp.int32, (LANES, LANES), 0)
     column = lax.broadcasted_iota(jnp.int32, (LANES, LANES), 1)
     earlier = (row < column).astype(jnp.float32).astype(jnp.bfloat16)
@@ -62,12 +68,19 @@
         for side in range(GROUP // LANES):
             here = (place == column + side * LANES).astype(jnp.float32)
             place_ref[span, side * LANES : (side + 1) * LANES] = here.astype(jnp.bfloat16)
+    read_conc.wait()
     conc = conc_ref[...]
     low = conc - conc.astype(jnp.bfloat16).astype(jnp.float32)
     filler = jnp.zeros((ROWS - species, parcels), jnp.float32)
     parts_ref[0:ROWS, :] = jnp.concatenate([conc, filler], axis=0).astype(jnp.bfloat16)
     parts_ref[ROWS:, :] = jnp.concatenate([low, filler], axis=0).astype(jnp.bfloat16)
     around = 16
+
+    sent = TOGETHER * (GROUP // CAP) * CHUNK
+
+    def write(i):
+        rows = pl.ds(pl.multiple_of(i * sent, sent), sent)
+        return pltpu.make_async_copy(out_ref.at[rows], out_hbm.at[rows], sems.at[2 + i])
 
     def step(i, carry):
         chosen = []
@@ -98,12 +111,16 @@
                             west = chip // around * around + (chip + around - 1) % around
                             to = (west * 2 + half) * CHUNK + 2 * QUARTER
                             out_ref[pl.ds(to, QUARTER), :] = chunk
+        write(i).start()
         return carry
 
     lax.fori_loop(0, 16 // TOGETHER, step, 0)
+    for i in range(16 // TOGETHER):
+        write(i).wait()
 
 
 IN_VMEM = pl.BlockSpec(memory_space=pltpu.VMEM)
+IN_HBM = pl.BlockSpec(memory_space=pltpu.HBM)
 IN_SMEM = pl.BlockSpec(memory_space=pltpu.SMEM)
 
 
@@ -112,67 +129,113 @@
     return pl.pallas_call(
         pack_kernel,
         out_shape=jax.ShapeDtypeStruct((devices * CHUNK, LANES), jnp.float32),
-        in_specs=[IN_VMEM, IN_VMEM],
-        out_specs=IN_VMEM,
+        in_specs=[IN_HBM, IN_HBM],
+        out_specs=IN_HBM,
         scratch_shapes=[
+            pltpu.VMEM((devices * CHUNK, LANES), jnp.float32),
+            pltpu.VMEM(conc.shape, jnp.float32),
+            pltpu.VMEM(targets.shape, jnp.int32),
             pltpu.VMEM((2 * ROWS, parcels), jnp.bfloat16),
             pltpu.VMEM((parcels, GROUP), jnp.bfloat16),
             pltpu.VMEM((16, parcels), jnp.int32),
             pltpu.VMEM((TOGETHER, GROUP // LANES, ROWS, LANES), jnp.float32),
+            pltpu.SemaphoreType.DMA((2 + 16 // TOGETHER,)),
         ],
-        compiler_params=pltpu.CompilerParams(vmem_limit_bytes=40 * 1024 * 1024),
+        compiler_params=pltpu.CompilerParams(vmem_limit_bytes=63 * 1024 * 1024),
         name="pack",
     )(conc, targets)
 
 
-def mix_kernel(first, core_ref, arrived_ref, share_ref, partner_ref, keep_ref, give_ref):
+def mix_block(m, place, core, arrived_ref, share_ref, partner_ref, keep_ref, give_ref):
+    tiles = []
+    for tile in range(3):
+        parts = []
+        for s in range(4):
+            start = (m * 4 + s) * CHUNK + tile * QUARTER
+            parts.append(arrived_ref[pl.ds(start, QUARTER), :])
+        tiles.append(regroup(parts))
+    mixed = []
+    for tile in range(2):
+        own, east = tiles[tile], tiles[tile + 1]
+        index = jnp.broadcast_to(partner_ref[tile, pl.ds(place, 1), :], (QUARTER, LANES))
+        chosen = [jnp.take_along_axis(e, index, axis=1) for e in east]
+        present = (own[0][0:1] > 0.0).astype(jnp.float32)
+        alive = (chosen[0][0:1] > 0.0).astype(jnp.float32)
+        weight = share_ref[tile, pl.ds(place, 1), :] * present * alive
+        weight = jnp.broadcast_to(weight, (QUARTER, LANES))
+        mixed.append([o + weight * (c - o) for o, c in zip(own, chosen)])
+    for j in range(4):
+        rows = slice(QUARTER * j, QUARTER * (j + 1))
+        keep_ref[m, rows, :] = jnp.where(core == 0, mixed[0][j], mixed[1][j])
+        give_ref[m, rows, :] = jnp.where(core == 0, mixed[1][j], mixed[0][j])
+
+
+def mix_first_kernel(core_ref, arrived_hbm, share_ref, partner_ref, keep_ref, give_ref, rest_ref, land, sems):
+    blocks = keep_ref.shape[0]
+    each = blocks // PIECES
+    length = each * 4 * CHUNK
+    core = core_ref[0]
+    reads = []
+    for piece in range(PIECES):
+        rows = slice(piece * length, (piece + 1) * length)
+        reads.append(pltpu.make_async_copy(arrived_hbm.at[rows], land.at[rows], sems.at[piece]))
+    rest = pltpu.make_async_copy(
+        arrived_hbm.at[PIECES * length : 2 * PIECES * length], rest_ref, sems.at[PIECES]
+    )
+    for read in (*reads, rest):
+        read.start()
+    for piece in range(PIECES):
+        reads[piece].wait()
+
+        def body(m, carry):
+            mix_block(m, m, core, land, share_ref, partner_ref, keep_ref, give_ref)
+            return carry
+
+        lax.fori_loop(piece * each, (piece + 1) * each, body, 0, unroll=2)
+    rest.wait()
+
+
+def mix_second_kernel(core_ref, rest_ref, share_ref, partner_ref, keep_ref, give_ref):
     blocks = keep_ref.shape[0]
     core = core_ref[0]
 
     def body(m, carry):
-        tiles = []
-        for tile in range(3):
-            parts = []
-            for s in range(4):
-                start = ((first + m) * 4 + s) * CHUNK + tile * QUARTER
-                parts.append(arrived_ref[pl.ds(start, QUARTER), :])
-            tiles.append(regroup(parts))
-        mixed = []
-        for tile in range(2):
-            own, east = tiles[tile], tiles[tile + 1]
-            place = tile * 32 + first + m
-            index = jnp.broadcast_to(partner_ref[pl.ds(place, 1), :], (QUARTER, LANES))
-            chosen = [jnp.take_along_axis(e, index, axis=1) for e in east]
-            present = (own[0][0:1] > 0.0).astype(jnp.float32)
-            alive = (chosen[0][0:1] > 0.0).astype(jnp.float32)
-            weight = share_ref[pl.ds(place, 1), :] * present * alive
-            weight = jnp.broadcast_to(weight, (QUARTER, LANES))
-            mixed.append([o + weight * (c - o) for o, c in zip(own, chosen)])
-        for j in range(4):
-            rows = slice(QUARTER * j, QUARTER * (j + 1))
-            keep_ref[m, rows, :] = jnp.where(core == 0, mixed[0][j], mixed[1][j])
-            give_ref[m, rows, :] = jnp.where(core == 0, mixed[1][j], mixed[0][j])
+        mix_block(m, blocks + m, core, rest_ref, share_ref, partner_ref, keep_ref, give_ref)
         return carry
 
     lax.fori_loop(0, blocks, body, 0, unroll=2)
 
 
-def mix(part, core, arrived, share, partner):
-    blocks = arrived.shape[0] // (4 * CHUNK) // PARTS
+def mix(core, arrived, share, partner):
+    half = arrived.shape[0] // 2
+    blocks = half // (4 * CHUNK)
     shape = jax.ShapeDtypeStruct((blocks, HALF, LANES), jnp.float32)
-
-    def kernel(*refs):
-        mix_kernel(part * blocks, *refs)
-
-    return pl.pallas_call(
-        kernel,
+    params = pltpu.CompilerParams(vmem_limit_bytes=8 * 1024 * 1024)
+    cost = pl.CostEstimate(flops=0, bytes_accessed=8 * 1024 * 1024, transcendentals=0)
+    rest_shape = jax.ShapeDtypeStruct((half, LANES), jnp.float32)
+    keep, give, rest = pl.pallas_call(
+        mix_first_kernel,
+        out_shape=(shape, shape, rest_shape),
+        in_specs=[IN_SMEM, IN_HBM, IN_VMEM, IN_VMEM],
+        out_specs=(IN_VMEM, IN_VMEM, IN_VMEM),
+        scratch_shapes=[
+            pltpu.VMEM((half, LANES), jnp.float32),
+            pltpu.SemaphoreType.DMA((PIECES + 1,)),
+        ],
+        compiler_params=params,
+        cost_estimate=cost,
+        name="mix_first",
+    )(core, arrived, share, partner)
+    second = pl.pallas_call(
+        mix_second_kernel,
         out_shape=(shape, shape),
         in_specs=[IN_SMEM, IN_VMEM, IN_VMEM, IN_VMEM],
         out_specs=(IN_VMEM, IN_VMEM),
-        compiler_params=pltpu.CompilerParams(vmem_limit_bytes=16 * 1024 * 1024),
-        cost_estimate=pl.CostEstimate(flops=0, bytes_accessed=8 * 1024 * 1024, transcendentals=0),
-        name="mix",
-    )(core, arrived, share, partner)
+        compiler_params=params,
+        cost_estimate=cost,
+        name="mix_second",
+    )(core, rest, share, partner)
+    return (keep, give), second
 
 
 def product(weights, value):
@@ -256,7 +319,7 @@
             pltpu.SemaphoreType.DMA((steps,)),
         ],
         input_output_aliases=aliases,
-        compiler_params=pltpu.CompilerParams(vmem_limit_bytes=32 * 1024 * 1024),
+        compiler_params=pltpu.CompilerParams(vmem_limit_bytes=16 * 1024 * 1024),
         cost_estimate=pl.CostEstimate(
             flops=6 * 2 * 256 * 512 * blocks * LANES, bytes_accessed=8 * 1024 * 1024, transcendentals=0
         ),
@@ -290,7 +353,7 @@
     def both_tiles(array):
         array = array.reshape(rows, LANES)
         other = lax.ppermute(array, "core", SWAP)
-        return jnp.where(core[0] == 0, jnp.concatenate([array, other]), jnp.concatenate([other, array]))
+        return jnp.where(core[0] == 0, jnp.stack([array, other]), jnp.stack([other, array]))
 
     share, index = both_tiles(mixing_share), both_tiles(partner)
     photo = photolysis.reshape(rows, LANES)
@@ -306,7 +369,10 @@
     arrived = lax.all_to_all(
         packed, ("lat", "chip", "core"), split_axis=0, concat_axis=0, tiled=True
     ).reshape(devices * CHUNK, LANES)
-    halves = [mix(part, core, arrived, share, index) for part in range(PARTS)]
+    arrived, share, index, photo, *weights = lax.optimization_barrier(
+        (arrived, share, index, photo, *weights)
+    )
+    halves = mix(core, arrived, share, index)
     others = [lax.ppermute(give, "core", SWAP) for _, give in halves]
     result = None
     for part in range(PARTS):

time: 94.3 us -> 87.3 us (0.926)
  local copies, waits for them, and re-layouts: 4.57 us -> 0.75 us
  Pallas kernels: 25.1 us -> 23.5 us
  waiting for transfers between devices: 48.6 us -> 47.6 us
    unnamed x20 -> x16, local copies, waits for them, and re-layouts: 3.88 us -> 0.05 us
    pallas_call x2, Pallas kernels: 8.78 us -> 5.63 us  [the longest x1 3.36 us: mix(): pl.pallas_call(mix_first_kernel, out_shape=(shape, shape, rest_shape), in...]
    pallas_call x1, Pallas kernels: 8.03 us -> 9.56 us  [pack(): pl.pallas_call(pack_kernel, out_shape=jax.ShapeDtypeStruct((devices * CHU...]
  transfers between devices with their start and end apart: 5 -> 5, of which waited for: 3 -> 2; matrix products, arithmetic and copies ran while one was open for 2% -> 1% of each run, Pallas kernels for 9% -> 7%
where the time goes in v4:
time: 87.3 us; the launch traced here: 87 us
  waiting for transfers between devices  47.6 us (55%)
  Pallas kernels  23.5 us (27%)
  starting transfers between devices  14.5 us (17%)
    all_to_all x1, waiting for transfers between devices, shards(): lax.all_to_all(packed, ('lat', 'chip', 'core'), split_axis=0, concat_axis...  47.5 us
    all_to_all x1, starting transfers between devices, shards(): lax.all_to_all(packed, ('lat', 'chip', 'core'), split_axis=0, concat_axis...  11.9 us
    pallas_call x1, Pallas kernels, pack(): pl.pallas_call(pack_kernel, out_shape=jax.ShapeDtypeStruct((devices * CHU...  9.56 us
    pallas_call x2, Pallas kernels, react(): pl.pallas_call(kernel, out_shape=jax.ShapeDtypeStruct((species, blocks *...  8.32 us
    pallas_call x1, Pallas kernels, mix(): pl.pallas_call(mix_first_kernel, out_shape=(shape, shape, rest_shape), in...  3.36 us
    pallas_call x1, Pallas kernels, mix(): pl.pallas_call(mix_second_kernel, out_shape=(shape, shape), in_specs=[IN_...  2.27 us
  transfers between devices with their start and end apart: 5, of which 2 were waited for; matrix products, arithmetic and copies ran while one was open for 1% of the time, Pallas kernels for 7%

profile of v4, /device:TPU:1, one launch (start us, length us, event | category | flops | bytes accessed | tf_op | source)
XLA Modules:
  0.0 87.0 jit_solution(2971705691643130315)
XLA Ops:
  0.0 9.6 %pack.1 = f32[7680,128]{1,0:T(8,128)} custom-call(f32[150,2048]{1,0:T(8,128)} %conc_hbm.1, s32[16,128]{1,0:T(8,128)} %bitcast.20), custom_call_target="tpu_custom_call" | custom-call | tf_op jit(solution)/shard_map/pack/pallas_call | solution.py:129
  9.6 0.0 copy-start.3
  9.6 0.0 copy-start.4
  9.6 0.0 copy-start.5
  9.6 11.9 %all-to-all-start = ((f32[128,15,4,128]{3,2,1,0:T(4,128)}), f32[128,15,4,128]{3,2,1,0:T(4,128)}, u32[]{:S(2)}, u32[]{:S(2)}) async-start(f32[128,15,4,128]{3,2,1,0:T(4,128)} %bitcast.13), calls=%async_computation | async-start | bytes 7864320 | tf_op jit(solution)/shard_map/all_to_all | solution.py:369
  21.5 0.0 copy-start.1
  21.5 0.0 copy-start.2
  21.5 0.0 copy-start.6
  21.6 0.0 copy-start.7
  21.6 0.0 copy-done.3
  21.6 1.2 %collective-permute-start = (f32[32,128]{1,0:T(8,128)S(1)}, f32[32,128]{1,0:T(8,128)S(1)}, u32[]{:S(2)}, u32[]{:S(2)}) collective-permute-start(f32[32,128]{1,0:T(8,128)S(1)} %bitcast.14), channel_id=1, source_target_pairs={{0,1},{1,0},{2,3},{3,2},{4,5},{5,4},{6,7},{7,6},{8,9},{9,8},{10,11... | collective-permute-start | bytes 49160 | tf_op jit(solution)/shard_map/ppermute | solution.py:355
  22.8 0.0 copy-done.4
  22.8 0.1 collective-permute-start.1
  22.9 0.0 copy-done.5
  22.9 0.1 mul.34
  23.1 0.4 mul.35
  23.4 0.0 copy-done.1
  23.5 0.0 copy-done.2
  23.5 0.0 copy-done.6
  23.6 0.0 copy-done.7
  23.6 0.2 pad_maximum_fusion
  23.8 0.0 collective-permute-done
  23.8 0.1 collective-permute-done.1
  24.0 47.5 %all-to-all-done = f32[128,15,4,128]{3,2,1,0:T(4,128)} async-done(((f32[128,15,4,128]{3,2,1,0:T(4,128)}), f32[128,15,4,128]{3,2,1,0:T(4,128)}, u32[]{:S(2)}, u32[]{:S(2)}) %all-to-all-start) | async-done | bytes 3932192 | tf_op jit(solution)/shard_map/all_to_all | solution.py:369
  71.4 0.1 broadcast_in_dim.11.refs_6_
  71.5 0.1 broadcast_in_dim.12.refs_7_
  71.6 0.0 copy-start
  71.6 3.4 %mix_first.1 = (f32[16,80,128]{2,1,0:T(8,128)S(1)}, f32[16,80,128]{2,1,0:T(8,128)S(1)}, f32[3840,128]{1,0:T(8,128)S(1)}) custom-call(s32[1]{0:T(128)} %bitcast.core_ref.refs_0_, f32[7680,128]{1,0:T(8,128)} %bitcast.3.arrived_hbm, f32[2,32,128]{2,1,0:T(8,128)S(1)} %maximum_select_fusion.share_ref, s32[2,32,128]{2,1,0:T(8,128)S(1)} %add_select_fusion.partner_ref), custom_call_target="tpu_custom_call" | custom-call | bytes 8388608 | tf_op jit(solution)/shard_map/mix_first/pallas_call | solution.py:216
  75.0 1.0 %collective-permute-start.3 = (f32[16,80,128]{2,1,0:T(8,128)S(1)}, f32[16,80,128]{2,1,0:T(8,128)S(1)}, u32[]{:S(2)}, u32[]{:S(2)}) collective-permute-start(f32[16,80,128]{2,1,0:T(8,128)S(1)} %get-tuple-element.30), channel_id=1, source_target_pairs={{0,1},{1,0},{2,3},{3,2},{4,5},{5,4},{6,7},{7,6},{8,9},{9,8},{10,11... | collective-permute-start | bytes 1966088 | tf_op jit(solution)/shard_map/ppermute | solution.py:376
  76.0 2.3 %mix_second.1 = (f32[16,80,128]{2,1,0:T(8,128)S(1)}, f32[16,80,128]{2,1,0:T(8,128)S(1)}) custom-call(s32[1]{0:T(128)} %bitcast.core_ref.refs_0_, f32[3840,128]{1,0:T(8,128)S(1)} %get-tuple-element.21.rest_ref, f32[2,32,128]{2,1,0:T(8,128)S(1)} %maximum_select_fusion.share_ref, s32[2,32,128]{2,1,0:T(8,128)S(1)} %add_select_fusion.partner_ref), custom_call_target="tpu_custom_call" | custom-call | bytes 8388608 | tf_op jit(solution)/shard_map/mix_second/pallas_call | solution.py:229
  78.2 0.3 collective-permute-start.2
  78.5 0.0 collective-permute-done.3.refs_2_
  78.5 0.0 copy-done
  78.5 4.2 %react.2.refs_8_ = f32[150,4096]{1,0:T(8,128)} custom-call(s32[1]{0:T(128)} %bitcast.core_ref.refs_0_, f32[16,80,128]{2,1,0:T(8,128)S(1)} %get-tuple-element.29.refs_1_, f32[16,80,128]{2,1,0:T(8,128)S(1)} %collective-permute-done.3.refs_2_, f32[32,128]{1,0:T(8,128)S(1)} %bitcast.11, bf16[160,480]{1,0:T(8,128)(2,1)S(1)} %get-tuple-element.25.refs_4_, ...), custom_call_target="tpu_custom_call" | custom-call | flops 3221225472 | bytes 8388608 | tf_op jit(solution)/shard_map/react/pallas_call | solution.py:312
  82.7 0.0 collective-permute-done.2.refs_2_
  82.7 4.2 %react.3 = f32[150,4096]{1,0:T(8,128)} custom-call(s32[1]{0:T(128)} %bitcast.core_ref.refs_0_, f32[16,80,128]{2,1,0:T(8,128)S(1)} %get-tuple-element.22.refs_1_, f32[16,80,128]{2,1,0:T(8,128)S(1)} %collective-permute-done.2.refs_2_, f32[32,128]{1,0:T(8,128)S(1)} %bitcast.12, ...), custom_call_target="tpu_custom_call", output_to_operand_aliasing={{}: (8, {})} | custom-call | flops 3221225472 | bytes 8388608 | tf_op jit(solution)/shard_map/react/pallas_call | solution.py:312
  (10 shorter events, 0.1 us)
Async XLA Ops:
  9.6 12.0 %copy-start.3 = (f32[4096]{0:T(1024)S(1)}, f32[4096]{0:T(1024)}, u32[]{:S(2)}) copy-start(f32[4096]{0:T(1024)} %param.12) | copy-start | bytes 49156
  9.6 13.2 %copy-start.4 = (s32[4096]{0:T(1024)S(1)}, s32[4096]{0:T(1024)}, u32[]{:S(2)}) copy-start(s32[4096]{0:T(1024)} %param.13) | copy-start | bytes 49156
  9.6 13.3 %copy-start.5 = (s32[10,10]{1,0:T(8,128)S(1)}, s32[10,10]{1,0:T(8,128)}, u32[]{:S(2)}) copy-start(s32[10,10]{1,0:T(8,128)} %param.18) | copy-start | bytes 1204
  9.6 61.8 %all-to-all-start = ((f32[128,15,4,128]{3,2,1,0:T(4,128)}), f32[128,15,4,128]{3,2,1,0:T(4,128)}, u32[]{:S(2)}, u32[]{:S(2)}) async-start(f32[128,15,4,128]{3,2,1,0:T(4,128)} %bitcast.13), calls=%async_computation | async-start | bytes 7864320 | tf_op jit(solution)/shard_map/all_to_all | solution.py:369
  21.5 1.9 %copy-start.1 = (f32[150,150]{1,0:T(8,128)S(1)}, f32[150,150]{1,0:T(8,128)}, u32[]{:S(2)}) copy-start(f32[150,150]{1,0:T(8,128)} %param.17) | copy-start | bytes 270004
  21.5 2.0 %copy-start.2 = (f32[150,150]{1,0:T(8,128)S(1)}, f32[150,150]{1,0:T(8,128)}, u32[]{:S(2)}) copy-start(f32[150,150]{1,0:T(8,128)} %param.19) | copy-start | bytes 270004
  21.5 2.0 %copy-start.6 = (f32[150]{0:T(256)S(1)}, f32[150]{0:T(256)}, u32[]{:S(2)}) copy-start(f32[150]{0:T(256)} %param.15) | copy-start | bytes 1804
  21.6 2.0 %copy-start.7 = (f32[150]{0:T(256)S(1)}, f32[150]{0:T(256)}, u32[]{:S(2)}) copy-start(f32[150]{0:T(256)} %param.16) | copy-start | bytes 1804
  21.6 2.3 %collective-permute-start = (f32[32,128]{1,0:T(8,128)S(1)}, f32[32,128]{1,0:T(8,128)S(1)}, u32[]{:S(2)}, u32[]{:S(2)}) collective-permute-start(f32[32,128]{1,0:T(8,128)S(1)} %bitcast.14), channel_id=1, source_target_pairs={{0,1},{1,0},{2,3},{3,2},{4,5},{5,4},{6,7},{7,6},{8,9},{9,8},{10,11... | collective-permute-start | bytes 49160 | tf_op jit(solution)/shard_map/ppermute | solution.py:355
  22.8 1.2 %collective-permute-start.1 = (s32[32,128]{1,0:T(8,128)S(1)}, s32[32,128]{1,0:T(8,128)S(1)}, u32[]{:S(2)}, u32[]{:S(2)}) collective-permute-start(s32[32,128]{1,0:T(8,128)S(1)} %bitcast.16), channel_id=1, source_target_pairs={{0,1},{1,0},{2,3},{3,2},{4,5},{5,4},{6,7},{7,6},{8,9},{9,8},{10,11... | collective-permute-start | bytes 49160 | tf_op jit(solution)/shard_map/ppermute | solution.py:355
  71.6 6.9 %copy-start = (f32[4096]{0:T(1024)S(1)}, f32[4096]{0:T(1024)}, u32[]{:S(2)}) copy-start(f32[4096]{0:T(1024)} %param.14) | copy-start | bytes 49156
  75.0 3.5 %collective-permute-start.3 = (f32[16,80,128]{2,1,0:T(8,128)S(1)}, f32[16,80,128]{2,1,0:T(8,128)S(1)}, u32[]{:S(2)}, u32[]{:S(2)}) collective-permute-start(f32[16,80,128]{2,1,0:T(8,128)S(1)} %get-tuple-element.30), channel_id=1, source_target_pairs={{0,1},{1,0},{2,3},{3,2},{4,5},{5,4},{6,7},{7,6},{8,9},{9,8},{10,11... | collective-permute-start | bytes 1966088 | tf_op jit(solution)/shard_map/ppermute | solution.py:376
  78.2 4.5 %collective-permute-start.2 = (f32[16,80,128]{2,1,0:T(8,128)S(1)}, f32[16,80,128]{2,1,0:T(8,128)S(1)}, u32[]{:S(2)}, u32[]{:S(2)}) collective-permute-start(f32[16,80,128]{2,1,0:T(8,128)S(1)} %get-tuple-element.23), channel_id=1, source_target_pairs={{0,1},{1,0},{2,3},{3,2},{4,5},{5,4},{6,7},{7,6},{8,9},{9,8},{10,11... | collective-permute-start | bytes 1966088 | tf_op jit(solution)/shard_map/ppermute | solution.py:376

commit v5 on v4

--- a/solution.py
+++ b/solution.py
@@ -12,9 +12,11 @@
 
 LANES = 128
 CAP = 32
-QUARTER = 20
+QUARTER = 19
 HALF = 4 * QUARTER
-ROWS = 2 * HALF
+SENT = 2 * HALF
+BLOCK = 80
+ROWS = 2 * BLOCK
 CHUNK = 3 * QUARTER
 GROUP = 256
 TOGETHER = 4
@@ -71,9 +73,8 @@
     read_conc.wait()
     conc = conc_ref[...]
     low = conc - conc.astype(jnp.bfloat16).astype(jnp.float32)
-    filler = jnp.zeros((ROWS - species, parcels), jnp.float32)
-    parts_ref[0:ROWS, :] = jnp.concatenate([conc, filler], axis=0).astype(jnp.bfloat16)
-    parts_ref[ROWS:, :] = jnp.concatenate([low, filler], axis=0).astype(jnp.bfloat16)
+    filler = jnp.zeros((SENT - species, parcels), jnp.float32)
+    parts_ref[...] = jnp.concatenate([conc, filler, low, filler], axis=0).astype(jnp.bfloat16)
     around = 16
 
     sent = TOGETHER * (GROUP // CAP) * CHUNK
@@ -86,13 +87,13 @@
         chosen = []
         for t in range(TOGETHER):
             mine = (group_ref[...] == i * TOGETHER + t).astype(jnp.float32).astype(jnp.bfloat16)
-            chosen.append(parts_ref[...] * jnp.concatenate([mine] * (2 * ROWS // 16), axis=0))
+            chosen.append(parts_ref[...] * jnp.concatenate([mine] * (2 * SENT // 16), axis=0))
         moved = jnp.dot(
             jnp.concatenate(chosen, axis=0), place_ref[...], preferred_element_type=jnp.float32
         )
         for t in range(TOGETHER):
-            base = 2 * t * ROWS
-            sums = moved[base : base + ROWS] + moved[base + ROWS : base + 2 * ROWS]
+            base = 2 * t * SENT
+            sums = moved[base : base + SENT] + moved[base + SENT : base + 2 * SENT]
             for side in range(GROUP // LANES):
                 sums_ref[t, side] = sums[:, side * LANES : (side + 1) * LANES]
         for t in range(TOGETHER):
@@ -135,10 +136,10 @@
             pltpu.VMEM((devices * CHUNK, LANES), jnp.float32),
             pltpu.VMEM(conc.shape, jnp.float32),
             pltpu.VMEM(targets.shape, jnp.int32),
-            pltpu.VMEM((2 * ROWS, parcels), jnp.bfloat16),
+            pltpu.VMEM((2 * SENT, parcels), jnp.bfloat16),
             pltpu.VMEM((parcels, GROUP), jnp.bfloat16),
             pltpu.VMEM((16, parcels), jnp.int32),
-            pltpu.VMEM((TOGETHER, GROUP // LANES, ROWS, LANES), jnp.float32),
+            pltpu.VMEM((TOGETHER, GROUP // LANES, SENT, LANES), jnp.float32),
             pltpu.SemaphoreType.DMA((2 + 16 // TOGETHER,)),
         ],
         compiler_params=pltpu.CompilerParams(vmem_limit_bytes=63 * 1024 * 1024),
@@ -168,6 +169,9 @@
         rows = slice(QUARTER * j, QUARTER * (j + 1))
         keep_ref[m, rows, :] = jnp.where(core == 0, mixed[0][j], mixed[1][j])
         give_ref[m, rows, :] = jnp.where(core == 0, mixed[1][j], mixed[0][j])
+    empty = jnp.zeros((BLOCK - HALF, LANES), jnp.float32)
+    keep_ref[m, HALF:, :] = empty
+    give_ref[m, HALF:, :] = empty
 
 
 def mix_first_kernel(core_ref, arrived_hbm, share_ref, partner_ref, keep_ref, give_ref, rest_ref, land, sems):
@@ -209,7 +213,7 @@
 def mix(core, arrived, share, partner):
     half = arrived.shape[0] // 2
     blocks = half // (4 * CHUNK)
-    shape = jax.ShapeDtypeStruct((blocks, HALF, LANES), jnp.float32)
+    shape = jax.ShapeDtypeStruct((blocks, BLOCK, LANES), jnp.float32)
     params = pltpu.CompilerParams(vmem_limit_bytes=8 * 1024 * 1024)
     cost = pl.CostEstimate(flops=0, bytes_accessed=8 * 1024 * 1024, transcendentals=0)
     rest_shape = jax.ShapeDtypeStruct((half, LANES), jnp.float32)
@@ -283,7 +287,9 @@
             first_pass = product(precond_ref[...], misfit)
             second_pass = product(precond_ref[...], 2.0 * part_loss * first_pass)
             current = current - (first_pass - second_pass)
-        result_ref[step] = (current * present)[:species]
+        result = current * present
+        result_ref[step, :HALF] = result[:HALF]
+        result_ref[step, HALF:] = result[BLOCK : BLOCK + species - HALF]
         start = first * LANES + step * width
         copy = pltpu.make_async_copy(
             result_ref.at[step], out_ref.at[:, start : start + width], sems.at[step]
@@ -327,16 +333,24 @@
     )(*operands)
 
 
+def spread(array, axis):
+    gaps = [(0, 0)] * array.ndim
+    first, second = jnp.split(array, [HALF], axis=axis)
+    gaps[axis] = (0, BLOCK - first.shape[axis])
+    first = jnp.pad(first, gaps)
+    gaps[axis] = (0, BLOCK - second.shape[axis])
+    return jnp.concatenate([first, jnp.pad(second, gaps)], axis=axis)
+
+
 def split(matrix):
-    size = matrix.shape[0]
-    padded = jnp.pad(matrix, ((0, ROWS - size), (0, ROWS - size)))
+    padded = spread(spread(matrix, 0), 1)
     high = lax.reduce_precision(padded, 8, 7)
     low = padded - high
     return jnp.concatenate([high, high, low], axis=1).astype(jnp.bfloat16)
 
 
 def column(vector):
-    return jnp.broadcast_to(jnp.pad(vector, (0, ROWS - vector.shape[0]))[:, None], (ROWS, LANES))
+    return jnp.broadcast_to(spread(vector, 0)[:, None], (ROWS, LANES))
 
 
 SWAP = ((0, 1), (1, 0))
@@ -365,7 +379,7 @@
         column(time_step * loss),
     )
     packed = pack(conc, dest_tile.reshape(parcels // LANES, LANES), devices)
-    packed = packed.reshape(devices, CHUNK // 4, 4, LANES)
+    packed = packed.reshape(devices, CHUNK, 1, LANES)
     arrived = lax.all_to_all(
         packed, ("lat", "chip", "core"), split_axis=0, concat_axis=0, tiled=True
     ).reshape(devices * CHUNK, LANES)

time: 87.3 us -> 85 us (0.974)
  waiting for transfers between devices: 47.6 us -> 44.7 us
    all_to_all x1, waiting for transfers between devices: 47.5 us -> 44.7 us  [shards(): lax.all_to_all(packed, ('lat', 'chip', 'core'), split_axis=0, concat_axis...]
  transfers between devices with their start and end apart: 5 -> 5, of which waited for: 2 -> 1; matrix products, arithmetic and copies ran while one was open for 1% -> 2% of each run, Pallas kernels for 7% -> 8%
where the time goes in v5:
time: 85 us; the launch traced here: 84.8 us
  waiting for transfers between devices  44.7 us (53%)
  Pallas kernels  23.4 us (28%)
  starting transfers between devices  14.4 us (17%)
  local copies, waits for them, and re-layouts  1.07 us (1%)
    all_to_all x1, waiting for transfers between devices, shards(): lax.all_to_all(packed, ('lat', 'chip', 'core'), split_axis=0, concat_axis...  44.7 us
    all_to_all x1, starting transfers between devices, shards(): lax.all_to_all(packed, ('lat', 'chip', 'core'), split_axis=0, concat_axis...  11.9 us
    pallas_call x1, Pallas kernels, pack(): pl.pallas_call(pack_kernel, out_shape=jax.ShapeDtypeStruct((devices * CHU...  9.39 us
    pallas_call x2, Pallas kernels, react(): pl.pallas_call(kernel, out_shape=jax.ShapeDtypeStruct((species, blocks *...  8.39 us
    pallas_call x1, Pallas kernels, mix(): pl.pallas_call(mix_first_kernel, out_shape=(shape, shape, rest_shape), in...  3.35 us
    pallas_call x1, Pallas kernels, mix(): pl.pallas_call(mix_second_kernel, out_shape=(shape, shape), in_specs=[IN_...  2.27 us
  transfers between devices with their start and end apart: 5, of which 1 were waited for; matrix products, arithmetic and copies ran while one was open for 2% of the time, Pallas kernels for 8%

profile of v5, /device:TPU:1, one launch (start us, length us, event | category | flops | bytes accessed | tf_op | source)
XLA Modules:
  0.0 84.8 jit_solution(14559974183896331936)
XLA Ops:
  0.0 9.4 %pack.1 = f32[7296,128]{1,0:T(8,128)} custom-call(f32[150,2048]{1,0:T(8,128)} %conc_hbm.1, s32[16,128]{1,0:T(8,128)} %bitcast.20), custom_call_target="tpu_custom_call" | custom-call | tf_op jit(solution)/shard_map/pack/pallas_call | solution.py:130
  9.4 0.0 copy-start.3
  9.4 0.0 copy-start.4
  9.4 0.0 copy-start.1
  9.4 0.0 copy-start.5
  9.4 11.9 %all-to-all-start = ((f32[128,57,1,128]{3,2,1,0:T(1,128)}), f32[128,57,1,128]{3,2,1,0:T(1,128)}, u32[]{:S(2)}, u32[]{:S(2)}) async-start(f32[128,57,1,128]{3,2,1,0:T(1,128)} %bitcast.13), calls=%async_computation | async-start | bytes 7471104 | tf_op jit(solution)/shard_map/all_to_all | solution.py:383
  21.4 0.0 copy-start.2
  21.4 0.0 copy-start.6
  21.4 0.0 copy-start.7
  21.4 0.0 copy-start.8
  21.4 0.0 copy-done.3
  21.4 1.2 %collective-permute-start = (f32[32,128]{1,0:T(8,128)S(1)}, f32[32,128]{1,0:T(8,128)S(1)}, u32[]{:S(2)}, u32[]{:S(2)}) collective-permute-start(f32[32,128]{1,0:T(8,128)S(1)} %bitcast.14), channel_id=1, source_target_pairs={{0,1},{1,0},{2,3},{3,2},{4,5},{5,4},{6,7},{7,6},{8,9},{9,8},{10,11... | collective-permute-start | bytes 49160 | tf_op jit(solution)/shard_map/ppermute | solution.py:369
  22.6 0.0 copy-done.4
  22.6 0.1 collective-permute-start.1
  22.7 0.0 copy-done.1
  22.8 0.0 copy-done.5
  22.8 0.1 mul.34
  22.9 0.4 mul.35
  23.3 0.0 copy-done.2
  23.4 0.0 copy-done.6
  23.4 0.1 slice_select_fusion.3
  23.5 0.1 split.31
  23.6 0.1 split.32
  23.7 0.0 copy-done.7
  23.7 0.1 split.29
  23.8 0.0 copy-done.8
  23.8 0.1 split.28
  23.9 0.1 reduce-precision_convert_fusion.1
  24.0 0.1 pad_maximum_fusion.refs_4_
  24.1 0.1 reduce-precision_convert_fusion
  24.2 0.1 pad_maximum_fusion.1.refs_5_
  24.4 0.1 select_maximum_fusion.4
  24.5 0.0 collective-permute-done
  24.5 0.0 collective-permute-done.1
  24.5 44.7 %all-to-all-done = f32[128,57,1,128]{3,2,1,0:T(1,128)} async-done(((f32[128,57,1,128]{3,2,1,0:T(1,128)}), f32[128,57,1,128]{3,2,1,0:T(1,128)}, u32[]{:S(2)}, u32[]{:S(2)}) %all-to-all-start) | async-done | bytes 3735584 | tf_op jit(solution)/shard_map/all_to_all | solution.py:383
  69.2 0.1 broadcast_in_dim.11.refs_6_
  69.3 0.1 broadcast_in_dim.12.refs_7_
  69.4 0.0 copy-start
  69.4 3.3 %mix_first.1 = (f32[16,80,128]{2,1,0:T(8,128)S(1)}, f32[16,80,128]{2,1,0:T(8,128)S(1)}, f32[3648,128]{1,0:T(8,128)S(1)}) custom-call(s32[1]{0:T(128)} %bitcast.core_ref.refs_0_, f32[7296,128]{1,0:T(8,128)} %bitcast.3.arrived_hbm, f32[2,32,128]{2,1,0:T(8,128)S(1)} %maximum_select_fusion.share_ref, s32[2,32,128]{2,1,0:T(8,128)S(1)} %add_select_fusion.partner_ref), custom_call_target="tpu_custom_call" | custom-call | bytes 8388608 | tf_op jit(solution)/shard_map/mix_first/pallas_call | solution.py:220
  72.7 1.0 %collective-permute-start.3 = (f32[16,80,128]{2,1,0:T(8,128)S(1)}, f32[16,80,128]{2,1,0:T(8,128)S(1)}, u32[]{:S(2)}, u32[]{:S(2)}) collective-permute-start(f32[16,80,128]{2,1,0:T(8,128)S(1)} %get-tuple-element.30), channel_id=1, source_target_pairs={{0,1},{1,0},{2,3},{3,2},{4,5},{5,4},{6,7},{7,6},{8,9},{9,8},{10,11... | collective-permute-start | bytes 1966088 | tf_op jit(solution)/shard_map/ppermute | solution.py:390
  73.7 2.3 %mix_second.1 = (f32[16,80,128]{2,1,0:T(8,128)S(1)}, f32[16,80,128]{2,1,0:T(8,128)S(1)}) custom-call(s32[1]{0:T(128)} %bitcast.core_ref.refs_0_, f32[3648,128]{1,0:T(8,128)S(1)} %get-tuple-element.21.rest_ref, f32[2,32,128]{2,1,0:T(8,128)S(1)} %maximum_select_fusion.share_ref, s32[2,32,128]{2,1,0:T(8,128)S(1)} %add_select_fusion.partner_ref), custom_call_target="tpu_custom_call" | custom-call | bytes 8388608 | tf_op jit(solution)/shard_map/mix_second/pallas_call | solution.py:233
  76.0 0.3 collective-permute-start.2
  76.2 0.0 collective-permute-done.3.refs_2_
  76.3 0.0 copy-done
  76.3 4.2 %react.2.refs_8_ = f32[150,4096]{1,0:T(8,128)} custom-call(s32[1]{0:T(128)} %bitcast.core_ref.refs_0_, f32[16,80,128]{2,1,0:T(8,128)S(1)} %get-tuple-element.29.refs_1_, f32[16,80,128]{2,1,0:T(8,128)S(1)} %collective-permute-done.3.refs_2_, f32[32,128]{1,0:T(8,128)S(1)} %bitcast.11, bf16[160,480]{1,0:T(8,128)(2,1)S(1)} %pad_maximum_fusion.refs_4_, ...), custom_call_target="tpu_custom_call" | custom-call | flops 3221225472 | bytes 8388608 | tf_op jit(solution)/shard_map/react/pallas_call | solution.py:318
  80.5 0.0 collective-permute-done.2.refs_2_
  80.5 4.2 %react.3 = f32[150,4096]{1,0:T(8,128)} custom-call(s32[1]{0:T(128)} %bitcast.core_ref.refs_0_, f32[16,80,128]{2,1,0:T(8,128)S(1)} %get-tuple-element.22.refs_1_, f32[16,80,128]{2,1,0:T(8,128)S(1)} %collective-permute-done.2.refs_2_, f32[32,128]{1,0:T(8,128)S(1)} %bitcast.12, ...), custom_call_target="tpu_custom_call", output_to_operand_aliasing={{}: (8, {})} | custom-call | flops 3221225472 | bytes 8388608 | tf_op jit(solution)/shard_map/react/pallas_call | solution.py:318
  (11 shorter events, 0.1 us)
Async XLA Ops:
  9.4 12.0 %copy-start.3 = (f32[4096]{0:T(1024)S(1)}, f32[4096]{0:T(1024)}, u32[]{:S(2)}) copy-start(f32[4096]{0:T(1024)} %param.12) | copy-start | bytes 49156
  9.4 13.2 %copy-start.4 = (s32[4096]{0:T(1024)S(1)}, s32[4096]{0:T(1024)}, u32[]{:S(2)}) copy-start(s32[4096]{0:T(1024)} %param.13) | copy-start | bytes 49156
  9.4 13.3 %copy-start.1 = (f32[150,150]{1,0:T(8,128)S(1)}, f32[150,150]{1,0:T(8,128)}, u32[]{:S(2)}) copy-start(f32[150,150]{1,0:T(8,128)} %param.19) | copy-start | bytes 270004
  9.4 13.3 %copy-start.5 = (s32[10,10]{1,0:T(8,128)S(1)}, s32[10,10]{1,0:T(8,128)}, u32[]{:S(2)}) copy-start(s32[10,10]{1,0:T(8,128)} %param.18) | copy-start | bytes 1204
  9.4 59.7 %all-to-all-start = ((f32[128,57,1,128]{3,2,1,0:T(1,128)}), f32[128,57,1,128]{3,2,1,0:T(1,128)}, u32[]{:S(2)}, u32[]{:S(2)}) async-start(f32[128,57,1,128]{3,2,1,0:T(1,128)} %bitcast.13), calls=%async_computation | async-start | bytes 7471104 | tf_op jit(solution)/shard_map/all_to_all | solution.py:383
  21.4 2.0 %copy-start.2 = (f32[150,150]{1,0:T(8,128)S(1)}, f32[150,150]{1,0:T(8,128)}, u32[]{:S(2)}) copy-start(f32[150,150]{1,0:T(8,128)} %param.17) | copy-start | bytes 270004
  21.4 2.0 %copy-start.6 = (pred[80]{0:T(512)(128)(4,1)S(1)}, pred[80]{0:T(512)(128)(4,1)}, u32[]{:S(2)}) copy-start(pred[80]{0:T(512)(128)(4,1)} %constant.16.clone.1) | copy-start | bytes 244
  21.4 2.3 %copy-start.7 = (f32[150]{0:T(256)S(1)}, f32[150]{0:T(256)}, u32[]{:S(2)}) copy-start(f32[150]{0:T(256)} %param.16) | copy-start | bytes 1804
  21.4 2.4 %copy-start.8 = (f32[150]{0:T(256)S(1)}, f32[150]{0:T(256)}, u32[]{:S(2)}) copy-start(f32[150]{0:T(256)} %param.15) | copy-start | bytes 1804
  21.4 3.0 %collective-permute-start = (f32[32,128]{1,0:T(8,128)S(1)}, f32[32,128]{1,0:T(8,128)S(1)}, u32[]{:S(2)}, u32[]{:S(2)}) collective-permute-start(f32[32,128]{1,0:T(8,128)S(1)} %bitcast.14), channel_id=1, source_target_pairs={{0,1},{1,0},{2,3},{3,2},{4,5},{5,4},{6,7},{7,6},{8,9},{9,8},{10,11... | collective-permute-start | bytes 49160 | tf_op jit(solution)/shard_map/ppermute | solution.py:369
  22.6 1.8 %collective-permute-start.1 = (s32[32,128]{1,0:T(8,128)S(1)}, s32[32,128]{1,0:T(8,128)S(1)}, u32[]{:S(2)}, u32[]{:S(2)}) collective-permute-start(s32[32,128]{1,0:T(8,128)S(1)} %bitcast.16), channel_id=1, source_target_pairs={{0,1},{1,0},{2,3},{3,2},{4,5},{5,4},{6,7},{7,6},{8,9},{9,8},{10,11... | collective-permute-start | bytes 49160 | tf_op jit(solution)/shard_map/ppermute | solution.py:369
  69.4 6.9 %copy-start = (f32[4096]{0:T(1024)S(1)}, f32[4096]{0:T(1024)}, u32[]{:S(2)}) copy-start(f32[4096]{0:T(1024)} %param.14) | copy-start | bytes 49156
  72.7 3.5 %collective-permute-start.3 = (f32[16,80,128]{2,1,0:T(8,128)S(1)}, f32[16,80,128]{2,1,0:T(8,128)S(1)}, u32[]{:S(2)}, u32[]{:S(2)}) collective-permute-start(f32[16,80,128]{2,1,0:T(8,128)S(1)} %get-tuple-element.30), channel_id=1, source_target_pairs={{0,1},{1,0},{2,3},{3,2},{4,5},{5,4},{6,7},{7,6},{8,9},{9,8},{10,11... | collective-permute-start | bytes 1966088 | tf_op jit(solution)/shard_map/ppermute | solution.py:390
  76.0 4.5 %collective-permute-start.2 = (f32[16,80,128]{2,1,0:T(8,128)S(1)}, f32[16,80,128]{2,1,0:T(8,128)S(1)}, u32[]{:S(2)}, u32[]{:S(2)}) collective-permute-start(f32[16,80,128]{2,1,0:T(8,128)S(1)} %get-tuple-element.23), channel_id=1, source_target_pairs={{0,1},{1,0},{2,3},{3,2},{4,5},{5,4},{6,7},{7,6},{8,9},{9,8},{10,11... | collective-permute-start | bytes 1966088 | tf_op jit(solution)/shard_map/ppermute | solution.py:390

commit v6 on v5

--- a/solution.py
+++ b/solution.py
@@ -19,9 +19,9 @@
 ROWS = 2 * BLOCK
 CHUNK = 3 * QUARTER
 GROUP = 256
-TOGETHER = 4
+TOGETHER = 2
 PARTS = 2
-PIECES = 4
+PIECES = 8
 
 
 def regroup(parts):
@@ -77,46 +77,51 @@
     parts_ref[...] = jnp.concatenate([conc, filler, low, filler], axis=0).astype(jnp.bfloat16)
     around = 16
 
-    sent = TOGETHER * (GROUP // CAP) * CHUNK
+    sent = around * 2 * CHUNK
+    per_lat = around * 2 * CAP // GROUP
 
     def write(i):
-        rows = pl.ds(pl.multiple_of(i * sent, sent), sent)
+        rows = slice(i * sent, (i + 1) * sent)
         return pltpu.make_async_copy(out_ref.at[rows], out_hbm.at[rows], sems.at[2 + i])
 
-    def step(i, carry):
+    def move(i):
         chosen = []
         for t in range(TOGETHER):
             mine = (group_ref[...] == i * TOGETHER + t).astype(jnp.float32).astype(jnp.bfloat16)
             chosen.append(parts_ref[...] * jnp.concatenate([mine] * (2 * SENT // 16), axis=0))
-        moved = jnp.dot(
+        return jnp.dot(
             jnp.concatenate(chosen, axis=0), place_ref[...], preferred_element_type=jnp.float32
         )
+
+    def arrange(i, moved):
         for t in range(TOGETHER):
             base = 2 * t * SENT
             sums = moved[base : base + SENT] + moved[base + SENT : base + 2 * SENT]
             for side in range(GROUP // LANES):
-                sums_ref[t, side] = sums[:, side * LANES : (side + 1) * LANES]
+                sums_ref[i % 2, t, side] = sums[:, side * LANES : (side + 1) * LANES]
         for t in range(TOGETHER):
             for side in range(GROUP // LANES):
                 quad = (i * TOGETHER + t) * (GROUP // LANES) + side
                 for half in range(2):
                     quarters = [
-                        sums_ref[t, side, half * HALF + QUARTER * j : half * HALF + QUARTER * (j + 1), :]
+                        sums_ref[i % 2, t, side, half * HALF + QUARTER * j : half * HALF + QUARTER * (j + 1), :]
                         for j in range(4)
                     ]
                     for d, chunk in enumerate(regroup(quarters)):
                         chip = quad * 2 + d // 2
                         to = (chip * 2 + half) * CHUNK + (d % 2) * QUARTER
-                        out_ref[pl.ds(to, QUARTER), :] = chunk
+                        out_ref[to : to + QUARTER, :] = chunk
                         if d % 2 == 0:
                             west = chip // around * around + (chip + around - 1) % around
                             to = (west * 2 + half) * CHUNK + 2 * QUARTER
-                            out_ref[pl.ds(to, QUARTER), :] = chunk
-        write(i).start()
-        return carry
-
-    lax.fori_loop(0, 16 // TOGETHER, step, 0)
-    for i in range(16 // TOGETHER):
+                            out_ref[to : to + QUARTER, :] = chunk
+            if (i * TOGETHER + t + 1) % per_lat == 0:
+                write((i * TOGETHER + t) // per_lat).start()
+
+    steps = parcels * 2 // GROUP // TOGETHER
+    for i in range(steps):
+        arrange(i, move(i))
+    for i in range(out_ref.shape[0] // sent):
         write(i).wait()
 
 
@@ -139,8 +144,8 @@
             pltpu.VMEM((2 * SENT, parcels), jnp.bfloat16),
             pltpu.VMEM((parcels, GROUP), jnp.bfloat16),
             pltpu.VMEM((16, parcels), jnp.int32),
-            pltpu.VMEM((TOGETHER, GROUP // LANES, SENT, LANES), jnp.float32),
-            pltpu.SemaphoreType.DMA((2 + 16 // TOGETHER,)),
+            pltpu.VMEM((2, TOGETHER, GROUP // LANES, SENT, LANES), jnp.float32),
+            pltpu.SemaphoreType.DMA((2 + 4,)),
         ],
         compiler_params=pltpu.CompilerParams(vmem_limit_bytes=63 * 1024 * 1024),
         name="pack",

time: 85 us -> 83.6 us (0.984)
  Pallas kernels: 23.4 us -> 22 us
    pallas_call x1, Pallas kernels: 9.39 us -> 8.04 us  [pack(): pl.pallas_call(pack_kernel, out_shape=jax.ShapeDtypeStruct((devices * CHU...]
where the time goes in v6:
time: 83.6 us; the launch traced here: 83.4 us
  waiting for transfers between devices  44.7 us (53%)
  Pallas kernels  22 us (26%)
  starting transfers between devices  14.4 us (17%)
  local copies, waits for them, and re-layouts  1.07 us (1%)
    all_to_all x1, waiting for transfers between devices, shards(): lax.all_to_all(packed, ('lat', 'chip', 'core'), split_axis=0, concat_axis...  44.7 us
    all_to_all x1, starting transfers between devices, shards(): lax.all_to_all(packed, ('lat', 'chip', 'core'), split_axis=0, concat_axis...  11.9 us
    pallas_call x2, Pallas kernels, react(): pl.pallas_call(kernel, out_shape=jax.ShapeDtypeStruct((species, blocks *...  8.38 us
    pallas_call x1, Pallas kernels, pack(): pl.pallas_call(pack_kernel, out_shape=jax.ShapeDtypeStruct((devices * CHU...  8.04 us
    pallas_call x1, Pallas kernels, mix(): pl.pallas_call(mix_first_kernel, out_shape=(shape, shape, rest_shape), in...  3.3 us
    pallas_call x1, Pallas kernels, mix(): pl.pallas_call(mix_second_kernel, out_shape=(shape, shape), in_specs=[IN_...  2.27 us
  transfers between devices with their start and end apart: 5, of which 1 were waited for; matrix products, arithmetic and copies ran while one was open for 2% of the time, Pallas kernels for 8%

profile of v6, /device:TPU:1, one launch (start us, length us, event | category | flops | bytes accessed | tf_op | source)
XLA Modules:
  0.0 83.4 jit_solution(14977862835632120329)
XLA Ops:
  0.0 8.0 %pack.1 = f32[7296,128]{1,0:T(8,128)} custom-call(f32[150,2048]{1,0:T(8,128)} %conc_hbm.1, s32[16,128]{1,0:T(8,128)} %bitcast.20), custom_call_target="tpu_custom_call" | custom-call | tf_op jit(solution)/shard_map/pack/pallas_call | solution.py:135
  8.0 0.0 copy-start.3
  8.1 0.0 copy-start.4
  8.1 0.0 copy-start.1
  8.1 0.0 copy-start.5
  8.1 11.9 %all-to-all-start = ((f32[128,57,1,128]{3,2,1,0:T(1,128)}), f32[128,57,1,128]{3,2,1,0:T(1,128)}, u32[]{:S(2)}, u32[]{:S(2)}) async-start(f32[128,57,1,128]{3,2,1,0:T(1,128)} %bitcast.13), calls=%async_computation | async-start | bytes 7471104 | tf_op jit(solution)/shard_map/all_to_all | solution.py:388
  20.0 0.0 copy-start.2
  20.0 0.0 copy-start.6
  20.0 0.0 copy-start.7
  20.0 0.0 copy-start.8
  20.1 0.0 copy-done.3
  20.1 1.2 %collective-permute-start = (f32[32,128]{1,0:T(8,128)S(1)}, f32[32,128]{1,0:T(8,128)S(1)}, u32[]{:S(2)}, u32[]{:S(2)}) collective-permute-start(f32[32,128]{1,0:T(8,128)S(1)} %bitcast.14), channel_id=1, source_target_pairs={{0,1},{1,0},{2,3},{3,2},{4,5},{5,4},{6,7},{7,6},{8,9},{9,8},{10,11... | collective-permute-start | bytes 49160 | tf_op jit(solution)/shard_map/ppermute | solution.py:374
  21.3 0.0 copy-done.4
  21.3 0.1 collective-permute-start.1
  21.4 0.0 copy-done.1
  21.4 0.0 copy-done.5
  21.4 0.1 mul.34
  21.6 0.4 mul.35
  22.0 0.0 copy-done.2
  22.0 0.0 copy-done.6
  22.0 0.1 slice_select_fusion.3
  22.1 0.1 split.31
  22.2 0.1 split.32
  22.3 0.0 copy-done.7
  22.3 0.1 split.29
  22.4 0.0 copy-done.8
  22.4 0.1 split.28
  22.5 0.1 reduce-precision_convert_fusion.1
  22.6 0.1 pad_maximum_fusion.refs_4_
  22.8 0.1 reduce-precision_convert_fusion
  22.9 0.1 pad_maximum_fusion.1.refs_5_
  23.0 0.1 select_maximum_fusion.4
  23.1 0.0 collective-permute-done
  23.1 0.0 collective-permute-done.1
  23.1 44.7 %all-to-all-done = f32[128,57,1,128]{3,2,1,0:T(1,128)} async-done(((f32[128,57,1,128]{3,2,1,0:T(1,128)}), f32[128,57,1,128]{3,2,1,0:T(1,128)}, u32[]{:S(2)}, u32[]{:S(2)}) %all-to-all-start) | async-done | bytes 3735584 | tf_op jit(solution)/shard_map/all_to_all | solution.py:388
  67.8 0.1 broadcast_in_dim.11.refs_6_
  67.9 0.1 broadcast_in_dim.12.refs_7_
  68.0 0.0 copy-start
  68.0 3.3 %mix_first.1 = (f32[16,80,128]{2,1,0:T(8,128)S(1)}, f32[16,80,128]{2,1,0:T(8,128)S(1)}, f32[3648,128]{1,0:T(8,128)S(1)}) custom-call(s32[1]{0:T(128)} %bitcast.core_ref.refs_0_, f32[7296,128]{1,0:T(8,128)} %bitcast.3.arrived_hbm, f32[2,32,128]{2,1,0:T(8,128)S(1)} %maximum_select_fusion.share_ref, s32[2,32,128]{2,1,0:T(8,128)S(1)} %add_select_fusion.partner_ref), custom_call_target="tpu_custom_call" | custom-call | bytes 8388608 | tf_op jit(solution)/shard_map/mix_first/pallas_call | solution.py:225
  71.3 1.0 %collective-permute-start.3 = (f32[16,80,128]{2,1,0:T(8,128)S(1)}, f32[16,80,128]{2,1,0:T(8,128)S(1)}, u32[]{:S(2)}, u32[]{:S(2)}) collective-permute-start(f32[16,80,128]{2,1,0:T(8,128)S(1)} %get-tuple-element.30), channel_id=1, source_target_pairs={{0,1},{1,0},{2,3},{3,2},{4,5},{5,4},{6,7},{7,6},{8,9},{9,8},{10,11... | collective-permute-start | bytes 1966088 | tf_op jit(solution)/shard_map/ppermute | solution.py:395
  72.3 2.3 %mix_second.1 = (f32[16,80,128]{2,1,0:T(8,128)S(1)}, f32[16,80,128]{2,1,0:T(8,128)S(1)}) custom-call(s32[1]{0:T(128)} %bitcast.core_ref.refs_0_, f32[3648,128]{1,0:T(8,128)S(1)} %get-tuple-element.21.rest_ref, f32[2,32,128]{2,1,0:T(8,128)S(1)} %maximum_select_fusion.share_ref, s32[2,32,128]{2,1,0:T(8,128)S(1)} %add_select_fusion.partner_ref), custom_call_target="tpu_custom_call" | custom-call | bytes 8388608 | tf_op jit(solution)/shard_map/mix_second/pallas_call | solution.py:238
  74.6 0.3 collective-permute-start.2
  74.8 0.0 collective-permute-done.3.refs_2_
  74.9 0.0 copy-done
  74.9 4.2 %react.2.refs_8_ = f32[150,4096]{1,0:T(8,128)} custom-call(s32[1]{0:T(128)} %bitcast.core_ref.refs_0_, f32[16,80,128]{2,1,0:T(8,128)S(1)} %get-tuple-element.29.refs_1_, f32[16,80,128]{2,1,0:T(8,128)S(1)} %collective-permute-done.3.refs_2_, f32[32,128]{1,0:T(8,128)S(1)} %bitcast.11, bf16[160,480]{1,0:T(8,128)(2,1)S(1)} %pad_maximum_fusion.refs_4_, ...), custom_call_target="tpu_custom_call" | custom-call | flops 3221225472 | bytes 8388608 | tf_op jit(solution)/shard_map/react/pallas_call | solution.py:323
  79.1 0.0 collective-permute-done.2.refs_2_
  79.1 4.2 %react.3 = f32[150,4096]{1,0:T(8,128)} custom-call(s32[1]{0:T(128)} %bitcast.core_ref.refs_0_, f32[16,80,128]{2,1,0:T(8,128)S(1)} %get-tuple-element.22.refs_1_, f32[16,80,128]{2,1,0:T(8,128)S(1)} %collective-permute-done.2.refs_2_, f32[32,128]{1,0:T(8,128)S(1)} %bitcast.12, ...), custom_call_target="tpu_custom_call", output_to_operand_aliasing={{}: (8, {})} | custom-call | flops 3221225472 | bytes 8388608 | tf_op jit(solution)/shard_map/react/pallas_call | solution.py:323
  (11 shorter events, 0.1 us)
Async XLA Ops:
  8.0 12.0 %copy-start.3 = (f32[4096]{0:T(1024)S(1)}, f32[4096]{0:T(1024)}, u32[]{:S(2)}) copy-start(f32[4096]{0:T(1024)} %param.12) | copy-start | bytes 49156
  8.1 13.2 %copy-start.4 = (s32[4096]{0:T(1024)S(1)}, s32[4096]{0:T(1024)}, u32[]{:S(2)}) copy-start(s32[4096]{0:T(1024)} %param.13) | copy-start | bytes 49156
  8.1 13.3 %copy-start.1 = (f32[150,150]{1,0:T(8,128)S(1)}, f32[150,150]{1,0:T(8,128)}, u32[]{:S(2)}) copy-start(f32[150,150]{1,0:T(8,128)} %param.19) | copy-start | bytes 270004
  8.1 13.3 %copy-start.5 = (s32[10,10]{1,0:T(8,128)S(1)}, s32[10,10]{1,0:T(8,128)}, u32[]{:S(2)}) copy-start(s32[10,10]{1,0:T(8,128)} %param.18) | copy-start | bytes 1204
  8.1 59.7 %all-to-all-start = ((f32[128,57,1,128]{3,2,1,0:T(1,128)}), f32[128,57,1,128]{3,2,1,0:T(1,128)}, u32[]{:S(2)}, u32[]{:S(2)}) async-start(f32[128,57,1,128]{3,2,1,0:T(1,128)} %bitcast.13), calls=%async_computation | async-start | bytes 7471104 | tf_op jit(solution)/shard_map/all_to_all | solution.py:388
  20.0 2.0 %copy-start.2 = (f32[150,150]{1,0:T(8,128)S(1)}, f32[150,150]{1,0:T(8,128)}, u32[]{:S(2)}) copy-start(f32[150,150]{1,0:T(8,128)} %param.17) | copy-start | bytes 270004
  20.0 2.0 %copy-start.6 = (pred[80]{0:T(512)(128)(4,1)S(1)}, pred[80]{0:T(512)(128)(4,1)}, u32[]{:S(2)}) copy-start(pred[80]{0:T(512)(128)(4,1)} %constant.16.clone.1) | copy-start | bytes 244
  20.0 2.3 %copy-start.7 = (f32[150]{0:T(256)S(1)}, f32[150]{0:T(256)}, u32[]{:S(2)}) copy-start(f32[150]{0:T(256)} %param.16) | copy-start | bytes 1804
  20.0 2.4 %copy-start.8 = (f32[150]{0:T(256)S(1)}, f32[150]{0:T(256)}, u32[]{:S(2)}) copy-start(f32[150]{0:T(256)} %param.15) | copy-start | bytes 1804
  20.1 3.0 %collective-permute-start = (f32[32,128]{1,0:T(8,128)S(1)}, f32[32,128]{1,0:T(8,128)S(1)}, u32[]{:S(2)}, u32[]{:S(2)}) collective-permute-start(f32[32,128]{1,0:T(8,128)S(1)} %bitcast.14), channel_id=1, source_target_pairs={{0,1},{1,0},{2,3},{3,2},{4,5},{5,4},{6,7},{7,6},{8,9},{9,8},{10,11... | collective-permute-start | bytes 49160 | tf_op jit(solution)/shard_map/ppermute | solution.py:374
  21.3 1.8 %collective-permute-start.1 = (s32[32,128]{1,0:T(8,128)S(1)}, s32[32,128]{1,0:T(8,128)S(1)}, u32[]{:S(2)}, u32[]{:S(2)}) collective-permute-start(s32[32,128]{1,0:T(8,128)S(1)} %bitcast.16), channel_id=1, source_target_pairs={{0,1},{1,0},{2,3},{3,2},{4,5},{5,4},{6,7},{7,6},{8,9},{9,8},{10,11... | collective-permute-start | bytes 49160 | tf_op jit(solution)/shard_map/ppermute | solution.py:374
  68.0 6.8 %copy-start = (f32[4096]{0:T(1024)S(1)}, f32[4096]{0:T(1024)}, u32[]{:S(2)}) copy-start(f32[4096]{0:T(1024)} %param.14) | copy-start | bytes 49156
  71.3 3.5 %collective-permute-start.3 = (f32[16,80,128]{2,1,0:T(8,128)S(1)}, f32[16,80,128]{2,1,0:T(8,128)S(1)}, u32[]{:S(2)}, u32[]{:S(2)}) collective-permute-start(f32[16,80,128]{2,1,0:T(8,128)S(1)} %get-tuple-element.30), channel_id=1, source_target_pairs={{0,1},{1,0},{2,3},{3,2},{4,5},{5,4},{6,7},{7,6},{8,9},{9,8},{10,11... | collective-permute-start | bytes 1966088 | tf_op jit(solution)/shard_map/ppermute | solution.py:395
  74.6 4.5 %collective-permute-start.2 = (f32[16,80,128]{2,1,0:T(8,128)S(1)}, f32[16,80,128]{2,1,0:T(8,128)S(1)}, u32[]{:S(2)}, u32[]{:S(2)}) collective-permute-start(f32[16,80,128]{2,1,0:T(8,128)S(1)} %get-tuple-element.23), channel_id=1, source_target_pairs={{0,1},{1,0},{2,3},{3,2},{4,5},{5,4},{6,7},{7,6},{8,9},{9,8},{10,11... | collective-permute-start | bytes 1966088 | tf_op jit(solution)/shard_map/ppermute | solution.py:395

commit v7 on v6

--- a/solution.py
+++ b/solution.py
@@ -20,7 +20,6 @@
 CHUNK = 3 * QUARTER
 GROUP = 256
 TOGETHER = 2
-PARTS = 2
 PIECES = 8
 
 
@@ -258,16 +257,12 @@
 
 
 def react_kernel(
-    first, core_ref, mine_ref, other_ref, photo_ref, coupled_ref, precond_ref, production_ref, loss_ref, *rest
+    first, core_ref, mine_ref, other_ref, photo_ref, coupled_ref, precond_ref, production_ref, loss_ref, result_ref, done
 ):
-    out_ref, result_ref, sems = rest[-3:]
     blocks = mine_ref.shape[0]
-    steps = result_ref.shape[0]
+    steps, species, width = result_ref.shape
     each = blocks // steps
-    width = each * LANES
-    species = out_ref.shape[0]
     core = core_ref[0]
-    copies = []
     for step in range(steps):
         columns = []
         for m in range(step * each, (step + 1) * each):
@@ -295,47 +290,59 @@
         result = current * present
         result_ref[step, :HALF] = result[:HALF]
         result_ref[step, HALF:] = result[BLOCK : BLOCK + species - HALF]
-        start = first * LANES + step * width
-        copy = pltpu.make_async_copy(
-            result_ref.at[step], out_ref.at[:, start : start + width], sems.at[step]
-        )
+        done(step)
+
+
+def react_first_kernel(*refs):
+    react_kernel(0, *refs, lambda step: None)
+
+
+def react_second_kernel(*refs):
+    *operands, earlier_ref, out_ref, result_ref, sems = refs
+    steps, _, width = result_ref.shape
+    blocks = steps * width // LANES
+    copies = []
+
+    def send(ref, step, place):
+        columns = slice(place * width, (place + 1) * width)
+        copy = pltpu.make_async_copy(ref.at[step], out_ref.at[:, columns], sems.at[place])
         copy.start()
         copies.append(copy)
+
+    for step in range(steps):
+        send(earlier_ref, step, step)
+    react_kernel(blocks, *operands, result_ref, lambda step: send(result_ref, step, steps + step))
     for copy in copies:
         copy.wait()
 
 
-def react(part, species, core, mine, other, photo, weights, so_far):
-    blocks = mine.shape[0]
+def react(species, core, halves, others, photo, weights):
+    blocks = others[0].shape[0]
     steps = 2
-    width = blocks * LANES // steps
-    in_specs = [IN_SMEM] + [IN_VMEM] * 7
-    operands = [core, mine, other, photo, *weights]
-    aliases = {}
-    if so_far is not None:
-        in_specs.append(pl.BlockSpec(memory_space=pl.ANY))
-        operands.append(so_far)
-        aliases = {len(operands) - 1: 0}
-
-    def kernel(*refs):
-        react_kernel(part * blocks, *refs)
-
+    shape = (steps, species, blocks * LANES // steps)
+    params = pltpu.CompilerParams(vmem_limit_bytes=16 * 1024 * 1024)
+    cost = pl.CostEstimate(
+        flops=6 * 2 * 256 * 512 * blocks * LANES, bytes_accessed=8 * 1024 * 1024, transcendentals=0
+    )
+    earlier = pl.pallas_call(
+        react_first_kernel,
+        out_shape=jax.ShapeDtypeStruct(shape, jnp.float32),
+        in_specs=[IN_SMEM] + [IN_VMEM] * 7,
+        out_specs=IN_VMEM,
+        compiler_params=params,
+        cost_estimate=cost,
+        name="react_first",
+    )(core, halves[0][0], others[0], photo, *weights)
     return pl.pallas_call(
-        kernel,
-        out_shape=jax.ShapeDtypeStruct((species, blocks * PARTS * LANES), jnp.float32),
-        in_specs=in_specs,
+        react_second_kernel,
+        out_shape=jax.ShapeDtypeStruct((species, 2 * blocks * LANES), jnp.float32),
+        in_specs=[IN_SMEM] + [IN_VMEM] * 8,
         out_specs=pl.BlockSpec(memory_space=pl.ANY),
-        scratch_shapes=[
-            pltpu.VMEM((steps, species, width), jnp.float32),
-            pltpu.SemaphoreType.DMA((steps,)),
-        ],
-        input_output_aliases=aliases,
-        compiler_params=pltpu.CompilerParams(vmem_limit_bytes=16 * 1024 * 1024),
-        cost_estimate=pl.CostEstimate(
-            flops=6 * 2 * 256 * 512 * blocks * LANES, bytes_accessed=8 * 1024 * 1024, transcendentals=0
-        ),
-        name="react",
-    )(*operands)
+        scratch_shapes=[pltpu.VMEM(shape, jnp.float32), pltpu.SemaphoreType.DMA((2 * steps,))],
+        compiler_params=params,
+        cost_estimate=cost,
+        name="react_second",
+    )(core, halves[1][0], others[1], photo, *weights, earlier)
 
 
 def spread(array, axis):
@@ -393,10 +400,7 @@
     )
     halves = mix(core, arrived, share, index)
     others = [lax.ppermute(give, "core", SWAP) for _, give in halves]
-    result = None
-    for part in range(PARTS):
-        result = react(part, species, core, halves[part][0], others[part], photo, weights, result)
-    return result
+    return react(species, core, halves, others, photo, weights)
 
 
 def solution(mesh):

time: 83.6 us -> 82.8 us (level)
  Pallas kernels: 22 us -> 21.1 us
    pallas_call x2, Pallas kernels: 8.38 us -> 7.54 us  [the longest x1 4.2 us: react(): pl.pallas_call(react_second_kernel, out_shape=jax.ShapeDtypeStruct((speci...]
  transfers between devices with their start and end apart: 5 -> 5, of which waited for: 1 -> 1; matrix products, arithmetic and copies ran while one was open for 2% -> 2% of each run, Pallas kernels for 8% -> 7%
where the time goes in v7:
time: 82.8 us; the launch traced here: 82.6 us
  waiting for transfers between devices  44.7 us (54%)
  Pallas kernels  21.1 us (25%)
  starting transfers between devices  14.4 us (17%)
  local copies, waits for them, and re-layouts  1.07 us (1%)
    all_to_all x1, waiting for transfers between devices, shards(): lax.all_to_all(packed, ('lat', 'chip', 'core'), split_axis=0, concat_axis...  44.7 us
    all_to_all x1, starting transfers between devices, shards(): lax.all_to_all(packed, ('lat', 'chip', 'core'), split_axis=0, concat_axis...  11.9 us
    pallas_call x1, Pallas kernels, pack(): pl.pallas_call(pack_kernel, out_shape=jax.ShapeDtypeStruct((devices * CHU...  8.04 us
    pallas_call x1, Pallas kernels, react(): pl.pallas_call(react_second_kernel, out_shape=jax.ShapeDtypeStruct((speci...  4.2 us
    pallas_call x1, Pallas kernels, react(): pl.pallas_call(react_first_kernel, out_shape=jax.ShapeDtypeStruct(shape,...  3.34 us
    pallas_call x1, Pallas kernels, mix(): pl.pallas_call(mix_first_kernel, out_shape=(shape, shape, rest_shape), in...  3.29 us
    pallas_call x1, Pallas kernels, mix(): pl.pallas_call(mix_second_kernel, out_shape=(shape, shape), in_specs=[IN_...  2.27 us
  transfers between devices with their start and end apart: 5, of which 1 were waited for; matrix products, arithmetic and copies ran while one was open for 2% of the time, Pallas kernels for 7%

profile of v7, /device:TPU:1, one launch (start us, length us, event | category | flops | bytes accessed | tf_op | source)
XLA Modules:
  0.0 82.6 jit_solution(4891427427540643218)
XLA Ops:
  0.0 8.0 %pack.1 = f32[7296,128]{1,0:T(8,128)} custom-call(f32[150,2048]{1,0:T(8,128)} %conc_hbm.1, s32[16,128]{1,0:T(8,128)} %bitcast.20), custom_call_target="tpu_custom_call" | custom-call | tf_op jit(solution)/shard_map/pack/pallas_call | solution.py:134
  8.0 0.0 copy-start.3
  8.1 0.0 copy-start.4
  8.1 0.0 copy-start.1
  8.1 0.0 copy-start.5
  8.1 11.9 %all-to-all-start = ((f32[128,57,1,128]{3,2,1,0:T(1,128)}), f32[128,57,1,128]{3,2,1,0:T(1,128)}, u32[]{:S(2)}, u32[]{:S(2)}) async-start(f32[128,57,1,128]{3,2,1,0:T(1,128)} %bitcast.13), calls=%async_computation | async-start | bytes 7471104 | tf_op jit(solution)/shard_map/all_to_all | solution.py:395
  20.0 0.0 copy-start.2
  20.0 0.0 copy-start.6
  20.0 0.0 copy-done.3
  20.0 1.2 %collective-permute-start = (f32[32,128]{1,0:T(8,128)S(1)}, f32[32,128]{1,0:T(8,128)S(1)}, u32[]{:S(2)}, u32[]{:S(2)}) collective-permute-start(f32[32,128]{1,0:T(8,128)S(1)} %bitcast.14), channel_id=1, source_target_pairs={{0,1},{1,0},{2,3},{3,2},{4,5},{5,4},{6,7},{7,6},{8,9},{9,8},{10,11... | collective-permute-start | bytes 49160 | tf_op jit(solution)/shard_map/ppermute | solution.py:381
  21.3 0.0 copy-done.4
  21.3 0.1 collective-permute-start.1
  21.4 0.0 copy-done.1
  21.4 0.0 copy-done.5
  21.4 0.1 mul.34
  21.5 0.0 copy-start.7
  21.6 0.0 copy-start.8
  21.6 0.4 mul.35
  22.0 0.0 copy-done.2
  22.0 0.0 copy-done.6
  22.0 0.1 slice_select_fusion.3
  22.1 0.1 split.31
  22.2 0.1 split.32
  22.3 0.0 copy-done.7
  22.3 0.1 split.29
  22.4 0.0 copy-done.8
  22.4 0.1 split.28
  22.5 0.1 reduce-precision_convert_fusion.1
  22.6 0.1 pad_maximum_fusion.refs_4_
  22.8 0.1 reduce-precision_convert_fusion
  22.9 0.1 pad_maximum_fusion.1.refs_5_
  23.0 0.1 select_maximum_fusion.4
  23.1 0.0 collective-permute-done
  23.1 0.0 collective-permute-done.1
  23.1 44.7 %all-to-all-done = f32[128,57,1,128]{3,2,1,0:T(1,128)} async-done(((f32[128,57,1,128]{3,2,1,0:T(1,128)}), f32[128,57,1,128]{3,2,1,0:T(1,128)}, u32[]{:S(2)}, u32[]{:S(2)}) %all-to-all-start) | async-done | bytes 3735584 | tf_op jit(solution)/shard_map/all_to_all | solution.py:395
  67.8 0.1 broadcast_in_dim.11.refs_6_
  67.9 0.1 broadcast_in_dim.12.refs_7_
  68.0 3.3 %mix_first.1 = (f32[16,80,128]{2,1,0:T(8,128)S(1)}, f32[16,80,128]{2,1,0:T(8,128)S(1)}, f32[3648,128]{1,0:T(8,128)S(1)}) custom-call(s32[1]{0:T(128)} %bitcast.core_ref.refs_0_, f32[7296,128]{1,0:T(8,128)} %bitcast.3.arrived_hbm, f32[2,32,128]{2,1,0:T(8,128)S(1)} %maximum_select_fusion.share_ref, s32[2,32,128]{2,1,0:T(8,128)S(1)} %add_select_fusion.partner_ref), custom_call_target="tpu_custom_call" | custom-call | bytes 8388608 | tf_op jit(solution)/shard_map/mix_first/pallas_call | solution.py:224
  71.3 0.0 copy-start
  71.3 1.0 %collective-permute-start.3 = (f32[16,80,128]{2,1,0:T(8,128)S(1)}, f32[16,80,128]{2,1,0:T(8,128)S(1)}, u32[]{:S(2)}, u32[]{:S(2)}) collective-permute-start(f32[16,80,128]{2,1,0:T(8,128)S(1)} %get-tuple-element.30), channel_id=1, source_target_pairs={{0,1},{1,0},{2,3},{3,2},{4,5},{5,4},{6,7},{7,6},{8,9},{9,8},{10,11... | collective-permute-start | bytes 1966088 | tf_op jit(solution)/shard_map/ppermute | solution.py:402
  72.3 2.3 %mix_second.1 = (f32[16,80,128]{2,1,0:T(8,128)S(1)}, f32[16,80,128]{2,1,0:T(8,128)S(1)}) custom-call(s32[1]{0:T(128)} %bitcast.core_ref.refs_0_, f32[3648,128]{1,0:T(8,128)S(1)} %get-tuple-element.21.rest_ref, f32[2,32,128]{2,1,0:T(8,128)S(1)} %maximum_select_fusion.share_ref, s32[2,32,128]{2,1,0:T(8,128)S(1)} %add_select_fusion.partner_ref), custom_call_target="tpu_custom_call" | custom-call | bytes 8388608 | tf_op jit(solution)/shard_map/mix_second/pallas_call | solution.py:237
  74.6 0.3 collective-permute-start.2
  74.8 0.0 collective-permute-done.3.refs_2_
  74.8 0.0 copy-done
  74.9 3.3 %react_first.1.refs_8_ = f32[2,150,1024]{2,1,0:T(8,128)S(1)} custom-call(s32[1]{0:T(128)} %bitcast.core_ref.refs_0_, f32[16,80,128]{2,1,0:T(8,128)S(1)} %get-tuple-element.29.refs_1_, f32[16,80,128]{2,1,0:T(8,128)S(1)} %collective-permute-done.3.refs_2_, f32[32,128]{1,0:T(8,128)S(1)} %bitcast.11, bf16[160,480]{1,0:T(8,128)(2,1)S(1)} %pad_maximum_fusion.refs_4_, ...), custom_call_target="tpu_custom_call" | custom-call | flops 3221225472 | bytes 8388608 | tf_op jit(solution)/shard_map/react_first/pallas_call | solution.py:327
  78.2 0.0 collective-permute-done.2.refs_2_
  78.2 4.2 %react_second.1 = f32[150,4096]{1,0:T(8,128)} custom-call(s32[1]{0:T(128)} %bitcast.core_ref.refs_0_, f32[16,80,128]{2,1,0:T(8,128)S(1)} %get-tuple-element.22.refs_1_, f32[16,80,128]{2,1,0:T(8,128)S(1)} %collective-permute-done.2.refs_2_, f32[32,128]{1,0:T(8,128)S(1)} %bitcast.12, bf16[160,480]{1,0:T(8,128)(2,1)S(1)} %pad_maximum_fusion.refs_4_, ...), custom_call_target="tpu_custom_call" | custom-call | flops 3221225472 | bytes 8388608 | tf_op jit(solution)/shard_map/react_second/pallas_call | solution.py:336
  (11 shorter events, 0.1 us)
Async XLA Ops:
  8.0 12.0 %copy-start.3 = (f32[4096]{0:T(1024)S(1)}, f32[4096]{0:T(1024)}, u32[]{:S(2)}) copy-start(f32[4096]{0:T(1024)} %param.12) | copy-start | bytes 49156
  8.1 13.2 %copy-start.4 = (s32[4096]{0:T(1024)S(1)}, s32[4096]{0:T(1024)}, u32[]{:S(2)}) copy-start(s32[4096]{0:T(1024)} %param.13) | copy-start | bytes 49156
  8.1 13.3 %copy-start.1 = (f32[150,150]{1,0:T(8,128)S(1)}, f32[150,150]{1,0:T(8,128)}, u32[]{:S(2)}) copy-start(f32[150,150]{1,0:T(8,128)} %param.19) | copy-start | bytes 270004
  8.1 13.3 %copy-start.5 = (s32[10,10]{1,0:T(8,128)S(1)}, s32[10,10]{1,0:T(8,128)}, u32[]{:S(2)}) copy-start(s32[10,10]{1,0:T(8,128)} %param.18) | copy-start | bytes 1204
  8.1 59.7 %all-to-all-start = ((f32[128,57,1,128]{3,2,1,0:T(1,128)}), f32[128,57,1,128]{3,2,1,0:T(1,128)}, u32[]{:S(2)}, u32[]{:S(2)}) async-start(f32[128,57,1,128]{3,2,1,0:T(1,128)} %bitcast.13), calls=%async_computation | async-start | bytes 7471104 | tf_op jit(solution)/shard_map/all_to_all | solution.py:395
  20.0 2.0 %copy-start.2 = (f32[150,150]{1,0:T(8,128)S(1)}, f32[150,150]{1,0:T(8,128)}, u32[]{:S(2)}) copy-start(f32[150,150]{1,0:T(8,128)} %param.17) | copy-start | bytes 270004
  20.0 2.0 %copy-start.6 = (pred[80]{0:T(512)(128)(4,1)S(1)}, pred[80]{0:T(512)(128)(4,1)}, u32[]{:S(2)}) copy-start(pred[80]{0:T(512)(128)(4,1)} %constant.16.clone.1) | copy-start | bytes 244
  20.0 3.1 %collective-permute-start = (f32[32,128]{1,0:T(8,128)S(1)}, f32[32,128]{1,0:T(8,128)S(1)}, u32[]{:S(2)}, u32[]{:S(2)}) collective-permute-start(f32[32,128]{1,0:T(8,128)S(1)} %bitcast.14), channel_id=1, source_target_pairs={{0,1},{1,0},{2,3},{3,2},{4,5},{5,4},{6,7},{7,6},{8,9},{9,8},{10,11... | collective-permute-start | bytes 49160 | tf_op jit(solution)/shard_map/ppermute | solution.py:381
  21.3 1.9 %collective-permute-start.1 = (s32[32,128]{1,0:T(8,128)S(1)}, s32[32,128]{1,0:T(8,128)S(1)}, u32[]{:S(2)}, u32[]{:S(2)}) collective-permute-start(s32[32,128]{1,0:T(8,128)S(1)} %bitcast.16), channel_id=1, source_target_pairs={{0,1},{1,0},{2,3},{3,2},{4,5},{5,4},{6,7},{7,6},{8,9},{9,8},{10,11... | collective-permute-start | bytes 49160 | tf_op jit(solution)/shard_map/ppermute | solution.py:381
  21.5 0.8 copy-start.7
  21.6 0.9 %copy-start.8 = (f32[150]{0:T(256)S(1)}, f32[150]{0:T(256)}, u32[]{:S(2)}) copy-start(f32[150]{0:T(256)} %param.15) | copy-start | bytes 1804
  71.3 3.5 %copy-start = (f32[4096]{0:T(1024)S(1)}, f32[4096]{0:T(1024)}, u32[]{:S(2)}) copy-start(f32[4096]{0:T(1024)} %param.14) | copy-start | bytes 49156
  71.3 3.5 %collective-permute-start.3 = (f32[16,80,128]{2,1,0:T(8,128)S(1)}, f32[16,80,128]{2,1,0:T(8,128)S(1)}, u32[]{:S(2)}, u32[]{:S(2)}) collective-permute-start(f32[16,80,128]{2,1,0:T(8,128)S(1)} %get-tuple-element.30), channel_id=1, source_target_pairs={{0,1},{1,0},{2,3},{3,2},{4,5},{5,4},{6,7},{7,6},{8,9},{9,8},{10,11... | collective-permute-start | bytes 1966088 | tf_op jit(solution)/shard_map/ppermute | solution.py:402
  74.6 3.6 %collective-permute-start.2 = (f32[16,80,128]{2,1,0:T(8,128)S(1)}, f32[16,80,128]{2,1,0:T(8,128)S(1)}, u32[]{:S(2)}, u32[]{:S(2)}) collective-permute-start(f32[16,80,128]{2,1,0:T(8,128)S(1)} %get-tuple-element.23), channel_id=1, source_target_pairs={{0,1},{1,0},{2,3},{3,2},{4,5},{5,4},{6,7},{7,6},{8,9},{9,8},{10,11... | collective-permute-start | bytes 1966088 | tf_op jit(solution)/shard_map/ppermute | solution.py:402

commit v8 on v7

--- a/solution.py
+++ b/solution.py
@@ -12,6 +12,7 @@
 
 LANES = 128
 CAP = 32
+SPARE = 8
 QUARTER = 19
 HALF = 4 * QUARTER
 SENT = 2 * HALF
@@ -120,7 +121,7 @@
     steps = parcels * 2 // GROUP // TOGETHER
     for i in range(steps):
         arrange(i, move(i))
-    for i in range(out_ref.shape[0] // sent):
+    for i in range(out_hbm.shape[0] // sent):
         write(i).wait()
 
 
@@ -137,7 +138,7 @@
         in_specs=[IN_HBM, IN_HBM],
         out_specs=IN_HBM,
         scratch_shapes=[
-            pltpu.VMEM((devices * CHUNK, LANES), jnp.float32),
+            pltpu.VMEM((devices * CHUNK + SPARE, LANES), jnp.float32),
             pltpu.VMEM(conc.shape, jnp.float32),
             pltpu.VMEM(targets.shape, jnp.int32),
             pltpu.VMEM((2 * SENT, parcels), jnp.bfloat16),
@@ -188,7 +189,9 @@
         rows = slice(piece * length, (piece + 1) * length)
         reads.append(pltpu.make_async_copy(arrived_hbm.at[rows], land.at[rows], sems.at[piece]))
     rest = pltpu.make_async_copy(
-        arrived_hbm.at[PIECES * length : 2 * PIECES * length], rest_ref, sems.at[PIECES]
+        arrived_hbm.at[PIECES * length : 2 * PIECES * length],
+        rest_ref.at[0 : PIECES * length],
+        sems.at[PIECES],
     )
     for read in (*reads, rest):
         read.start()
@@ -220,14 +223,14 @@
     shape = jax.ShapeDtypeStruct((blocks, BLOCK, LANES), jnp.float32)
     params = pltpu.CompilerParams(vmem_limit_bytes=8 * 1024 * 1024)
     cost = pl.CostEstimate(flops=0, bytes_accessed=8 * 1024 * 1024, transcendentals=0)
-    rest_shape = jax.ShapeDtypeStruct((half, LANES), jnp.float32)
+    rest_shape = jax.ShapeDtypeStruct((half + SPARE, LANES), jnp.float32)
     keep, give, rest = pl.pallas_call(
         mix_first_kernel,
         out_shape=(shape, shape, rest_shape),
         in_specs=[IN_SMEM, IN_HBM, IN_VMEM, IN_VMEM],
         out_specs=(IN_VMEM, IN_VMEM, IN_VMEM),
         scratch_shapes=[
-            pltpu.VMEM((half, LANES), jnp.float32),
+            pltpu.VMEM((half + SPARE, LANES), jnp.float32),
             pltpu.SemaphoreType.DMA((PIECES + 1,)),
         ],
         compiler_params=params,

time: 82.8 us -> 82.8 us (level)
  no operation moved by 1% of the time
where the time goes in v8:
time: 82.8 us; the launch traced here: 82.6 us
  waiting for transfers between devices  44.7 us (54%)
  Pallas kernels  21.1 us (25%)
  starting transfers between devices  14.4 us (17%)
  local copies, waits for them, and re-layouts  1.07 us (1%)
    all_to_all x1, waiting for transfers between devices, shards(): lax.all_to_all(packed, ('lat', 'chip', 'core'), split_axis=0, concat_axis...  44.7 us
    all_to_all x1, starting transfers between devices, shards(): lax.all_to_all(packed, ('lat', 'chip', 'core'), split_axis=0, concat_axis...  11.9 us
    pallas_call x1, Pallas kernels, pack(): pl.pallas_call(pack_kernel, out_shape=jax.ShapeDtypeStruct((devices * CHU...  8.04 us
    pallas_call x1, Pallas kernels, react(): pl.pallas_call(react_second_kernel, out_shape=jax.ShapeDtypeStruct((speci...  4.2 us
    pallas_call x1, Pallas kernels, react(): pl.pallas_call(react_first_kernel, out_shape=jax.ShapeDtypeStruct(shape,...  3.34 us
    pallas_call x1, Pallas kernels, mix(): pl.pallas_call(mix_first_kernel, out_shape=(shape, shape, rest_shape), in...  3.29 us
    pallas_call x1, Pallas kernels, mix(): pl.pallas_call(mix_second_kernel, out_shape=(shape, shape), in_specs=[IN_...  2.27 us
  transfers between devices with their start and end apart: 5, of which 1 were waited for; matrix products, arithmetic and copies ran while one was open for 2% of the time, Pallas kernels for 7%

profile of v8, /device:TPU:1, one launch (start us, length us, event | category | flops | bytes accessed | tf_op | source)
XLA Modules:
  0.0 82.6 jit_solution(15703727528493064207)
XLA Ops:
  0.0 8.0 %pack.1 = f32[7296,128]{1,0:T(8,128)} custom-call(f32[150,2048]{1,0:T(8,128)} %conc_hbm.1, s32[16,128]{1,0:T(8,128)} %bitcast.20), custom_call_target="tpu_custom_call" | custom-call | tf_op jit(solution)/shard_map/pack/pallas_call | solution.py:135
  8.0 0.0 copy-start.3
  8.1 0.0 copy-start.4
  8.1 0.0 copy-start.1
  8.1 0.0 copy-start.5
  8.1 11.9 %all-to-all-start = ((f32[128,57,1,128]{3,2,1,0:T(1,128)}), f32[128,57,1,128]{3,2,1,0:T(1,128)}, u32[]{:S(2)}, u32[]{:S(2)}) async-start(f32[128,57,1,128]{3,2,1,0:T(1,128)} %bitcast.13), calls=%async_computation | async-start | bytes 7471104 | tf_op jit(solution)/shard_map/all_to_all | solution.py:398
  20.0 0.0 copy-start.2
  20.0 0.0 copy-start.6
  20.0 0.0 copy-done.3
  20.0 1.2 %collective-permute-start = (f32[32,128]{1,0:T(8,128)S(1)}, f32[32,128]{1,0:T(8,128)S(1)}, u32[]{:S(2)}, u32[]{:S(2)}) collective-permute-start(f32[32,128]{1,0:T(8,128)S(1)} %bitcast.14), channel_id=1, source_target_pairs={{0,1},{1,0},{2,3},{3,2},{4,5},{5,4},{6,7},{7,6},{8,9},{9,8},{10,11... | collective-permute-start | bytes 49160 | tf_op jit(solution)/shard_map/ppermute | solution.py:384
  21.3 0.0 copy-done.4
  21.3 0.1 collective-permute-start.1
  21.4 0.0 copy-done.1
  21.4 0.0 copy-done.5
  21.4 0.1 mul.34
  21.5 0.0 copy-start.7
  21.6 0.0 copy-start.8
  21.6 0.4 mul.35
  22.0 0.0 copy-done.2
  22.0 0.0 copy-done.6
  22.0 0.1 slice_select_fusion.3
  22.1 0.1 split.31
  22.2 0.1 split.32
  22.3 0.0 copy-done.7
  22.3 0.1 split.29
  22.4 0.0 copy-done.8
  22.4 0.1 split.28
  22.5 0.1 reduce-precision_convert_fusion.1
  22.6 0.1 pad_maximum_fusion.refs_4_
  22.8 0.1 reduce-precision_convert_fusion
  22.9 0.1 pad_maximum_fusion.1.refs_5_
  23.0 0.1 select_maximum_fusion.4
  23.1 0.0 collective-permute-done
  23.1 0.0 collective-permute-done.1
  23.1 44.7 %all-to-all-done = f32[128,57,1,128]{3,2,1,0:T(1,128)} async-done(((f32[128,57,1,128]{3,2,1,0:T(1,128)}), f32[128,57,1,128]{3,2,1,0:T(1,128)}, u32[]{:S(2)}, u32[]{:S(2)}) %all-to-all-start) | async-done | bytes 3735584 | tf_op jit(solution)/shard_map/all_to_all | solution.py:398
  67.8 0.1 broadcast_in_dim.11.refs_6_
  67.9 0.1 broadcast_in_dim.12.refs_7_
  68.0 3.3 %mix_first.1 = (f32[16,80,128]{2,1,0:T(8,128)S(1)}, f32[16,80,128]{2,1,0:T(8,128)S(1)}, f32[3656,128]{1,0:T(8,128)S(1)}) custom-call(s32[1]{0:T(128)} %bitcast.core_ref.refs_0_, f32[7296,128]{1,0:T(8,128)} %bitcast.3.arrived_hbm, f32[2,32,128]{2,1,0:T(8,128)S(1)} %maximum_select_fusion.share_ref, s32[2,32,128]{2,1,0:T(8,128)S(1)} %add_select_fusion.partner_ref), custom_call_target="tpu_custom_call" | custom-call | bytes 8388608 | tf_op jit(solution)/shard_map/mix_first/pallas_call | solution.py:227
  71.3 0.0 copy-start
  71.3 1.0 %collective-permute-start.3 = (f32[16,80,128]{2,1,0:T(8,128)S(1)}, f32[16,80,128]{2,1,0:T(8,128)S(1)}, u32[]{:S(2)}, u32[]{:S(2)}) collective-permute-start(f32[16,80,128]{2,1,0:T(8,128)S(1)} %get-tuple-element.30), channel_id=1, source_target_pairs={{0,1},{1,0},{2,3},{3,2},{4,5},{5,4},{6,7},{7,6},{8,9},{9,8},{10,11... | collective-permute-start | bytes 1966088 | tf_op jit(solution)/shard_map/ppermute | solution.py:405
  72.3 2.3 %mix_second.1 = (f32[16,80,128]{2,1,0:T(8,128)S(1)}, f32[16,80,128]{2,1,0:T(8,128)S(1)}) custom-call(s32[1]{0:T(128)} %bitcast.core_ref.refs_0_, f32[3656,128]{1,0:T(8,128)S(1)} %get-tuple-element.21.rest_ref, f32[2,32,128]{2,1,0:T(8,128)S(1)} %maximum_select_fusion.share_ref, s32[2,32,128]{2,1,0:T(8,128)S(1)} %add_select_fusion.partner_ref), custom_call_target="tpu_custom_call" | custom-call | bytes 8388608 | tf_op jit(solution)/shard_map/mix_second/pallas_call | solution.py:240
  74.6 0.3 collective-permute-start.2
  74.8 0.0 collective-permute-done.3.refs_2_
  74.8 0.0 copy-done
  74.9 3.3 %react_first.1.refs_8_ = f32[2,150,1024]{2,1,0:T(8,128)S(1)} custom-call(s32[1]{0:T(128)} %bitcast.core_ref.refs_0_, f32[16,80,128]{2,1,0:T(8,128)S(1)} %get-tuple-element.29.refs_1_, f32[16,80,128]{2,1,0:T(8,128)S(1)} %collective-permute-done.3.refs_2_, f32[32,128]{1,0:T(8,128)S(1)} %bitcast.11, bf16[160,480]{1,0:T(8,128)(2,1)S(1)} %pad_maximum_fusion.refs_4_, ...), custom_call_target="tpu_custom_call" | custom-call | flops 3221225472 | bytes 8388608 | tf_op jit(solution)/shard_map/react_first/pallas_call | solution.py:330
  78.2 0.0 collective-permute-done.2.refs_2_
  78.2 4.2 %react_second.1 = f32[150,4096]{1,0:T(8,128)} custom-call(s32[1]{0:T(128)} %bitcast.core_ref.refs_0_, f32[16,80,128]{2,1,0:T(8,128)S(1)} %get-tuple-element.22.refs_1_, f32[16,80,128]{2,1,0:T(8,128)S(1)} %collective-permute-done.2.refs_2_, f32[32,128]{1,0:T(8,128)S(1)} %bitcast.12, bf16[160,480]{1,0:T(8,128)(2,1)S(1)} %pad_maximum_fusion.refs_4_, ...), custom_call_target="tpu_custom_call" | custom-call | flops 3221225472 | bytes 8388608 | tf_op jit(solution)/shard_map/react_second/pallas_call | solution.py:339
  (11 shorter events, 0.1 us)
Async XLA Ops:
  8.0 12.0 %copy-start.3 = (f32[4096]{0:T(1024)S(1)}, f32[4096]{0:T(1024)}, u32[]{:S(2)}) copy-start(f32[4096]{0:T(1024)} %param.12) | copy-start | bytes 49156
  8.1 13.2 %copy-start.4 = (s32[4096]{0:T(1024)S(1)}, s32[4096]{0:T(1024)}, u32[]{:S(2)}) copy-start(s32[4096]{0:T(1024)} %param.13) | copy-start | bytes 49156
  8.1 13.3 %copy-start.1 = (f32[150,150]{1,0:T(8,128)S(1)}, f32[150,150]{1,0:T(8,128)}, u32[]{:S(2)}) copy-start(f32[150,150]{1,0:T(8,128)} %param.19) | copy-start | bytes 270004
  8.1 13.3 %copy-start.5 = (s32[10,10]{1,0:T(8,128)S(1)}, s32[10,10]{1,0:T(8,128)}, u32[]{:S(2)}) copy-start(s32[10,10]{1,0:T(8,128)} %param.18) | copy-start | bytes 1204
  8.1 59.7 %all-to-all-start = ((f32[128,57,1,128]{3,2,1,0:T(1,128)}), f32[128,57,1,128]{3,2,1,0:T(1,128)}, u32[]{:S(2)}, u32[]{:S(2)}) async-start(f32[128,57,1,128]{3,2,1,0:T(1,128)} %bitcast.13), calls=%async_computation | async-start | bytes 7471104 | tf_op jit(solution)/shard_map/all_to_all | solution.py:398
  20.0 2.0 %copy-start.2 = (f32[150,150]{1,0:T(8,128)S(1)}, f32[150,150]{1,0:T(8,128)}, u32[]{:S(2)}) copy-start(f32[150,150]{1,0:T(8,128)} %param.17) | copy-start | bytes 270004
  20.0 2.0 %copy-start.6 = (pred[80]{0:T(512)(128)(4,1)S(1)}, pred[80]{0:T(512)(128)(4,1)}, u32[]{:S(2)}) copy-start(pred[80]{0:T(512)(128)(4,1)} %constant.16.clone.1) | copy-start | bytes 244
  20.0 3.1 %collective-permute-start = (f32[32,128]{1,0:T(8,128)S(1)}, f32[32,128]{1,0:T(8,128)S(1)}, u32[]{:S(2)}, u32[]{:S(2)}) collective-permute-start(f32[32,128]{1,0:T(8,128)S(1)} %bitcast.14), channel_id=1, source_target_pairs={{0,1},{1,0},{2,3},{3,2},{4,5},{5,4},{6,7},{7,6},{8,9},{9,8},{10,11... | collective-permute-start | bytes 49160 | tf_op jit(solution)/shard_map/ppermute | solution.py:384
  21.3 1.9 %collective-permute-start.1 = (s32[32,128]{1,0:T(8,128)S(1)}, s32[32,128]{1,0:T(8,128)S(1)}, u32[]{:S(2)}, u32[]{:S(2)}) collective-permute-start(s32[32,128]{1,0:T(8,128)S(1)} %bitcast.16), channel_id=1, source_target_pairs={{0,1},{1,0},{2,3},{3,2},{4,5},{5,4},{6,7},{7,6},{8,9},{9,8},{10,11... | collective-permute-start | bytes 49160 | tf_op jit(solution)/shard_map/ppermute | solution.py:384
  21.5 0.8 copy-start.7
  21.6 0.9 %copy-start.8 = (f32[150]{0:T(256)S(1)}, f32[150]{0:T(256)}, u32[]{:S(2)}) copy-start(f32[150]{0:T(256)} %param.15) | copy-start | bytes 1804
  71.3 3.5 %copy-start = (f32[4096]{0:T(1024)S(1)}, f32[4096]{0:T(1024)}, u32[]{:S(2)}) copy-start(f32[4096]{0:T(1024)} %param.14) | copy-start | bytes 49156
  71.3 3.5 %collective-permute-start.3 = (f32[16,80,128]{2,1,0:T(8,128)S(1)}, f32[16,80,128]{2,1,0:T(8,128)S(1)}, u32[]{:S(2)}, u32[]{:S(2)}) collective-permute-start(f32[16,80,128]{2,1,0:T(8,128)S(1)} %get-tuple-element.30), channel_id=1, source_target_pairs={{0,1},{1,0},{2,3},{3,2},{4,5},{5,4},{6,7},{7,6},{8,9},{9,8},{10,11... | collective-permute-start | bytes 1966088 | tf_op jit(solution)/shard_map/ppermute | solution.py:405
  74.6 3.6 %collective-permute-start.2 = (f32[16,80,128]{2,1,0:T(8,128)S(1)}, f32[16,80,128]{2,1,0:T(8,128)S(1)}, u32[]{:S(2)}, u32[]{:S(2)}) collective-permute-start(f32[16,80,128]{2,1,0:T(8,128)S(1)} %get-tuple-element.23), channel_id=1, source_target_pairs={{0,1},{1,0},{2,3},{3,2},{4,5},{5,4},{6,7},{7,6},{8,9},{9,8},{10,11... | collective-permute-start | bytes 1966088 | tf_op jit(solution)/shard_map/ppermute | solution.py:405

commit v9 on v8

--- a/solution.py
+++ b/solution.py
@@ -249,14 +249,14 @@
     return (keep, give), second
 
 
-def product(weights, value):
+def parts_of(value):
     high = value.astype(jnp.bfloat16)
     low = (value - high.astype(jnp.float32)).astype(jnp.bfloat16)
-    return jnp.dot(
-        weights,
-        jnp.concatenate([high, low, high], axis=0),
-        preferred_element_type=jnp.float32,
-    )
+    return jnp.concatenate([high, low, high], axis=0)
+
+
+def product(weights, parts):
+    return jnp.dot(weights, parts, preferred_element_type=jnp.float32)
 
 
 def react_kernel(
@@ -266,7 +266,8 @@
     steps, species, width = result_ref.shape
     each = blocks // steps
     core = core_ref[0]
-    for step in range(steps):
+
+    def newton(step):
         columns = []
         for m in range(step * each, (step + 1) * each):
             mine, other = mine_ref[m], other_ref[m]
@@ -283,17 +284,34 @@
         half_loss = jnp.concatenate([loss_ref[...]] * each, axis=1)
         source = jnp.concatenate([production_ref[...]] * each, axis=1) * photo
         current = initial
+        parts = parts_of(current)
         for iteration in range(NEWTON):
+            yield
+            linear = product(coupled_ref[...], parts)
+            yield
             part_loss = half_loss * current
             moved = current - (initial + source) if iteration else -source
-            misfit = moved - product(coupled_ref[...], current) + part_loss * current
-            first_pass = product(precond_ref[...], misfit)
-            second_pass = product(precond_ref[...], 2.0 * part_loss * first_pass)
+            parts = parts_of(moved - linear + part_loss * current)
+            yield
+            first_pass = product(precond_ref[...], parts)
+            yield
+            parts = parts_of(2.0 * part_loss * first_pass)
+            yield
+            second_pass = product(precond_ref[...], parts)
+            yield
             current = current - (first_pass - second_pass)
+            if iteration < NEWTON - 1:
+                parts = parts_of(current)
         result = current * present
         result_ref[step, :HALF] = result[:HALF]
         result_ref[step, HALF:] = result[BLOCK : BLOCK + species - HALF]
         done(step)
+
+    running = [newton(step) for step in range(steps)]
+    while running:
+        for work in list(running):
+            if next(work, "done") == "done":
+                running.remove(work)
 
 
 def react_first_kernel(*refs):
@@ -321,7 +339,7 @@
 
 def react(species, core, halves, others, photo, weights):
     blocks = others[0].shape[0]
-    steps = 2
+    steps = 4
     shape = (steps, species, blocks * LANES // steps)
     params = pltpu.CompilerParams(vmem_limit_bytes=16 * 1024 * 1024)
     cost = pl.CostEstimate(

time: 82.8 us -> 82.7 us (level)
  no operation moved by 1% of the time
where the time goes in v9:
time: 82.7 us; the launch traced here: 82.5 us
  waiting for transfers between devices  44.7 us (54%)
  Pallas kernels  21 us (25%)
  starting transfers between devices  14.4 us (17%)
  local copies, waits for them, and re-layouts  1.07 us (1%)
    all_to_all x1, waiting for transfers between devices, shards(): lax.all_to_all(packed, ('lat', 'chip', 'core'), split_axis=0, concat_axis...  44.7 us
    all_to_all x1, starting transfers between devices, shards(): lax.all_to_all(packed, ('lat', 'chip', 'core'), split_axis=0, concat_axis...  11.9 us
    pallas_call x1, Pallas kernels, pack(): pl.pallas_call(pack_kernel, out_shape=jax.ShapeDtypeStruct((devices * CHU...  8.04 us
    pallas_call x1, Pallas kernels, react(): pl.pallas_call(react_second_kernel, out_shape=jax.ShapeDtypeStruct((speci...  4.13 us
    pallas_call x1, Pallas kernels, mix(): pl.pallas_call(mix_first_kernel, out_shape=(shape, shape, rest_shape), in...  3.29 us
    pallas_call x1, Pallas kernels, react(): pl.pallas_call(react_first_kernel, out_shape=jax.ShapeDtypeStruct(shape,...  3.29 us
    pallas_call x1, Pallas kernels, mix(): pl.pallas_call(mix_second_kernel, out_shape=(shape, shape), in_specs=[IN_...  2.27 us
  transfers between devices with their start and end apart: 5, of which 1 were waited for; matrix products, arithmetic and copies ran while one was open for 2% of the time, Pallas kernels for 7%

profile of v9, /device:TPU:1, one launch (start us, length us, event | category | flops | bytes accessed | tf_op | source)
XLA Modules:
  0.0 82.5 jit_solution(10439042147005133345)
XLA Ops:
  0.0 8.0 %pack.1 = f32[7296,128]{1,0:T(8,128)} custom-call(f32[150,2048]{1,0:T(8,128)} %conc_hbm.1, s32[16,128]{1,0:T(8,128)} %bitcast.20), custom_call_target="tpu_custom_call" | custom-call | tf_op jit(solution)/shard_map/pack/pallas_call | solution.py:135
  8.0 0.0 copy-start.3
  8.1 0.0 copy-start.4
  8.1 0.0 copy-start.1
  8.1 0.0 copy-start.5
  8.1 11.9 %all-to-all-start = ((f32[128,57,1,128]{3,2,1,0:T(1,128)}), f32[128,57,1,128]{3,2,1,0:T(1,128)}, u32[]{:S(2)}, u32[]{:S(2)}) async-start(f32[128,57,1,128]{3,2,1,0:T(1,128)} %bitcast.13), calls=%async_computation | async-start | bytes 7471104 | tf_op jit(solution)/shard_map/all_to_all | solution.py:416
  20.0 0.0 copy-start.2
  20.0 0.0 copy-start.6
  20.0 0.0 copy-done.3
  20.0 1.2 %collective-permute-start = (f32[32,128]{1,0:T(8,128)S(1)}, f32[32,128]{1,0:T(8,128)S(1)}, u32[]{:S(2)}, u32[]{:S(2)}) collective-permute-start(f32[32,128]{1,0:T(8,128)S(1)} %bitcast.14), channel_id=1, source_target_pairs={{0,1},{1,0},{2,3},{3,2},{4,5},{5,4},{6,7},{7,6},{8,9},{9,8},{10,11... | collective-permute-start | bytes 49160 | tf_op jit(solution)/shard_map/ppermute | solution.py:402
  21.3 0.0 copy-done.4
  21.3 0.1 collective-permute-start.1
  21.4 0.0 copy-done.1
  21.4 0.0 copy-done.5
  21.4 0.1 mul.34
  21.5 0.0 copy-start.7
  21.6 0.0 copy-start.8
  21.6 0.4 mul.35
  22.0 0.0 copy-done.2
  22.0 0.0 copy-done.6
  22.0 0.1 slice_select_fusion.3
  22.1 0.1 split.31
  22.2 0.1 split.32
  22.3 0.0 copy-done.7
  22.3 0.1 split.29
  22.4 0.0 copy-done.8
  22.4 0.1 split.28
  22.5 0.1 reduce-precision_convert_fusion.1
  22.6 0.1 pad_maximum_fusion.refs_4_
  22.8 0.1 reduce-precision_convert_fusion
  22.9 0.1 pad_maximum_fusion.1.refs_5_
  23.0 0.1 select_maximum_fusion.4
  23.1 0.0 collective-permute-done
  23.1 0.0 collective-permute-done.1
  23.1 44.7 %all-to-all-done = f32[128,57,1,128]{3,2,1,0:T(1,128)} async-done(((f32[128,57,1,128]{3,2,1,0:T(1,128)}), f32[128,57,1,128]{3,2,1,0:T(1,128)}, u32[]{:S(2)}, u32[]{:S(2)}) %all-to-all-start) | async-done | bytes 3735584 | tf_op jit(solution)/shard_map/all_to_all | solution.py:416
  67.8 0.1 broadcast_in_dim.11.refs_6_
  67.9 0.1 broadcast_in_dim.12.refs_7_
  68.0 3.3 %mix_first.1 = (f32[16,80,128]{2,1,0:T(8,128)S(1)}, f32[16,80,128]{2,1,0:T(8,128)S(1)}, f32[3656,128]{1,0:T(8,128)S(1)}) custom-call(s32[1]{0:T(128)} %bitcast.core_ref.refs_0_, f32[7296,128]{1,0:T(8,128)} %bitcast.3.arrived_hbm, f32[2,32,128]{2,1,0:T(8,128)S(1)} %maximum_select_fusion.share_ref, s32[2,32,128]{2,1,0:T(8,128)S(1)} %add_select_fusion.partner_ref), custom_call_target="tpu_custom_call" | custom-call | bytes 8388608 | tf_op jit(solution)/shard_map/mix_first/pallas_call | solution.py:227
  71.3 0.0 copy-start
  71.3 1.0 %collective-permute-start.3 = (f32[16,80,128]{2,1,0:T(8,128)S(1)}, f32[16,80,128]{2,1,0:T(8,128)S(1)}, u32[]{:S(2)}, u32[]{:S(2)}) collective-permute-start(f32[16,80,128]{2,1,0:T(8,128)S(1)} %get-tuple-element.30), channel_id=1, source_target_pairs={{0,1},{1,0},{2,3},{3,2},{4,5},{5,4},{6,7},{7,6},{8,9},{9,8},{10,11... | collective-permute-start | bytes 1966088 | tf_op jit(solution)/shard_map/ppermute | solution.py:423
  72.3 2.3 %mix_second.1 = (f32[16,80,128]{2,1,0:T(8,128)S(1)}, f32[16,80,128]{2,1,0:T(8,128)S(1)}) custom-call(s32[1]{0:T(128)} %bitcast.core_ref.refs_0_, f32[3656,128]{1,0:T(8,128)S(1)} %get-tuple-element.21.rest_ref, f32[2,32,128]{2,1,0:T(8,128)S(1)} %maximum_select_fusion.share_ref, s32[2,32,128]{2,1,0:T(8,128)S(1)} %add_select_fusion.partner_ref), custom_call_target="tpu_custom_call" | custom-call | bytes 8388608 | tf_op jit(solution)/shard_map/mix_second/pallas_call | solution.py:240
  74.6 0.3 collective-permute-start.2
  74.8 0.0 collective-permute-done.3.refs_2_
  74.8 0.0 copy-done
  74.9 3.3 %react_first.1.refs_8_ = f32[4,150,512]{2,1,0:T(8,128)S(1)} custom-call(s32[1]{0:T(128)} %bitcast.core_ref.refs_0_, f32[16,80,128]{2,1,0:T(8,128)S(1)} %get-tuple-element.29.refs_1_, f32[16,80,128]{2,1,0:T(8,128)S(1)} %collective-permute-done.3.refs_2_, f32[32,128]{1,0:T(8,128)S(1)} %bitcast.11, bf16[160,480]{1,0:T(8,128)(2,1)S(1)} %pad_maximum_fusion.refs_4_, ...), custom_call_target="tpu_custom_call" | custom-call | flops 3221225472 | bytes 8388608 | tf_op jit(solution)/shard_map/react_first/pallas_call | solution.py:348
  78.2 0.0 collective-permute-done.2.refs_2_
  78.2 4.1 %react_second.1 = f32[150,4096]{1,0:T(8,128)} custom-call(s32[1]{0:T(128)} %bitcast.core_ref.refs_0_, f32[16,80,128]{2,1,0:T(8,128)S(1)} %get-tuple-element.22.refs_1_, f32[16,80,128]{2,1,0:T(8,128)S(1)} %collective-permute-done.2.refs_2_, f32[32,128]{1,0:T(8,128)S(1)} %bitcast.12, bf16[160,480]{1,0:T(8,128)(2,1)S(1)} %pad_maximum_fusion.refs_4_, ...), custom_call_target="tpu_custom_call" | custom-call | flops 3221225472 | bytes 8388608 | tf_op jit(solution)/shard_map/react_second/pallas_call | solution.py:357
  (11 shorter events, 0.1 us)
Async XLA Ops:
  8.0 12.0 %copy-start.3 = (f32[4096]{0:T(1024)S(1)}, f32[4096]{0:T(1024)}, u32[]{:S(2)}) copy-start(f32[4096]{0:T(1024)} %param.12) | copy-start | bytes 49156
  8.1 13.2 %copy-start.4 = (s32[4096]{0:T(1024)S(1)}, s32[4096]{0:T(1024)}, u32[]{:S(2)}) copy-start(s32[4096]{0:T(1024)} %param.13) | copy-start | bytes 49156
  8.1 13.3 %copy-start.1 = (f32[150,150]{1,0:T(8,128)S(1)}, f32[150,150]{1,0:T(8,128)}, u32[]{:S(2)}) copy-start(f32[150,150]{1,0:T(8,128)} %param.19) | copy-start | bytes 270004
  8.1 13.3 %copy-start.5 = (s32[10,10]{1,0:T(8,128)S(1)}, s32[10,10]{1,0:T(8,128)}, u32[]{:S(2)}) copy-start(s32[10,10]{1,0:T(8,128)} %param.18) | copy-start | bytes 1204
  8.1 59.7 %all-to-all-start = ((f32[128,57,1,128]{3,2,1,0:T(1,128)}), f32[128,57,1,128]{3,2,1,0:T(1,128)}, u32[]{:S(2)}, u32[]{:S(2)}) async-start(f32[128,57,1,128]{3,2,1,0:T(1,128)} %bitcast.13), calls=%async_computation | async-start | bytes 7471104 | tf_op jit(solution)/shard_map/all_to_all | solution.py:416
  20.0 2.0 %copy-start.2 = (f32[150,150]{1,0:T(8,128)S(1)}, f32[150,150]{1,0:T(8,128)}, u32[]{:S(2)}) copy-start(f32[150,150]{1,0:T(8,128)} %param.17) | copy-start | bytes 270004
  20.0 2.0 %copy-start.6 = (pred[80]{0:T(512)(128)(4,1)S(1)}, pred[80]{0:T(512)(128)(4,1)}, u32[]{:S(2)}) copy-start(pred[80]{0:T(512)(128)(4,1)} %constant.16.clone.1) | copy-start | bytes 244
  20.0 3.1 %collective-permute-start = (f32[32,128]{1,0:T(8,128)S(1)}, f32[32,128]{1,0:T(8,128)S(1)}, u32[]{:S(2)}, u32[]{:S(2)}) collective-permute-start(f32[32,128]{1,0:T(8,128)S(1)} %bitcast.14), channel_id=1, source_target_pairs={{0,1},{1,0},{2,3},{3,2},{4,5},{5,4},{6,7},{7,6},{8,9},{9,8},{10,11... | collective-permute-start | bytes 49160 | tf_op jit(solution)/shard_map/ppermute | solution.py:402
  21.3 1.9 %collective-permute-start.1 = (s32[32,128]{1,0:T(8,128)S(1)}, s32[32,128]{1,0:T(8,128)S(1)}, u32[]{:S(2)}, u32[]{:S(2)}) collective-permute-start(s32[32,128]{1,0:T(8,128)S(1)} %bitcast.16), channel_id=1, source_target_pairs={{0,1},{1,0},{2,3},{3,2},{4,5},{5,4},{6,7},{7,6},{8,9},{9,8},{10,11... | collective-permute-start | bytes 49160 | tf_op jit(solution)/shard_map/ppermute | solution.py:402
  21.5 0.8 copy-start.7
  21.6 0.9 %copy-start.8 = (f32[150]{0:T(256)S(1)}, f32[150]{0:T(256)}, u32[]{:S(2)}) copy-start(f32[150]{0:T(256)} %param.15) | copy-start | bytes 1804
  71.3 3.5 %copy-start = (f32[4096]{0:T(1024)S(1)}, f32[4096]{0:T(1024)}, u32[]{:S(2)}) copy-start(f32[4096]{0:T(1024)} %param.14) | copy-start | bytes 49156
  71.3 3.5 %collective-permute-start.3 = (f32[16,80,128]{2,1,0:T(8,128)S(1)}, f32[16,80,128]{2,1,0:T(8,128)S(1)}, u32[]{:S(2)}, u32[]{:S(2)}) collective-permute-start(f32[16,80,128]{2,1,0:T(8,128)S(1)} %get-tuple-element.30), channel_id=1, source_target_pairs={{0,1},{1,0},{2,3},{3,2},{4,5},{5,4},{6,7},{7,6},{8,9},{9,8},{10,11... | collective-permute-start | bytes 1966088 | tf_op jit(solution)/shard_map/ppermute | solution.py:423
  74.6 3.6 %collective-permute-start.2 = (f32[16,80,128]{2,1,0:T(8,128)S(1)}, f32[16,80,128]{2,1,0:T(8,128)S(1)}, u32[]{:S(2)}, u32[]{:S(2)}) collective-permute-start(f32[16,80,128]{2,1,0:T(8,128)S(1)} %get-tuple-element.23), channel_id=1, source_target_pairs={{0,1},{1,0},{2,3},{3,2},{4,5},{5,4},{6,7},{7,6},{8,9},{9,8},{10,11... | collective-permute-start | bytes 1966088 | tf_op jit(solution)/shard_map/ppermute | solution.py:423
